TPU v7x, 128 devices: a whole 4x4x4 slice. The times are simulated.
128 devices in a mesh: grp: 4 (over x_hi, core), dp: 32 (over z, y, x_lo).
Axes of the slice: x: 4 (x_hi: 2, x_lo: 2; x = x_hi * 2 + x_lo), y: 4, z: 4, core: 2. Of those that a mesh axis runs over, the one named last changes fastest.
Arguments:
- tokens: bfloat16 [16384, 2048], P(('grp', 'dp')), may hold values from -6 to 6
- cotangent: bfloat16 [16384, 2048], P(('grp', 'dp')), may hold values from -6 to 6
- segment_ids: int32 [16384], P(('grp', 'dp')), may hold values from 0 to 15, as said below
- positions: int32 [16384], P(('grp', 'dp')), may hold values from 0 to 127, as said below
- padding: int32 [16384], P(('grp', 'dp')), may hold values from 0 to 1, as said below
- attn_gain: float32 [2048], replicated, may hold values from 0.5 to 1.5
- query_weight: float32 [2048, 2048], P('dp'), may hold values from -0.125 to 0.125
- key_weight: float32 [2048, 256], P('dp'), may hold values from -0.125 to 0.125
- value_weight: float32 [2048, 256], P('dp'), may hold values from -0.125 to 0.125
- output_weight: float32 [2048, 2048], P('dp'), may hold values from -0.5 to 0.5
- mlp_gain: float32 [2048], replicated, may hold values from 0.5 to 1.5
- gate_weight: float32 [2048, 5632], P('dp'), may hold values from -0.125 to 0.125
- up_weight: float32 [2048, 5632], P('dp'), may hold values from -0.125 to 0.125
- down_weight: float32 [5632, 2048], P('dp'), may hold values from -0.078125 to 0.078125
- attn_moment: float32 [2048], replicated, may hold values from -96 to 96
- query_moment: float32 [2048, 2048], P('dp', 'grp'), may hold values from -96 to 96
- key_moment: float32 [2048, 256], P('dp', 'grp'), may hold values from -96 to 96
- value_moment: float32 [2048, 256], P('dp', 'grp'), may hold values from -1536 to 1536
- output_moment: float32 [2048, 2048], P('dp', 'grp'), may hold values from -96 to 96
- mlp_moment: float32 [2048], replicated, may hold values from -96 to 96
- gate_moment: float32 [2048, 5632], P('dp', 'grp'), may hold values from -96 to 96
- up_moment: float32 [2048, 5632], P('dp', 'grp'), may hold values from -96 to 96
- down_moment: float32 [5632, 2048], P('dp', 'grp'), may hold values from -96 to 96
Outputs:
- block_output: bfloat16 [16384, 2048], P(('grp', 'dp'))
- input_grad: float32 [16384, 2048], P(('grp', 'dp'))
- attn_momentum: float32 [2048], replicated
- query_momentum: float32 [2048, 2048], P('dp', 'grp')
- key_momentum: float32 [2048, 256], P('dp', 'grp')
- value_momentum: float32 [2048, 256], P('dp', 'grp')
- output_momentum: float32 [2048, 2048], P('dp', 'grp')
- mlp_momentum: float32 [2048], replicated
- gate_momentum: float32 [2048, 5632], P('dp', 'grp')
- up_momentum: float32 [2048, 5632], P('dp', 'grp')
- down_momentum: float32 [5632, 2048], P('dp', 'grp')
- attn_updated: float32 [2048], replicated
- query_updated: float32 [2048, 2048], P('dp')
- key_updated: float32 [2048, 256], P('dp')
- value_updated: float32 [2048, 256], P('dp')
- output_updated: float32 [2048, 2048], P('dp')
- mlp_updated: float32 [2048], replicated
- gate_updated: float32 [2048, 5632], P('dp')
- up_updated: float32 [2048, 5632], P('dp')
- down_updated: float32 [5632, 2048], P('dp')
Inputs may be any that keep to these rules, and one draw needn't show every extreme that they name: `segment_ids`: within each sequence of 128 tokens the segment numbers start at 0, never fall, and rise by one only at tokens whose place in the sequence is a multiple of 8. `positions`: A token's place in its document, 0 at each document's first token. `padding`: padding stands at the end of a sequence, at most 17 tokens of it.
All inputs are finite; a program needn't handle non-finite values.
Results may differ from a plain program's by a relative error of at most 0.028.
Values may be sent and summed in bfloat16 or wider, within the bound.
No kernel may reach another device: no remote copies, remote signals or barrier semaphores. Data moves between devices by JAX's collectives and lax.ppermute only.
A program may use at most 384 MiB of HBM per device.

v0:
```python
import jax
import jax.numpy as jnp
from jax import lax
from jax.sharding import PartitionSpec as P

HEADS = 32
KV_HEADS = 4
HEAD_DIM = 64
QD = 2048
KVD = 256


epsilon = 1e-05
learn_rate = 0.005
score_scale = 0.125


def normalize(values, gain):
    return values * lax.rsqrt(jnp.mean(values * values, axis=-1, keepdims=True) + epsilon) * gain


def rotary_tables(places):
    half = HEAD_DIM // 2
    freq = 10000.0 ** (-(jnp.arange(half, dtype=jnp.float32) * 2.0 / HEAD_DIM))
    angles = places.astype(jnp.float32)[..., None] * freq
    cosine = jnp.concatenate([jnp.cos(angles), jnp.cos(angles)], axis=-1)
    sine = jnp.concatenate([jnp.sin(angles), jnp.sin(angles)], axis=-1)
    return (cosine, sine)


def rotate(values, cosine, sine):
    half = values.shape[-1] // 2
    turned = jnp.concatenate([-values[..., half:], values[..., :half]], axis=-1)
    return values * cosine + turned * sine


def swiglu(gate, upper):
    return jax.nn.silu(gate) * upper


def rounded_gain(gain):
    return lax.optimization_barrier(gain.astype(jnp.bfloat16)).astype(jnp.float32)


def left_product(left, right):
    return lax.dot_general(
        left, right, (((0,), (0,)), ((), ())), preferred_element_type=jnp.float32
    )


def right_product(left, right):
    return lax.dot_general(
        left, right, (((1,), (1,)), ((), ())), preferred_element_type=jnp.float32
    )


def momentum_step(master, moment, total, member):
    width = moment.shape[1]
    mine = lax.dynamic_slice_in_dim(master, member * width, width, 1)
    moved = 0.5 * moment + 0.5 * total
    return (moved, mine - learn_rate * moved)


def masked_scores(query_rot, key_rot, allowed):
    scores = (
        jnp.einsum("qkgd,skd->kgqs", query_rot, key_rot, preferred_element_type=jnp.float32)
        * score_scale
    )
    return jnp.where(allowed[None, None], scores, -1e30)


def on_device(
    tokens,
    cotangent,
    segment_ids,
    positions,
    padding,
    attn_gain,
    query_weight,
    key_weight,
    value_weight,
    output_weight,
    mlp_gain,
    gate_weight,
    up_weight,
    down_weight,
    attn_moment,
    query_moment,
    key_moment,
    value_moment,
    output_moment,
    mlp_moment,
    gate_moment,
    up_moment,
    down_moment,
):
    member = lax.axis_index("grp")
    query_full, key_full, value_full, output_full, gate_full, up_full, down_full = (
        lax.all_gather(query_weight.astype(jnp.bfloat16), "dp", axis=0, tiled=True),
        lax.all_gather(key_weight.astype(jnp.bfloat16), "dp", axis=0, tiled=True),
        lax.all_gather(value_weight.astype(jnp.bfloat16), "dp", axis=0, tiled=True),
        lax.all_gather(output_weight.astype(jnp.bfloat16), "dp", axis=0, tiled=True),
        lax.all_gather(gate_weight.astype(jnp.bfloat16), "dp", axis=0, tiled=True),
        lax.all_gather(up_weight.astype(jnp.bfloat16), "dp", axis=0, tiled=True),
        lax.all_gather(down_weight.astype(jnp.bfloat16), "dp", axis=0, tiled=True),
    )
    rows = tokens.shape[0]
    groups = HEADS // KV_HEADS
    inputs = tokens.astype(jnp.float32)
    cosine, sine = rotary_tables(positions)
    first_gain = rounded_gain(attn_gain)
    second_gain = rounded_gain(mlp_gain)
    normed_first, pull_first = jax.vjp(normalize, inputs, first_gain)
    first_low = normed_first.astype(jnp.bfloat16)
    query_lin = jnp.dot(first_low, query_full, preferred_element_type=jnp.float32).reshape(
        rows, KV_HEADS, groups, HEAD_DIM
    )
    key_lin = jnp.dot(first_low, key_full, preferred_element_type=jnp.float32).reshape(
        rows, KV_HEADS, HEAD_DIM
    )
    value_low = (
        jnp.dot(first_low, value_full, preferred_element_type=jnp.float32)
        .astype(jnp.bfloat16)
        .reshape(rows, KV_HEADS, HEAD_DIM)
    )
    query_turned, pull_query = jax.vjp(
        lambda values: rotate(values, cosine[:, None, None, :], sine[:, None, None, :]), query_lin
    )
    key_turned, pull_key = jax.vjp(
        lambda values: rotate(values, cosine[:, None, :], sine[:, None, :]), key_lin
    )
    query_rot = query_turned.astype(jnp.bfloat16)
    key_rot = key_turned.astype(jnp.bfloat16)
    column_index = jnp.arange(rows, dtype=jnp.int32)
    diagonal = column_index[None, :] == column_index[:, None]
    allowed = jnp.logical_and(
        jnp.logical_and(
            segment_ids[:, None] == segment_ids[None, :],
            column_index[None, :] <= column_index[:, None],
        ),
        jnp.logical_or(padding[None, :] == 1, diagonal),
    )
    masked = masked_scores(query_rot, key_rot, allowed)
    row_max = jnp.max(masked, axis=-1, keepdims=True)
    log_total = row_max + jnp.log(jnp.sum(jnp.exp(masked - row_max), axis=-1, keepdims=True))
    probs_low = jnp.exp(masked - log_total).astype(jnp.bfloat16)
    attended = jnp.einsum(
        "kgqs,skd->qkgd", probs_low, value_low, preferred_element_type=jnp.float32
    )
    attended_low = attended.reshape(rows, QD).astype(jnp.bfloat16)
    middle = inputs + jnp.dot(attended_low, output_full, preferred_element_type=jnp.float32)
    normed_second, pull_second = jax.vjp(normalize, middle, second_gain)
    second_low = normed_second.astype(jnp.bfloat16)
    gate_lin = jnp.dot(second_low, gate_full, preferred_element_type=jnp.float32)
    up_lin = jnp.dot(second_low, up_full, preferred_element_type=jnp.float32)
    activated, pull_act = jax.vjp(swiglu, gate_lin, up_lin)
    activated_low = activated.astype(jnp.bfloat16)
    block_output = (
        middle + jnp.dot(activated_low, down_full, preferred_element_type=jnp.float32)
    ).astype(jnp.bfloat16)
    grad_out = cotangent.astype(jnp.float32)
    grad_down = left_product(activated_low, cotangent)
    grad_activated = right_product(cotangent, down_full)
    grad_gate_lin, grad_up_lin = pull_act(grad_activated)
    grad_gate_low = grad_gate_lin.astype(jnp.bfloat16)
    grad_up_low = grad_up_lin.astype(jnp.bfloat16)
    grad_gate = left_product(second_low, grad_gate_low)
    grad_up = left_product(second_low, grad_up_low)
    grad_second = right_product(grad_gate_low, gate_full) + right_product(grad_up_low, up_full)
    grad_middle_norm, grad_mlp_gain = pull_second(grad_second)
    grad_middle = grad_out + grad_middle_norm
    gate_part, up_part, down_part = (
        lax.psum_scatter(
            grad_gate.astype(jnp.bfloat16), "grp", scatter_dimension=1, tiled=True
        ).astype(jnp.float32),
        lax.psum_scatter(
            grad_up.astype(jnp.bfloat16), "grp", scatter_dimension=1, tiled=True
        ).astype(jnp.float32),
        lax.psum_scatter(
            grad_down.astype(jnp.bfloat16), "grp", scatter_dimension=1, tiled=True
        ).astype(jnp.float32),
    )
    gate_sum, up_sum, down_sum = (
        lax.psum_scatter(
            gate_part.astype(jnp.bfloat16), "dp", scatter_dimension=0, tiled=True
        ).astype(jnp.float32),
        lax.psum_scatter(
            up_part.astype(jnp.bfloat16), "dp", scatter_dimension=0, tiled=True
        ).astype(jnp.float32),
        lax.psum_scatter(
            down_part.astype(jnp.bfloat16), "dp", scatter_dimension=0, tiled=True
        ).astype(jnp.float32),
    )
    gate_momentum, gate_mine = momentum_step(gate_weight, gate_moment, gate_sum, member)
    up_momentum, up_mine = momentum_step(up_weight, up_moment, up_sum, member)
    down_momentum, down_mine = momentum_step(down_weight, down_moment, down_sum, member)
    gate_updated, up_updated, down_updated = (
        lax.all_gather(gate_mine.astype(jnp.bfloat16), "grp", axis=1, tiled=True).astype(
            gate_mine.dtype
        ),
        lax.all_gather(up_mine.astype(jnp.bfloat16), "grp", axis=1, tiled=True).astype(
            up_mine.dtype
        ),
        lax.all_gather(down_mine.astype(jnp.bfloat16), "grp", axis=1, tiled=True).astype(
            down_mine.dtype
        ),
    )
    grad_middle_low = grad_middle.astype(jnp.bfloat16)
    grad_output = left_product(attended_low, grad_middle_low)
    grad_attended = (
        right_product(grad_middle_low, output_full)
        .reshape(rows, KV_HEADS, groups, HEAD_DIM)
        .astype(jnp.bfloat16)
    )
    again = masked_scores(query_rot, key_rot, allowed)
    probs = jnp.exp(again - log_total)
    probs_again = probs.astype(jnp.bfloat16)
    grad_value_low = (
        jnp.einsum("kgqs,qkgd->skd", probs_again, grad_attended, preferred_element_type=jnp.float32)
        .astype(jnp.bfloat16)
        .reshape(rows, KVD)
    )
    grad_probs = jnp.einsum(
        "qkgd,skd->kgqs", grad_attended, value_low, preferred_element_type=jnp.float32
    )
    grad_scores_low = (
        probs * (grad_probs - jnp.sum(grad_probs * probs, axis=-1, keepdims=True))
    ).astype(jnp.bfloat16)
    grad_query_rot = (
        jnp.einsum("kgqs,skd->qkgd", grad_scores_low, key_rot, preferred_element_type=jnp.float32)
        * score_scale
    )
    grad_key_rot = (
        jnp.einsum("kgqs,qkgd->skd", grad_scores_low, query_rot, preferred_element_type=jnp.float32)
        * score_scale
    )
    grad_query_low = pull_query(grad_query_rot)[0].astype(jnp.bfloat16).reshape(rows, QD)
    grad_key_low = pull_key(grad_key_rot)[0].astype(jnp.bfloat16).reshape(rows, KVD)
    grad_query = left_product(first_low, grad_query_low)
    grad_key = left_product(first_low, grad_key_low)
    grad_value = left_product(first_low, grad_value_low)
    grad_first = (
        right_product(grad_query_low, query_full)
        + right_product(grad_key_low, key_full)
        + right_product(grad_value_low, value_full)
    )
    grad_inputs_norm, grad_attn_gain = pull_first(grad_first)
    input_grad = grad_middle + grad_inputs_norm
    query_part, key_part, value_part, output_part = (
        lax.psum_scatter(
            grad_query.astype(jnp.bfloat16), "grp", scatter_dimension=1, tiled=True
        ).astype(jnp.float32),
        lax.psum_scatter(
            grad_key.astype(jnp.bfloat16), "grp", scatter_dimension=1, tiled=True
        ).astype(jnp.float32),
        lax.psum_scatter(
            grad_value.astype(jnp.bfloat16), "grp", scatter_dimension=1, tiled=True
        ).astype(jnp.float32),
        lax.psum_scatter(
            grad_output.astype(jnp.bfloat16), "grp", scatter_dimension=1, tiled=True
        ).astype(jnp.float32),
    )
    query_sum, key_sum, value_sum, output_sum = (
        lax.psum_scatter(
            query_part.astype(jnp.bfloat16), "dp", scatter_dimension=0, tiled=True
        ).astype(jnp.float32),
        lax.psum_scatter(
            key_part.astype(jnp.bfloat16), "dp", scatter_dimension=0, tiled=True
        ).astype(jnp.float32),
        lax.psum_scatter(
            value_part.astype(jnp.bfloat16), "dp", scatter_dimension=0, tiled=True
        ).astype(jnp.float32),
        lax.psum_scatter(
            output_part.astype(jnp.bfloat16), "dp", scatter_dimension=0, tiled=True
        ).astype(jnp.float32),
    )
    query_momentum, query_mine = momentum_step(query_weight, query_moment, query_sum, member)
    key_momentum, key_mine = momentum_step(key_weight, key_moment, key_sum, member)
    value_momentum, value_mine = momentum_step(value_weight, value_moment, value_sum, member)
    output_momentum, output_mine = momentum_step(output_weight, output_moment, output_sum, member)
    query_updated, key_updated, value_updated, output_updated = (
        lax.all_gather(query_mine.astype(jnp.bfloat16), "grp", axis=1, tiled=True).astype(
            query_mine.dtype
        ),
        lax.all_gather(key_mine.astype(jnp.bfloat16), "grp", axis=1, tiled=True).astype(
            key_mine.dtype
        ),
        lax.all_gather(value_mine.astype(jnp.bfloat16), "grp", axis=1, tiled=True).astype(
            value_mine.dtype
        ),
        lax.all_gather(output_mine.astype(jnp.bfloat16), "grp", axis=1, tiled=True).astype(
            output_mine.dtype
        ),
    )
    attn_total, mlp_total = lax.psum((grad_attn_gain, grad_mlp_gain), ("grp", "dp"))
    attn_momentum = 0.5 * attn_moment + 0.5 * attn_total
    mlp_momentum = 0.5 * mlp_moment + 0.5 * mlp_total
    attn_updated = attn_gain - learn_rate * attn_momentum
    mlp_updated = mlp_gain - learn_rate * mlp_momentum
    return (
        block_output,
        input_grad,
        attn_momentum,
        query_momentum,
        key_momentum,
        value_momentum,
        output_momentum,
        mlp_momentum,
        gate_momentum,
        up_momentum,
        down_momentum,
        attn_updated,
        query_updated,
        key_updated,
        value_updated,
        output_updated,
        mlp_updated,
        gate_updated,
        up_updated,
        down_updated,
    )


def solution(mesh):
    placed = (
        P(("grp", "dp"), None),
        P(("grp", "dp"), None),
        P(("grp", "dp")),
        P(("grp", "dp")),
        P(("grp", "dp")),
        P(),
        P("dp", None),
        P("dp", None),
        P("dp", None),
        P("dp", None),
        P(),
        P("dp", None),
        P("dp", None),
        P("dp", None),
        P(),
        P("dp", "grp"),
        P("dp", "grp"),
        P("dp", "grp"),
        P("dp", "grp"),
        P(),
        P("dp", "grp"),
        P("dp", "grp"),
        P("dp", "grp"),
    )
    return jax.shard_map(
        on_device,
        mesh=mesh,
        in_specs=placed,
        out_specs=(
            P(("grp", "dp"), None),
            P(("grp", "dp"), None),
            P(),
            P("dp", "grp"),
            P("dp", "grp"),
            P("dp", "grp"),
            P("dp", "grp"),
            P(),
            P("dp", "grp"),
            P("dp", "grp"),
            P("dp", "grp"),
            P(),
            P("dp", None),
            P("dp", None),
            P("dp", None),
            P("dp", None),
            P(),
            P("dp", None),
            P("dp", None),
            P("dp", None),
        ),
        check_vma=False,
    )
```

profile of v0, /device:TPU:1, one launch (start us, length us, event | category | flops | bytes accessed | tf_op | source)
XLA Modules:
  0.0 4199.7 jit_solution(3593103372278978909)
XLA Ops:
  20.7 123.6 %all-gather.8.cloned.1.call-done = bf16[2048,256]{1,0:T(8,128)(2,1)} async-done(((bf16[64,256]{1,0:T(8,128)(2,1)}), bf16[2048,256]{1,0:T(8,128)(2,1)}) %all-gather.8.cloned.1.call-update) | async-done | bytes 1048592 | tf_op jit(solution)/shard_map/all_gather | solution.py:101
  145.9 151.8 %all-gather.10.cloned.1.call-done = bf16[2048,256]{1,0:T(8,128)(2,1)} async-done(((bf16[64,256]{1,0:T(8,128)(2,1)}), bf16[2048,256]{1,0:T(8,128)(2,1)}) %all-gather.10.cloned.1.call-update) | async-done | bytes 1048592 | tf_op jit(solution)/shard_map/all_gather | solution.py:100
  299.5 211.6 %all-gather.12.cloned.1.call-done = bf16[2048,2048]{1,0:T(8,128)(2,1)} async-done(((bf16[64,2048]{1,0:T(8,128)(2,1)}), bf16[2048,2048]{1,0:T(8,128)(2,1)}) %all-gather.12.cloned.1.call-update) | async-done | bytes 8388624 | tf_op jit(solution)/shard_map/all_gather | solution.py:99
  519.7 181.5 %all-gather.14.cloned.1.call-done = bf16[2048,2048]{1,0:T(8,128)(2,1)} async-done(((bf16[64,2048]{1,0:T(8,128)(2,1)}), bf16[2048,2048]{1,0:T(8,128)(2,1)}) %all-gather.14.cloned.1.call-update) | async-done | bytes 8388624 | tf_op jit(solution)/shard_map/all_gather | solution.py:102
  707.1 487.6 %all-gather.16.cloned.1.call-done = bf16[2048,5632]{1,0:T(8,128)(2,1)} async-done(((bf16[64,5632]{1,0:T(8,128)(2,1)}), bf16[2048,5632]{1,0:T(8,128)(2,1)}) %all-gather.16.cloned.1.call-update) | async-done | bytes 23068688 | tf_op jit(solution)/shard_map/all_gather | solution.py:103
  1207.2 481.6 %all-gather.18.cloned.1.call-done = bf16[2048,5632]{1,0:T(8,128)(2,1)} async-done(((bf16[64,5632]{1,0:T(8,128)(2,1)}), bf16[2048,5632]{1,0:T(8,128)(2,1)}) %all-gather.18.cloned.1.call-update) | async-done | bytes 23068688 | tf_op jit(solution)/shard_map/all_gather | solution.py:104
  1701.4 481.5 %all-gather.20.cloned.1.call-done = bf16[5632,2048]{1,0:T(8,128)(2,1)} async-done(((bf16[176,2048]{1,0:T(8,128)(2,1)}), bf16[5632,2048]{1,0:T(8,128)(2,1)}) %all-gather.20.cloned.1.call-update) | async-done | bytes 23068688 | tf_op jit(solution)/shard_map/all_gather | solution.py:105
  2387.0 81.0 %reduce-scatter.31.cloned.1.call-done = bf16[2048,512]{1,0:T(8,128)(2,1)} async-done(((bf16[2048,2048]{1,0:T(8,128)(2,1)}), bf16[2048,512]{1,0:T(8,128)(2,1)}) %reduce-scatter.31.cloned.1.call-update) | async-done | bytes 2097168 | tf_op jit(solution)/shard_map/reduce_scatter | solution.py:259
  2468.0 175.6 %reduce-scatter.47.cloned.1.call-done = bf16[1408,2048]{1,0:T(8,128)(2,1)} async-done(((bf16[5632,2048]{1,0:T(8,128)(2,1)}), bf16[1408,2048]{1,0:T(8,128)(2,1)}) %reduce-scatter.47.cloned.1.call-update) | async-done | bytes 5767184
  2652.0 167.7 %reduce-scatter.49.cloned.1.call-done = bf16[1408,2048]{1,0:T(8,128)(2,1)} async-done(((bf16[5632,2048]{1,0:T(8,128)(2,1)}), bf16[1408,2048]{1,0:T(8,128)(2,1)}) %reduce-scatter.49.cloned.1.call-update) | async-done | bytes 5767184
  2828.2 167.2 %reduce-scatter.39.cloned.1.call-done = bf16[5632,512]{1,0:T(8,128)(2,1)} async-done(((bf16[5632,2048]{1,0:T(8,128)(2,1)}), bf16[5632,512]{1,0:T(8,128)(2,1)}) %reduce-scatter.39.cloned.1.call-update) | async-done | bytes 5767184 | tf_op jit(solution)/shard_map/reduce_scatter | solution.py:179
  3005.9 65.8 %all-reduce.4 = (f32[2048]{0:T(1024)S(1)}, f32[2048]{0:T(1024)S(1)}) all-reduce(f32[2048]{0:T(1024)S(1)} %get-tuple-element.82, f32[2048]{0:T(1024)S(1)} %get-tuple-element.80), channel_id=1, replica_groups=mesh['grp'=4,'dp'=32] {'grp','dp'}, use_global_device_ids=true, to_apply=%region_8.9 | all-reduce | flops 4096 | bytes 32768 | tf_op jit(solution)/shard_map/psum | solution.py:295
  3086.6 46.2 %reduce-scatter.43.cloned.1.call-done = bf16[64,64]{1,0:T(8,128)(2,1)} async-done(((bf16[2048,64]{1,0:T(8,128)(2,1)}), bf16[64,64]{1,0:T(8,128)(2,1)}) %reduce-scatter.43.cloned.1.call-update) | async-done | bytes 8208
  3134.3 157.4 %reduce-scatter.45.cloned.1.call-done = bf16[64,64]{1,0:T(8,128)(2,1)} async-done(((bf16[2048,64]{1,0:T(8,128)(2,1)}), bf16[64,64]{1,0:T(8,128)(2,1)}) %reduce-scatter.45.cloned.1.call-update) | async-done | bytes 8208
  3293.2 33.2 all_gather.50
  3334.6 124.0 %reduce-scatter.25.cloned.1.call-done = bf16[64,512]{1,0:T(8,128)(2,1)} async-done(((bf16[2048,512]{1,0:T(8,128)(2,1)}), bf16[64,512]{1,0:T(8,128)(2,1)}) %reduce-scatter.25.cloned.1.call-update) | async-done | bytes 65552 | tf_op jit(solution)/shard_map/reduce_scatter | solution.py:264
  3491.2 130.1 %reduce-scatter.33.cloned.1.call-done = bf16[64,512]{1,0:T(8,128)(2,1)} async-done(((bf16[2048,512]{1,0:T(8,128)(2,1)}), bf16[64,512]{1,0:T(8,128)(2,1)}) %reduce-scatter.33.cloned.1.call-update) | async-done | bytes 65552 | tf_op jit(solution)/shard_map/reduce_scatter | solution.py:273
  3622.9 31.2 all_gather.52
  3654.9 144.3 %reduce-scatter.35.cloned.1.call-done = bf16[64,1408]{1,0:T(8,128)(2,1)} async-done(((bf16[2048,1408]{1,0:T(8,128)(2,1)}), bf16[64,1408]{1,0:T(8,128)(2,1)}) %reduce-scatter.35.cloned.1.call-update) | async-done | bytes 180240 | tf_op jit(solution)/shard_map/reduce_scatter | solution.py:184
  3801.1 32.2 all_gather.53
  3834.5 143.7 %reduce-scatter.37.cloned.1.call-done = bf16[64,1408]{1,0:T(8,128)(2,1)} async-done(((bf16[2048,1408]{1,0:T(8,128)(2,1)}), bf16[64,1408]{1,0:T(8,128)(2,1)}) %reduce-scatter.37.cloned.1.call-update) | async-done | bytes 180240 | tf_op jit(solution)/shard_map/reduce_scatter | solution.py:187
  3980.1 32.2 all_gather.54
  4013.5 143.7 %reduce-scatter.41.cloned.1.call-done = bf16[176,512]{1,0:T(8,128)(2,1)} async-done(((bf16[5632,512]{1,0:T(8,128)(2,1)}), bf16[176,512]{1,0:T(8,128)(2,1)}) %reduce-scatter.41.cloned.1.call-update) | async-done | bytes 180240 | tf_op jit(solution)/shard_map/reduce_scatter | solution.py:190
  4159.0 32.2 all_gather.55
  (220 shorter events, 357.5 us)
Async XLA Ops:
  7.2 137.0 %all-gather.8.cloned.1.call-start = ((), (), s32[]{:S(2)}) async-start(), calls=%async_computation.14 | async-start | bytes 1081344 | tf_op jit(solution)/shard_map/all_gather | solution.py:101
  8.8 288.8 %all-gather.10.cloned.1.call-start = ((), (), s32[]{:S(2)}) async-start(), calls=%async_computation.15 | async-start | bytes 1081344 | tf_op jit(solution)/shard_map/all_gather | solution.py:100
  10.4 500.7 %all-gather.12.cloned.1.call-start = ((), (), s32[]{:S(2)}) async-start(), calls=%async_computation.16 | async-start | bytes 8650752 | tf_op jit(solution)/shard_map/all_gather | solution.py:99
  12.2 688.9 %all-gather.14.cloned.1.call-start = ((), (), s32[]{:S(2)}) async-start(), calls=%async_computation.17 | async-start | bytes 8650752 | tf_op jit(solution)/shard_map/all_gather | solution.py:102
  14.1 1180.7 %all-gather.16.cloned.1.call-start = ((), (), s32[]{:S(2)}) async-start(), calls=%async_computation.18 | async-start | bytes 23789568 | tf_op jit(solution)/shard_map/all_gather | solution.py:103
  15.2 1673.6 %all-gather.18.cloned.1.call-start = ((), (), s32[]{:S(2)}) async-start(), calls=%async_computation.19 | async-start | bytes 23789568 | tf_op jit(solution)/shard_map/all_gather | solution.py:104
  17.6 2165.4 %all-gather.20.cloned.1.call-start = ((), (), s32[]{:S(2)}) async-start(), calls=%async_computation.20 | async-start | bytes 23789568 | tf_op jit(solution)/shard_map/all_gather | solution.py:105
  20.0 2337.8 %reduce-scatter.27.cloned.1.call-start = ((), (), s32[]{:S(2)}) async-start(), calls=%async_computation.23 | async-start | bytes 1310720 | tf_op jit(solution)/shard_map/reduce_scatter | solution.py:253
  20.5 497.4 %copy-start.34 = (f32[128]{0:T(128)}, f32[128]{0:T(128)S(1)}, u32[]{:S(2)}) copy-start(f32[128]{0:T(128)S(1)} %fusion.16) | copy-start | bytes 1540
  2241.9 117.9 %reduce-scatter.29.cloned.1.call-start = ((), (), s32[]{:S(2)}) async-start(), calls=%async_computation.24 | async-start | bytes 1310720 | tf_op jit(solution)/shard_map/reduce_scatter | solution.py:256
  2245.2 141.8 %reduce-scatter.23.cloned.1.call-start = ((), (), s32[]{:S(2)}) async-start(), calls=%async_computation.21 | async-start | bytes 10485760 | tf_op jit(solution)/shard_map/reduce_scatter | solution.py:250
  2251.8 216.2 %reduce-scatter.31.cloned.1.call-start = ((), (), s32[]{:S(2)}) async-start(), calls=%async_computation.25 | async-start | bytes 10485760 | tf_op jit(solution)/shard_map/reduce_scatter | solution.py:259
  2258.7 384.9 %reduce-scatter.47.cloned.1.call-start = ((), (), s32[]{:S(2)}) async-start(), calls=%async_computation.33 | async-start | bytes 28835840
  2300.9 518.8 %reduce-scatter.49.cloned.1.call-start = ((), (), s32[]{:S(2)}) async-start(), calls=%async_computation.34 | async-start | bytes 28835840
  2344.4 651.0 %reduce-scatter.39.cloned.1.call-start = ((), (), s32[]{:S(2)}) async-start(), calls=%async_computation.29 | async-start | bytes 28835840 | tf_op jit(solution)/shard_map/reduce_scatter | solution.py:179
  2357.7 775.1 %reduce-scatter.43.cloned.1.call-start = ((), (), s32[]{:S(2)}) async-start(), calls=%async_computation.31 | async-start | bytes 540672
  2359.7 932.0 %reduce-scatter.45.cloned.1.call-start = ((), (), s32[]{:S(2)}) async-start(), calls=%async_computation.32 | async-start | bytes 540672
  2361.8 1096.8 %reduce-scatter.25.cloned.1.call-start = ((), (), s32[]{:S(2)}) async-start(), calls=%async_computation.22 | async-start | bytes 2162688 | tf_op jit(solution)/shard_map/reduce_scatter | solution.py:264
  2386.9 1234.3 %reduce-scatter.33.cloned.1.call-start = ((), (), s32[]{:S(2)}) async-start(), calls=%async_computation.26 | async-start | bytes 2162688 | tf_op jit(solution)/shard_map/reduce_scatter | solution.py:273
  2468.0 1331.3 %reduce-scatter.35.cloned.1.call-start = ((), (), s32[]{:S(2)}) async-start(), calls=%async_computation.27 | async-start | bytes 5947392 | tf_op jit(solution)/shard_map/reduce_scatter | solution.py:184
  2651.9 1326.3 %reduce-scatter.37.cloned.1.call-start = ((), (), s32[]{:S(2)}) async-start(), calls=%async_computation.28 | async-start | bytes 5947392 | tf_op jit(solution)/shard_map/reduce_scatter | solution.py:187
  2828.1 1329.0 %reduce-scatter.41.cloned.1.call-start = ((), (), s32[]{:S(2)}) async-start(), calls=%async_computation.30 | async-start | bytes 5947392 | tf_op jit(solution)/shard_map/reduce_scatter | solution.py:190
  3074.9 546.4 %copy-start.24 = (f32[64,512]{1,0:T(8,128)S(1)}, f32[64,512]{1,0:T(8,128)}, u32[]{:S(2)}) copy-start(f32[64,512]{1,0:T(8,128)} %param.41) | copy-start | bytes 393220
  3086.6 712.6 %copy-start.18 = (f32[64,1408]{1,0:T(8,128)S(1)}, f32[64,1408]{1,0:T(8,128)}, u32[]{:S(2)}) copy-start(f32[64,1408]{1,0:T(8,128)} %param.43) | copy-start | bytes 1081348
  (35 other events, 1752.6 us)
Sparse Core Ops, SparseCore 0:
  10.3 133.9 all-gather.7
  146.4 151.1 all-gather.9
  299.9 211.1 all-gather.11
  513.2 187.9 all-gather.13
  703.2 491.4 all-gather.15
  1196.8 491.9 all-gather.17
  1691.0 491.9 all-gather.19
  2242.1 30.0 reduce-scatter.26
  2275.0 31.2 reduce-scatter.28
  2308.8 78.0 reduce-scatter.22
  2389.8 78.0 reduce-scatter.30
  2470.5 173.0 reduce-scatter.46
  2646.5 173.1 reduce-scatter.48
  2822.2 173.0 reduce-scatter.38
  2998.3 134.5 reduce-scatter.42
  3135.6 156.0 reduce-scatter.44
  3294.0 164.5 reduce-scatter.24
  3460.8 160.4 reduce-scatter.32
  3623.8 175.3 reduce-scatter.34
  3801.6 176.5 reduce-scatter.36
  3980.8 176.3 reduce-scatter.40
where the time goes:
time: 4210 us; the launch traced here: 4200 us
  waiting for transfers between devices  3630 us (86%)
  blocking collectives  264 us (6%)
  matrix products  165 us (4%)
  local copies, waits for them, and re-layouts  95.3 us (2%)
    unnamed x25, waiting for transfers between devices  547 us
    all_gather x1, waiting for transfers between devices, on_device(): lax.all_gather(gate_weight.astype(jnp.bfloat16), 'dp', axis=0, tiled=True)  488 us
    all_gather x1, waiting for transfers between devices, on_device(): lax.all_gather(up_weight.astype(jnp.bfloat16), 'dp', axis=0, tiled=True)  482 us
    all_gather x1, waiting for transfers between devices, on_device(): lax.all_gather(down_weight.astype(jnp.bfloat16), 'dp', axis=0, tiled=True)  482 us
    all_gather x1, waiting for transfers between devices, on_device(): lax.all_gather(query_weight.astype(jnp.bfloat16), 'dp', axis=0, tiled=True)  212 us
    all_gather x1, waiting for transfers between devices, on_device(): lax.all_gather(output_weight.astype(jnp.bfloat16), 'dp', axis=0, tiled=True)  181 us
    reduce_scatter x1, waiting for transfers between devices, on_device(): lax.psum_scatter(grad_down.astype(jnp.bfloat16), 'grp', scatter_dimension...  167 us
    all_gather x1, waiting for transfers between devices, on_device(): lax.all_gather(key_weight.astype(jnp.bfloat16), 'dp', axis=0, tiled=True)  152 us
  transfers between devices with their start and end apart: 21, of which 19 were waited for; matrix products, arithmetic and copies ran while one was open for 5% of the time, Pallas kernels for 0%

commit v1 on v0

v1 whole, which is shorter than its diff:
```python
import jax
import jax.numpy as jnp
from jax import lax
from jax.sharding import PartitionSpec as P

D = 2048
HEAD_DIM = 64
GROUPS = 8
ROWS = 128
MEMBERS = 4
SLOTS = ROWS * MEMBERS
QW = 512
KW = 64
QKVW = QW + 2 * KW
FW = 1408
GUW = 2 * FW
PANEL = 512
DOWN_ROWS = 176
OUT_ROWS = 64
W_ROWS = 64

epsilon = 1e-05
learn_rate = 0.005
score_scale = 0.125

BF = jnp.bfloat16
F32 = jnp.float32


def dp_index(z, y, x):
    return z * 8 + y * 2 + x


PLANES = [[dp_index(z, y, x) for z in range(4) for y in range(4)] for x in range(2)]
SWAP_X = [(i, i ^ 1) for i in range(32)]
SWAP_CORE = [(m, m ^ 1) for m in range(4)]
SWAP_FAR = [(m, m ^ 2) for m in range(4)]
TURN = [
    (m * 32 + z * 8 + q, z * 32 + m * 8 + q) for m in range(4) for z in range(4) for q in range(8)
]


def ring(place, k):
    return [(i, i + ((i // place + k) % 4 - i // place % 4) * place) for i in range(32)]


RING_Z = [ring(8, k) for k in (1, 2, 3)]
RING_Y = [ring(2, k) for k in (1, 2, 3)]


def swap_x(v):
    return lax.ppermute(v, "dp", SWAP_X)


def swap_core(v):
    return lax.ppermute(v, "grp", SWAP_CORE)


def swap_far(v):
    return lax.ppermute(v, "grp", SWAP_FAR)


def turn(v):
    return lax.ppermute(v, ("grp", "dp"), TURN)


def plane_gather(v):
    return lax.all_gather(v, "dp", axis=0, tiled=True, axis_index_groups=PLANES)


def plane_scatter(v):
    return lax.psum_scatter(
        v, "dp", scatter_dimension=0, tiled=True, axis_index_groups=PLANES
    )


def group_gather(v):
    pair = jnp.concatenate([v, swap_far(v)], axis=0)
    return jnp.concatenate([pair, swap_core(pair)], axis=0)


def group_scatter(partial):
    half = 2 * ROWS
    near = partial[:half] + swap_core(partial[half:].astype(BF)).astype(F32)
    return near[:ROWS] + swap_far(near[ROWS:].astype(BF)).astype(F32)


def pair_x(v, low):
    other = swap_x(v)
    return jnp.concatenate([jnp.where(low, v, other), jnp.where(low, other, v)], axis=0)


def sum_x(v, low):
    rows = v.shape[0] // 2
    mine = jnp.where(low, v[:rows], v[rows:])
    theirs = jnp.where(low, v[rows:], v[:rows])
    return mine.astype(F32) + swap_x(theirs).astype(F32)


def dot(left, right):
    return jnp.dot(left, right, preferred_element_type=F32)


def left_product(left, right):
    return lax.dot_general(left, right, (((0,), (0,)), ((), ())), preferred_element_type=F32)


def right_product(left, right):
    return lax.dot_general(left, right, (((1,), (1,)), ((), ())), preferred_element_type=F32)


def rounded_gain(gain):
    return lax.optimization_barrier(gain.astype(BF)).astype(F32)


def inverse_rms(v):
    return lax.rsqrt(jnp.mean(v * v, axis=-1, keepdims=True) + epsilon)


def norm_back(v, gain, grad):
    r = inverse_rms(v)
    n = v * r
    scaled = grad * gain
    return r * (scaled - n * jnp.mean(scaled * n, axis=-1, keepdims=True)), n


def turned(v):
    half = HEAD_DIM // 2
    lane = lax.broadcasted_iota(jnp.int32, v.shape, v.ndim - 1) % HEAD_DIM
    return jnp.where(lane < half, -jnp.roll(v, -half, axis=-1), jnp.roll(v, half, axis=-1))


def on_device(
    tokens,
    cotangent,
    segment_ids,
    positions,
    padding,
    attn_gain,
    query_weight,
    key_weight,
    value_weight,
    output_weight,
    mlp_gain,
    gate_weight,
    up_weight,
    down_weight,
    attn_moment,
    query_moment,
    key_moment,
    value_moment,
    output_moment,
    mlp_moment,
    gate_moment,
    up_moment,
    down_moment,
):
    member = lax.axis_index("grp")
    low = (lax.axis_index("dp") % 2) == 0

    def mine(weight, width):
        return lax.dynamic_slice_in_dim(weight, member * width, width, 1).astype(BF)

    out_block = turn(mine(output_weight, QW))
    attn_shard = jnp.concatenate(
        [mine(query_weight, QW), mine(key_weight, KW), mine(value_weight, KW), out_block], axis=1
    )
    attn_full = plane_gather(pair_x(attn_shard, low))
    qkv_full = attn_full[:, :QKVW]
    out_full = attn_full[:, QKVW:].reshape(4, QW, PANEL)

    gu_shard = pair_x(
        jnp.concatenate([mine(gate_weight, FW), mine(up_weight, FW)], axis=1), low
    )
    down_shard = pair_x(turn(mine(down_weight, PANEL)), low)
    pieces = [gu_shard[:, j * PANEL : (j + 1) * PANEL] for j in range(5)]
    tail = gu_shard[:, 5 * PANEL :]
    pieces.append(jnp.concatenate([tail[:W_ROWS], tail[W_ROWS:]], axis=1))
    pieces.append(down_shard)
    mlp_full = plane_gather(jnp.concatenate(pieces, axis=0)).reshape(16, 1056, PANEL)
    gu_panels = [mlp_full[:, j * 128 : (j + 1) * 128].reshape(D, PANEL) for j in range(5)]
    last = mlp_full[:, 640:704]
    gu_panels.append(
        jnp.stack([last[:, :, :256], last[:, :, 256:]], axis=1).reshape(D, 256)
    )
    down_full = mlp_full[:, 704:].reshape(4, FW, PANEL)

    places = jnp.stack([segment_ids, positions, padding])
    places = group_gather(places[None])
    segments, spots, pads = places[:, 0], places[:, 1], places[:, 2]
    rows_in = group_gather(tokens)
    grads_in = group_gather(cotangent)

    first_gain = rounded_gain(attn_gain)
    second_gain = rounded_gain(mlp_gain)
    inputs = rows_in.astype(F32)
    n_first = inputs * inverse_rms(inputs)
    first_low = (n_first * first_gain).astype(BF)

    qkv = dot(first_low, qkv_full)
    half = HEAD_DIM // 2
    freq = 10000.0 ** (-(jnp.arange(half, dtype=F32) * 2.0 / HEAD_DIM))
    angles = spots.reshape(SLOTS, 1).astype(F32) * jnp.tile(freq, 2)[None]
    cosine, sine = jnp.cos(angles), jnp.sin(angles)
    cosine_q, sine_q = jnp.tile(cosine, (1, GROUPS)), jnp.tile(sine, (1, GROUPS))

    q_lin, k_lin = qkv[:, :QW], qkv[:, QW : QW + KW]
    query_rot = (q_lin * cosine_q + turned(q_lin) * sine_q).astype(BF)
    key_rot = (k_lin * cosine + turned(k_lin) * sine).astype(BF)
    value_low = qkv[:, QW + KW :].astype(BF)
    query_rot = query_rot.reshape(MEMBERS, ROWS, GROUPS, HEAD_DIM)
    key_rot = key_rot.reshape(MEMBERS, ROWS, HEAD_DIM)
    value_low = value_low.reshape(MEMBERS, ROWS, HEAD_DIM)

    column = jnp.arange(ROWS, dtype=jnp.int32)
    allowed = jnp.logical_and(
        jnp.logical_and(
            segments[:, :, None] == segments[:, None, :],
            (column[None, :] <= column[:, None])[None],
        ),
        jnp.logical_or(pads[:, None, :] == 1, (column[None, :] == column[:, None])[None]),
    )
    scores = jnp.einsum("bqgd,bsd->bgqs", query_rot, key_rot, preferred_element_type=F32)
    masked = jnp.where(allowed[:, None], scores * score_scale, -1e30)
    row_max = jnp.max(masked, axis=-1, keepdims=True)
    log_total = row_max + jnp.log(jnp.sum(jnp.exp(masked - row_max), axis=-1, keepdims=True))
    probs = jnp.exp(masked - log_total)
    probs_low = probs.astype(BF)
    attended = jnp.einsum("bgqs,bsd->bqgd", probs_low, value_low, preferred_element_type=F32)
    attended_low = attended.reshape(SLOTS, QW).astype(BF)

    out_part = jnp.concatenate([dot(attended_low, out_full[c]) for c in range(4)], axis=1)
    middle = tokens.astype(F32) + group_scatter(out_part)
    second_low = (middle * inverse_rms(middle) * second_gain).astype(BF)
    second_all = group_gather(second_low)

    gu = jnp.concatenate([dot(second_all, panel) for panel in gu_panels], axis=1)
    gate, up = gu[:, :FW], gu[:, FW:]
    sig = 1.0 / (1.0 + jnp.exp(-gate))
    silu = gate * sig
    active = (silu * up).astype(BF)
    down_part = jnp.concatenate([dot(active, down_full[c]) for c in range(4)], axis=1)
    block_output = (middle + group_scatter(down_part)).astype(BF)

    grad_product = sum(
        right_product(grads_in[:, c * PANEL : (c + 1) * PANEL], down_full[c]) for c in range(4)
    )
    grad_gate = (grad_product * up * sig * (1.0 + gate * (1.0 - sig))).astype(BF)
    grad_up = (grad_product * silu).astype(BF)
    grad_gu = jnp.concatenate([grad_gate, grad_up], axis=1)

    cuts = [grad_gu[:, j * PANEL : (j + 1) * PANEL] for j in range(5)] + [grad_gu[:, 5 * PANEL :]]
    sends = [left_product(second_all, cut).astype(BF) for cut in cuts]
    send = [block.reshape(16, 128, PANEL) for block in sends[:5]]
    tail = sends[5].reshape(16, 2, W_ROWS, 256)
    send.append(jnp.concatenate([tail[:, 0], tail[:, 1]], axis=2))
    grad_down = jnp.concatenate(
        [left_product(active, grads_in[:, c * PANEL : (c + 1) * PANEL]) for c in range(4)], axis=0
    ).astype(BF)
    send.append(grad_down.reshape(16, 2 * DOWN_ROWS, PANEL))
    mlp_sum = plane_scatter(jnp.concatenate(send, axis=1).reshape(16 * 1056, PANEL))

    grad_second = sum(right_product(cut, panel) for cut, panel in zip(cuts, gu_panels))
    grad_second = group_scatter(grad_second)
    back, n_second = norm_back(middle, second_gain, grad_second)
    mlp_gain_part = jnp.sum(grad_second * n_second, axis=0)
    grad_middle = cotangent.astype(F32) + back
    middle_all = group_gather(grad_middle.astype(BF))

    grad_out = jnp.concatenate(
        [
            left_product(attended_low, middle_all[:, c * PANEL : (c + 1) * PANEL])
            for c in range(4)
        ],
        axis=0,
    )
    grad_attended = sum(
        right_product(middle_all[:, c * PANEL : (c + 1) * PANEL], out_full[c]) for c in range(4)
    ).astype(BF)
    grad_attended = grad_attended.reshape(MEMBERS, ROWS, GROUPS, HEAD_DIM)

    grad_value = jnp.einsum(
        "bgqs,bqgd->bsd", probs_low, grad_attended, preferred_element_type=F32
    )
    grad_probs = jnp.einsum(
        "bqgd,bsd->bgqs", grad_attended, value_low, preferred_element_type=F32
    )
    grad_scores = (
        probs * (grad_probs - jnp.sum(grad_probs * probs, axis=-1, keepdims=True))
    ).astype(BF)
    grad_query = (
        jnp.einsum("bgqs,bsd->bqgd", grad_scores, key_rot, preferred_element_type=F32) * score_scale
    ).reshape(SLOTS, QW)
    grad_key = (
        jnp.einsum("bgqs,bqgd->bsd", grad_scores, query_rot, preferred_element_type=F32)
        * score_scale
    ).reshape(SLOTS, KW)
    grad_query = grad_query * cosine_q - turned(grad_query) * sine_q
    grad_key = grad_key * cosine - turned(grad_key) * sine
    grad_qkv = jnp.concatenate(
        [grad_query.astype(BF), grad_key.astype(BF), grad_value.reshape(SLOTS, KW).astype(BF)],
        axis=1,
    )

    qkv_send = left_product(first_low, grad_qkv)
    attn_sum = plane_scatter(
        jnp.concatenate([qkv_send.astype(BF), grad_out.astype(BF)], axis=1)
    )

    grad_first = right_product(grad_qkv, qkv_full)
    attn_gain_part = jnp.sum(grad_first * n_first, axis=0)
    grad_first = group_scatter(grad_first)
    back, _ = norm_back(tokens.astype(F32), first_gain, grad_first)
    input_grad = grad_middle + back

    gains = jnp.stack([attn_gain_part, mlp_gain_part])
    for ring in (RING_Z, RING_Y):
        gains = gains + sum(lax.ppermute(gains, "dp", pairs) for pairs in ring)
    gains = gains + swap_x(gains)
    gains = gains + swap_far(gains)
    gains = gains + swap_core(gains)

    gu_rows = sum_x(
        jnp.concatenate(
            [mlp_sum[j * 128 : (j + 1) * 128] for j in range(5)]
            + [jnp.concatenate([mlp_sum[640:704, :256], mlp_sum[640:704, 256:]], axis=0)],
            axis=1,
        ),
        low,
    )
    down_rows = turn(sum_x(mlp_sum[704:], low).astype(BF)).astype(F32)
    attn_rows = sum_x(attn_sum, low)
    out_rows = turn(attn_rows[:, QKVW:].astype(BF)).astype(F32)

    def step(moment, total):
        return 0.5 * moment + 0.5 * total

    gate_momentum = step(gate_moment, gu_rows[:, :FW])
    up_momentum = step(up_moment, gu_rows[:, FW:])
    down_momentum = step(down_moment, down_rows)
    query_momentum = step(query_moment, attn_rows[:, :QW])
    key_momentum = step(key_moment, attn_rows[:, QW : QW + KW])
    value_momentum = step(value_moment, attn_rows[:, QW + KW : QKVW])
    output_momentum = step(output_moment, out_rows)

    mine_at = (member // 2) + 2 * (member % 2)

    def spread(momentum):
        rows, width = momentum.shape
        slots = group_gather(momentum.astype(BF)).reshape(MEMBERS, rows, width)
        return [
            lax.dynamic_index_in_dim(slots, mine_at ^ at, 0, keepdims=False) for at in (0, 2, 1, 3)
        ]

    def updated(weight, columns, start, width):
        moved = jnp.concatenate([block[:, start : start + width] for block in columns], axis=1)
        return weight - learn_rate * moved.astype(F32)

    attn_moved = spread(
        jnp.concatenate(
            [query_momentum, key_momentum, value_momentum, output_momentum], axis=1
        )
    )
    gu_moved = spread(jnp.concatenate([gate_momentum, up_momentum], axis=1))
    down_moved = spread(down_momentum)

    gains = 0.5 * jnp.stack([attn_moment, mlp_moment]) + 0.5 * gains
    return (
        block_output,
        input_grad,
        gains[0],
        query_momentum,
        key_momentum,
        value_momentum,
        output_momentum,
        gains[1],
        gate_momentum,
        up_momentum,
        down_momentum,
        attn_gain - learn_rate * gains[0],
        updated(query_weight, attn_moved, 0, QW),
        updated(key_weight, attn_moved, QW, KW),
        updated(value_weight, attn_moved, QW + KW, KW),
        updated(output_weight, attn_moved, QKVW, PANEL),
        mlp_gain - learn_rate * gains[1],
        updated(gate_weight, gu_moved, 0, FW),
        updated(up_weight, gu_moved, FW, FW),
        updated(down_weight, down_moved, 0, PANEL),
    )


def solution(mesh):
    rows = P(("grp", "dp"), None)
    flat = P(("grp", "dp"))
    weight = P("dp", None)
    moment = P("dp", "grp")
    whole = P()
    weights = (whole,) + (weight,) * 4 + (whole,) + (weight,) * 3
    moments = (whole,) + (moment,) * 4 + (whole,) + (moment,) * 3
    return jax.shard_map(
        on_device,
        mesh=mesh,
        in_specs=(rows, rows, flat, flat, flat) + weights + moments,
        out_specs=(rows, rows) + moments + weights,
        check_vma=False,
    )
```

time: 4210 us -> 632 us (0.15)
  waiting for transfers between devices: 3630 us -> 227 us
  blocking collectives: 264 us -> 0 us
  starting transfers between devices: 1.25 us -> 101 us
  other arithmetic: 33.2 us -> 86.5 us
  matrix products: 165 us -> 113 us
    all_gather x7 -> x2, waiting for transfers between devices: 2120 us -> 56.4 us  [plane_gather(): return lax.all_gather(v, 'dp', axis=0, tiled=True, axis_index_groups=PLANES)]
    reduce_scatter x10 -> x2, waiting for transfers between devices: 959 us -> 51.9 us  [plane_scatter(): lax.psum_scatter(v, 'dp', scatter_dimension=0, tiled=True, axis_index_gro...]
    unnamed x25 -> x4, waiting for transfers between devices: 547 us -> 0.07 us
    all_gather x7 -> x0, blocking collectives: 198 us -> none  [the longest x1 33.2 us: on_device(): lax.all_gather(key_mine.astype(jnp.bfloat16), 'grp', axis=1, tiled=True)]
    ppermute x0 -> x43, waiting for transfers between devices: none -> 118 us  [the longest x13 80.8 us: swap_far(): return lax.ppermute(v, 'grp', SWAP_FAR)]
    ppermute x0 -> x43, starting transfers between devices: none -> 101 us  [the longest x13 47.7 us: swap_far(): return lax.ppermute(v, 'grp', SWAP_FAR)]
    psum x1 -> x0, blocking collectives: 65.8 us -> none  [on_device(): lax.psum((grad_attn_gain, grad_mlp_gain), ('grp', 'dp'))]
    unnamed x92 -> x256, local copies, waits for them, and re-layouts: 93 us -> 39.6 us
  transfers between devices with their start and end apart: 21 -> 47, of which waited for: 19 -> 30; matrix products, arithmetic and copies ran while one was open for 5% -> 25% of each run, Pallas kernels for 0% -> 0%
where the time goes in v1:
time: 632 us; the launch traced here: 627 us
  waiting for transfers between devices  227 us (36%)
  matrix products  113 us (18%)
  starting transfers between devices  101 us (16%)
  other arithmetic  86.5 us (14%)
  local copies, waits for them, and re-layouts  83.2 us (13%)
  between operations  16.1 us (3%)
    ppermute x13, waiting for transfers between devices, swap_far(): return lax.ppermute(v, 'grp', SWAP_FAR)  80.8 us
    all_gather x2, waiting for transfers between devices, plane_gather(): return lax.all_gather(v, 'dp', axis=0, tiled=True, axis_index_groups=PLANES)  56.4 us
    reduce_scatter x2, waiting for transfers between devices, plane_scatter(): lax.psum_scatter(v, 'dp', scatter_dimension=0, tiled=True, axis_index_gro...  51.9 us
    ppermute x13, starting transfers between devices, swap_far(): return lax.ppermute(v, 'grp', SWAP_FAR)  47.7 us
    dot_general x15, matrix products, right_product(): lax.dot_general(left, right, (((1,), (1,)), ((), ())), preferred_element_...  45.2 us
    unnamed x256, local copies, waits for them, and re-layouts  39.6 us
    dot_general x15, matrix products, dot(): return jnp.dot(left, right, preferred_element_type=F32)  34.1 us
    dot_general x15, matrix products, left_product(): lax.dot_general(left, right, (((0,), (0,)), ((), ())), preferred_element_...  30.5 us
  transfers between devices with their start and end apart: 47, of which 30 were waited for; matrix products, arithmetic and copies ran while one was open for 25% of the time, Pallas kernels for 0%

profile of v1, /device:TPU:1, one launch (start us, length us, event | category | flops | bytes accessed | tf_op | source)
XLA Modules:
  0.0 626.6 jit_solution(6458780294109950029)
XLA Ops:
  23.5 5.1 collective-permute-start.11
  37.6 16.3 %collective-permute-start = (bf16[128,2048]{1,0:T(8,128)(2,1)S(1)}, bf16[128,2048]{1,0:T(8,128)(2,1)S(1)}, u32[]{:S(2)}, u32[]{:S(2)}) collective-permute-start(bf16[128,2048]{1,0:T(8,128)(2,1)S(1)} %copy-done.28), channel_id=1, source_target_pairs={{0,64},{32,96},{64,0},{96,32},{1,65},{33,97},{65,1},{97,33},{2,66}... | collective-permute-start | bytes 1572872 | tf_op jit(solution)/shard_map/ppermute | solution.py:60
  54.5 11.5 %collective-permute-done = bf16[128,2048]{1,0:T(8,128)(2,1)S(1)} collective-permute-done((bf16[128,2048]{1,0:T(8,128)(2,1)S(1)}, bf16[128,2048]{1,0:T(8,128)(2,1)S(1)}, u32[]{:S(2)}, u32[]{:S(2)}) %collective-permute-start) | collective-permute-done | bytes 524320 | tf_op jit(solution)/shard_map/ppermute | solution.py:60
  71.2 12.2 %all-gather.3.cloned.1.call-done = bf16[2048,1152]{1,0:T(8,128)(2,1)} async-done(((bf16[128,1152]{1,0:T(8,128)(2,1)}), bf16[2048,1152]{1,0:T(8,128)(2,1)}) %all-gather.3.cloned.1.call-update) | async-done | bytes 4718608 | tf_op jit(solution)/shard_map/all_gather | solution.py:68
  118.7 5.9 collective-permute-done.15
  129.1 6.8 %collective-permute-done.7 = bf16[128,2048]{0,1:T(8,128)(2,1)} collective-permute-done((bf16[128,2048]{0,1:T(8,128)(2,1)}, bf16[128,2048]{0,1:T(8,128)(2,1)}, u32[]{:S(2)}, u32[]{:S(2)}) %collective-permute-start.7) | collective-permute-done | bytes 524320 | tf_op jit(solution)/shard_map/ppermute | solution.py:60
  145.3 6.6 %collective-permute-done.8 = bf16[128,2048]{0,1:T(8,128)(2,1)S(1)} collective-permute-done((bf16[128,2048]{0,1:T(8,128)(2,1)S(1)}, bf16[128,2048]{0,1:T(8,128)(2,1)S(1)}, u32[]{:S(2)}, u32[]{:S(2)}) %collective-permute-start.8) | collective-permute-done | bytes 524320 | tf_op jit(solution)/shard_map/ppermute | solution.py:60
  155.5 44.3 %all-gather.5.cloned.1.call-done = bf16[16896,512]{1,0:T(8,128)(2,1)} async-done(((bf16[1056,512]{1,0:T(8,128)(2,1)}), bf16[16896,512]{1,0:T(8,128)(2,1)}) %all-gather.5.cloned.1.call-update) | async-done | bytes 17301520 | tf_op jit(solution)/shard_map/all_gather | solution.py:68
  204.1 6.0 fusion.78
  236.5 6.9 %multiply_convert_fusion.1 = (bf16[512,1408]{0,1:T(8,128)(2,1)S(1)}, bf16[512,1408]{0,1:T(8,128)(2,1)S(1)}, bf16[512,1408]{0,1:T(8,128)(2,1)}) fusion(f32[512,512]{0,1:T(8,128)S(1)} %fusion.132, f32[512,512]{0,1:T(8,128)S(1)} %fusion.133, f32[512,512]{0,1:T(8,128)S(1)} %fusion.134, f32[512,256]{0,1:T(8,128)S(1)} %fusion.129, f32[512,512]{0,1:T(8,128)} %fusion.130, ...), kind=kOutput, calls=%fused_computation.31 | convolution fusion | flops 754778112 | bytes 20709376 | tf_op jit(solution)/shard_map/dot_general | solution.py:109
  256.5 5.6 add_add_fusion
  276.4 7.5 %collective-permute-done.18 = bf16[128,2048]{0,1:T(8,128)(2,1)} collective-permute-done((bf16[128,2048]{0,1:T(8,128)(2,1)}, bf16[128,2048]{0,1:T(8,128)(2,1)}, u32[]{:S(2)}, u32[]{:S(2)}) %collective-permute-start.18) | collective-permute-done | bytes 524320 | tf_op jit(solution)/shard_map/ppermute | solution.py:60
  286.0 9.2 %collective-permute-done.14 = bf16[128,2048]{0,1:T(8,128)(2,1)} collective-permute-done((bf16[128,2048]{0,1:T(8,128)(2,1)}, bf16[128,2048]{0,1:T(8,128)(2,1)}, u32[]{:S(2)}, u32[]{:S(2)}) %collective-permute-start.14) | collective-permute-done | bytes 524320 | tf_op jit(solution)/shard_map/ppermute | solution.py:60
  301.1 10.6 %collective-permute-done.19 = bf16[128,2048]{0,1:T(8,128)(2,1)S(1)} collective-permute-done((bf16[128,2048]{0,1:T(8,128)(2,1)S(1)}, bf16[128,2048]{0,1:T(8,128)(2,1)S(1)}, u32[]{:S(2)}, u32[]{:S(2)}) %collective-permute-start.19) | collective-permute-done | bytes 524320 | tf_op jit(solution)/shard_map/ppermute | solution.py:60
  347.5 18.1 %maximum_maximum_fusion = bf16[2048,1152]{0,1:T(8,128)(2,1)} fusion(bf16[512,512]{0,1:T(8,128)(2,1)S(1)} %copy-done.73, bf16[512,512]{0,1:T(8,128)(2,1)S(1)} %copy-done.74, bf16[512,512]{0,1:T(8,128)(2,1)S(1)} %copy-done.75, bf16[512,512]{0,1:T(8,128)(2,1)S(1)} %copy-done.76, bf16[2048,640]{0,1:T(8,128)(2,1)S(1)} %convolution_convert_fusion), kind=kLoop, calls=%fused_computation.5 | loop fusion | flops 23592960 | bytes 9437184 | tf_op jit(solution)/shard_map/concatenate | solution.py:307
  365.6 6.7 %copy.244 = bf16[2048,1152]{1,0:T(8,128)(2,1)} copy(bf16[2048,1152]{0,1:T(8,128)(2,1)} %maximum_maximum_fusion) | data formatting | bytes 9437184
  402.1 20.1 %pad_maximum_fusion = bf16[5632,512]{1,0:T(8,128)(2,1)S(1)} fusion(bf16[1408,512]{1,0:T(8,128)(2,1)S(1)} %convolution_convert_fusion.1, bf16[1408,512]{1,0:T(8,128)(2,1)S(1)} %convolution_convert_fusion.2, bf16[1408,512]{1,0:T(8,128)(2,1)S(1)} %convolution_convert_fusion.3, bf16[1408,512]{1,0:T(8,128)(2,1)S(1)} %convolution_convert_fusion.4), kind=kLoop, calls=%fused_computation | loop fusion | flops 23068672 | bytes 11534336 | tf_op jit(solution)/shard_map/concatenate | solution.py:257
  426.7 5.6 fusion.3
  451.9 5.8 collective-permute-start.31
  475.1 10.4 %collective-permute-done.22 = bf16[128,2048]{0,1:T(8,128)(2,1)S(1)} collective-permute-done((bf16[128,2048]{0,1:T(8,128)(2,1)}, bf16[128,2048]{0,1:T(8,128)(2,1)S(1)}, u32[]{:S(2)}, u32[]{:S(2)}) %collective-permute-start.22) | collective-permute-done | bytes 524320 | tf_op jit(solution)/shard_map/ppermute | solution.py:60
  515.7 51.9 %reduce-scatter.5.cloned.1.call-done = bf16[1056,512]{1,0:T(8,128)(2,1)} async-done(((bf16[16896,512]{1,0:T(8,128)(2,1)}), bf16[1056,512]{1,0:T(8,128)(2,1)}) %reduce-scatter.5.cloned.1.call-update) | async-done | bytes 1081360 | tf_op jit(solution)/shard_map/reduce_scatter | solution.py:72
  574.9 11.2 %collective-permute-done.35 = bf16[176,512]{1,0:T(8,128)(2,1)S(1)} collective-permute-done((bf16[176,512]{1,0:T(8,128)(2,1)S(1)}, bf16[176,512]{1,0:T(8,128)(2,1)S(1)}, u32[]{:S(2)}, u32[]{:S(2)}) %collective-permute-start.35) | collective-permute-done | bytes 180256 | tf_op jit(solution)/shard_map/ppermute | solution.py:52
  586.1 4.9 collective-permute-start.36
  602.2 9.0 %collective-permute-done.41 = bf16[176,512]{1,0:T(8,128)(2,1)S(1)} collective-permute-done((bf16[176,512]{1,0:T(8,128)(2,1)S(1)}, bf16[176,512]{1,0:T(8,128)(2,1)S(1)}, u32[]{:S(2)}, u32[]{:S(2)}) %collective-permute-start.41) | collective-permute-done | bytes 180256 | tf_op jit(solution)/shard_map/ppermute | solution.py:60
  (542 shorter events, 312.3 us)
Async XLA Ops:
  7.2 76.2 %all-gather.3.cloned.1.call-start = ((), (), s32[]{:S(2)}) async-start(), calls=%async_computation.2 | async-start | bytes 5013504 | tf_op jit(solution)/shard_map/all_gather | solution.py:68
  20.0 179.8 %all-gather.5.cloned.1.call-start = ((), (), s32[]{:S(2)}) async-start(), calls=%async_computation.3 | async-start | bytes 18382848 | tf_op jit(solution)/shard_map/all_gather | solution.py:68
  21.2 11.1 %collective-permute-start.10 = (bf16[64,2816]{1,0:T(8,128)(2,1)S(1)}, bf16[64,2816]{1,0:T(8,128)(2,1)S(1)}, u32[]{:S(2)}, u32[]{:S(2)}) collective-permute-start(bf16[64,2816]{1,0:T(8,128)(2,1)S(1)} %pad_maximum_fusion.22), channel_id=1, source_target_pairs={{0,1},{1,0},{2,3},{3,2},{4,5},{5,4},{6,7},{7,6},{8,9},{9,8},{10,11... | collective-permute-start | bytes 1081352 | tf_op jit(solution)/shard_map/ppermute | solution.py:52
  23.5 8.5 %collective-permute-start.11 = (bf16[176,512]{1,0:T(8,128)(2,1)S(1)}, bf16[176,512]{1,0:T(8,128)(2,1)S(1)}, u32[]{:S(2)}, u32[]{:S(2)}) collective-permute-start(bf16[176,512]{1,0:T(8,128)(2,1)S(1)} %dynamic-slice_convert_fusion), channel_id=1, source_target_pairs={{0,0},{1,1},{2,2},{3,3},{4,4},{5,5},{6,6},{7,7},{8,32},{9,33},{10,... | collective-permute-start | bytes 540680 | tf_op jit(solution)/shard_map/ppermute | solution.py:64
  37.5 436.1 %reduce-scatter.7.cloned.1.call-start = ((), (), s32[]{:S(2)}) async-start(), calls=%async_computation.5 | async-start | bytes 5013504 | tf_op jit(solution)/shard_map/reduce_scatter | solution.py:72
  37.6 28.5 %collective-permute-start = (bf16[128,2048]{1,0:T(8,128)(2,1)S(1)}, bf16[128,2048]{1,0:T(8,128)(2,1)S(1)}, u32[]{:S(2)}, u32[]{:S(2)}) collective-permute-start(bf16[128,2048]{1,0:T(8,128)(2,1)S(1)} %copy-done.28), channel_id=1, source_target_pairs={{0,64},{32,96},{64,0},{96,32},{1,65},{33,97},{65,1},{97,33},{2,66}... | collective-permute-start | bytes 1572872 | tf_op jit(solution)/shard_map/ppermute | solution.py:60
  53.9 13.7 %collective-permute-start.4 = (s32[1,3,128]{2,1,0:T(4,128)S(1)}, s32[1,3,128]{2,1,0:T(4,128)S(1)}, u32[]{:S(2)}, u32[]{:S(2)}) collective-permute-start(s32[1,3,128]{2,1,0:T(4,128)S(1)} %add_bitcast_fusion), channel_id=1, source_target_pairs={{0,64},{32,96},{64,0},{96,32},{1,65},{33,97},{65,1},{97,33},{2,66}... | collective-permute-start | bytes 4616 | tf_op jit(solution)/shard_map/ppermute | solution.py:60
  110.2 14.4 %collective-permute-start.15 = (bf16[128,2048]{1,0:T(8,128)(2,1)S(1)}, bf16[128,2048]{1,0:T(8,128)(2,1)}, u32[]{:S(2)}, u32[]{:S(2)}) collective-permute-start(bf16[128,2048]{1,0:T(8,128)(2,1)S(1)} %copy-done.34), channel_id=1, source_target_pairs={{0,64},{32,96},{64,0},{96,32},{1,65},{33,97},{65,1},{97,33},{2,66}... | collective-permute-start | bytes 1572872 | tf_op jit(solution)/shard_map/ppermute | solution.py:60
  115.6 20.2 %collective-permute-start.7 = (bf16[128,2048]{0,1:T(8,128)(2,1)}, bf16[128,2048]{0,1:T(8,128)(2,1)}, u32[]{:S(2)}, u32[]{:S(2)}) collective-permute-start(bf16[128,2048]{0,1:T(8,128)(2,1)} %slice.828), channel_id=1, source_target_pairs={{0,64},{32,96},{64,0},{96,32},{1,65},{33,97},{65,1},{97,33},{2,66}... | collective-permute-start | bytes 1572872 | tf_op jit(solution)/shard_map/ppermute | solution.py:60
  125.8 18.4 %collective-permute-start.16 = (bf16[256,2048]{1,0:T(8,128)(2,1)S(1)}, bf16[256,2048]{1,0:T(8,128)(2,1)S(1)}, u32[]{:S(2)}, u32[]{:S(2)}) collective-permute-start(bf16[256,2048]{1,0:T(8,128)(2,1)S(1)} %pad_maximum_fusion.15), channel_id=1, source_target_pairs={{0,32},{32,0},{64,96},{96,64},{1,33},{33,1},{65,97},{97,65},{2,34}... | collective-permute-start | bytes 3145736 | tf_op jit(solution)/shard_map/ppermute | solution.py:56
  138.5 13.4 %collective-permute-start.8 = (bf16[128,2048]{0,1:T(8,128)(2,1)S(1)}, bf16[128,2048]{0,1:T(8,128)(2,1)S(1)}, u32[]{:S(2)}, u32[]{:S(2)}) collective-permute-start(bf16[128,2048]{0,1:T(8,128)(2,1)S(1)} %multiply_convert_fusion.3), channel_id=1, source_target_pairs={{0,64},{32,96},{64,0},{96,32},{1,65},{33,97},{65,1},{97,33},{2,66}... | collective-permute-start | bytes 1572872 | tf_op jit(solution)/shard_map/ppermute | solution.py:60
  153.1 65.9 %collective-permute-start.9 = (bf16[256,2048]{0,1:T(8,128)(2,1)}, bf16[256,2048]{0,1:T(8,128)(2,1)}, u32[]{:S(2)}, u32[]{:S(2)}) collective-permute-start(bf16[256,2048]{0,1:T(8,128)(2,1)} %pad_maximum_fusion.13), channel_id=1, source_target_pairs={{0,32},{32,0},{64,96},{96,64},{1,33},{33,1},{65,97},{97,65},{2,34}... | collective-permute-start | bytes 3145736 | tf_op jit(solution)/shard_map/ppermute | solution.py:56
  269.3 14.6 %collective-permute-start.18 = (bf16[128,2048]{0,1:T(8,128)(2,1)}, bf16[128,2048]{0,1:T(8,128)(2,1)}, u32[]{:S(2)}, u32[]{:S(2)}) collective-permute-start(bf16[128,2048]{0,1:T(8,128)(2,1)} %slice.826), channel_id=1, source_target_pairs={{0,64},{32,96},{64,0},{96,32},{1,65},{33,97},{65,1},{97,33},{2,66}... | collective-permute-start | bytes 1572872 | tf_op jit(solution)/shard_map/ppermute | solution.py:60
  273.9 21.2 %collective-permute-start.14 = (bf16[128,2048]{0,1:T(8,128)(2,1)}, bf16[128,2048]{0,1:T(8,128)(2,1)}, u32[]{:S(2)}, u32[]{:S(2)}) collective-permute-start(bf16[128,2048]{0,1:T(8,128)(2,1)} %slice.827), channel_id=1, source_target_pairs={{0,64},{32,96},{64,0},{96,32},{1,65},{33,97},{65,1},{97,33},{2,66}... | collective-permute-start | bytes 1572872 | tf_op jit(solution)/shard_map/ppermute | solution.py:60
  298.4 13.3 %collective-permute-start.19 = (bf16[128,2048]{0,1:T(8,128)(2,1)S(1)}, bf16[128,2048]{0,1:T(8,128)(2,1)S(1)}, u32[]{:S(2)}, u32[]{:S(2)}) collective-permute-start(bf16[128,2048]{0,1:T(8,128)(2,1)S(1)} %get-tuple-element.96), channel_id=1, source_target_pairs={{0,64},{32,96},{64,0},{96,32},{1,65},{33,97},{65,1},{97,33},{2,66}... | collective-permute-start | bytes 1572872 | tf_op jit(solution)/shard_map/ppermute | solution.py:60
  372.4 195.2 %reduce-scatter.5.cloned.1.call-start = ((), (), s32[]{:S(2)}) async-start(), calls=%async_computation.4 | async-start | bytes 18382848 | tf_op jit(solution)/shard_map/reduce_scatter | solution.py:72
  451.9 12.9 %collective-permute-start.31 = (f32[2,2048]{1,0:T(2,128)S(1)}, f32[2,2048]{1,0:T(2,128)S(1)}, u32[]{:S(2)}, u32[]{:S(2)}) collective-permute-start(f32[2,2048]{1,0:T(2,128)S(1)} %add.303), channel_id=1, source_target_pairs={{0,32},{32,0},{64,96},{96,64},{1,33},{33,1},{65,97},{97,65},{2,34}... | collective-permute-start | bytes 49160 | tf_op jit(solution)/shard_map/ppermute | solution.py:56
  470.2 15.2 %collective-permute-start.22 = (bf16[128,2048]{0,1:T(8,128)(2,1)}, bf16[128,2048]{0,1:T(8,128)(2,1)S(1)}, u32[]{:S(2)}, u32[]{:S(2)}) collective-permute-start(bf16[128,2048]{0,1:T(8,128)(2,1)} %slice.825), channel_id=1, source_target_pairs={{0,64},{32,96},{64,0},{96,32},{1,65},{33,97},{65,1},{97,33},{2,66}... | collective-permute-start | bytes 1572872 | tf_op jit(solution)/shard_map/ppermute | solution.py:60
  474.7 14.1 %collective-permute-start.32 = (bf16[64,1152]{1,0:T(8,128)(2,1)S(1)}, bf16[64,1152]{1,0:T(8,128)(2,1)S(1)}, u32[]{:S(2)}, u32[]{:S(2)}) collective-permute-start(bf16[64,1152]{1,0:T(8,128)(2,1)S(1)} %broadcast_select_fusion.4), channel_id=1, source_target_pairs={{0,1},{1,0},{2,3},{3,2},{4,5},{5,4},{6,7},{7,6},{8,9},{9,8},{10,11... | collective-permute-start | bytes 442376 | tf_op jit(solution)/shard_map/ppermute | solution.py:52
  573.1 18.0 %collective-permute-start.34 = (bf16[64,2816]{1,0:T(8,128)(2,1)S(1)}, bf16[64,2816]{1,0:T(8,128)(2,1)S(1)}, u32[]{:S(2)}, u32[]{:S(2)}) collective-permute-start(bf16[64,2816]{1,0:T(8,128)(2,1)S(1)} %broadcast_select_fusion), channel_id=1, source_target_pairs={{0,1},{1,0},{2,3},{3,2},{4,5},{5,4},{6,7},{7,6},{8,9},{9,8},{10,11... | collective-permute-start | bytes 1081352 | tf_op jit(solution)/shard_map/ppermute | solution.py:52
  574.3 11.7 %collective-permute-start.35 = (bf16[176,512]{1,0:T(8,128)(2,1)S(1)}, bf16[176,512]{1,0:T(8,128)(2,1)S(1)}, u32[]{:S(2)}, u32[]{:S(2)}) collective-permute-start(bf16[176,512]{1,0:T(8,128)(2,1)S(1)} %broadcast_select_fusion.3), channel_id=1, source_target_pairs={{0,1},{1,0},{2,3},{3,2},{4,5},{5,4},{6,7},{7,6},{8,9},{9,8},{10,11... | collective-permute-start | bytes 540680 | tf_op jit(solution)/shard_map/ppermute | solution.py:52
  586.1 10.3 %collective-permute-start.36 = (bf16[176,512]{1,0:T(8,128)(2,1)S(1)}, bf16[176,512]{1,0:T(8,128)(2,1)S(1)}, u32[]{:S(2)}, u32[]{:S(2)}) collective-permute-start(bf16[176,512]{1,0:T(8,128)(2,1)S(1)} %add_convert_fusion), channel_id=1, source_target_pairs={{0,0},{1,1},{2,2},{3,3},{4,4},{5,5},{6,6},{7,7},{8,32},{9,33},{10,... | collective-permute-start | bytes 540680 | tf_op jit(solution)/shard_map/ppermute | solution.py:64
  592.2 20.8 %collective-permute-start.39 = (bf16[64,2816]{1,0:T(8,128)(2,1)S(1)}, bf16[64,2816]{1,0:T(8,128)(2,1)S(1)}, u32[]{:S(2)}, u32[]{:S(2)}) collective-permute-start(bf16[64,2816]{1,0:T(8,128)(2,1)S(1)} %pad_maximum_fusion.23), channel_id=1, source_target_pairs={{0,64},{32,96},{64,0},{96,32},{1,65},{33,97},{65,1},{97,33},{2,66}... | collective-permute-start | bytes 1081352 | tf_op jit(solution)/shard_map/ppermute | solution.py:60
  597.2 13.9 %collective-permute-start.41 = (bf16[176,512]{1,0:T(8,128)(2,1)S(1)}, bf16[176,512]{1,0:T(8,128)(2,1)S(1)}, u32[]{:S(2)}, u32[]{:S(2)}) collective-permute-start(bf16[176,512]{1,0:T(8,128)(2,1)S(1)} %get-tuple-element.82), channel_id=1, source_target_pairs={{0,64},{32,96},{64,0},{96,32},{1,65},{33,97},{65,1},{97,33},{2,66}... | collective-permute-start | bytes 540680 | tf_op jit(solution)/shard_map/ppermute | solution.py:60
  (141 other events, 1215.5 us)
Sparse Core Ops, SparseCore 0:
  20.1 63.1 all-gather.2
  86.1 113.6 all-gather.4
  372.5 76.3 reduce-scatter.6
  452.2 115.3 reduce-scatter.4

commit v2 on v1

--- a/solution.py
+++ b/solution.py
@@ -1,6 +1,8 @@
 import jax
 import jax.numpy as jnp
 from jax import lax
+from jax.experimental import pallas as pl
+from jax.experimental.pallas import tpu as pltpu
 from jax.sharding import PartitionSpec as P
 
 D = 2048
@@ -38,6 +40,8 @@
 TURN = [
     (m * 32 + z * 8 + q, z * 32 + m * 8 + q) for m in range(4) for z in range(4) for q in range(8)
 ]
+TURN_X = [(a, b ^ 1) for a, b in TURN]
+SWAP_FAR_X = [(m * 32 + i, (m ^ 2) * 32 + (i ^ 1)) for m in range(4) for i in range(32)]
 
 
 def ring(place, k):
@@ -62,6 +66,12 @@
 
 def turn(v):
     return lax.ppermute(v, ("grp", "dp"), TURN)
+
+
+def turn_pair(v, low):
+    own = turn(v)
+    other = lax.ppermute(v, ("grp", "dp"), TURN_X)
+    return jnp.concatenate([jnp.where(low, own, other), jnp.where(low, other, own)], axis=0)
 
 
 def plane_gather(v):
@@ -109,6 +119,110 @@
     return lax.dot_general(left, right, (((1,), (1,)), ((), ())), preferred_element_type=F32)
 
 
+def tail_in(full, tail, sems):
+    return [pltpu.make_async_copy(full.at[:, pl.ds(640,64), pl.ds(256*h,256)], tail.at[:, pl.ds(64*h,64), :], sems.at[h]) for h in range(2)]
+
+def mlp_kernel(s_ref, st_ref, c_ref, panel_ref, full, ggu_ref, act_ref, send,
+               down, tail, gpan, gtail, gdown, in_sem, tail_sem, pan_sem, out_sem):
+    j = pl.program_id(0)
+    loads = [pltpu.make_async_copy(full.at[4*c+y, pl.ds(704,352), :], down.at[c, pl.ds(352*y,352), :], in_sem.at[4*c+y]) for c in range(4) for y in range(4)]
+    tails = tail_in(full, tail, tail_sem)
+    @pl.when(j == 0)
+    def _():
+        for l in loads: l.start()
+        for t in tails: t.start()
+
+    def panel_out(slot, at):
+        return pltpu.make_async_copy(gpan.at[slot], send.at[:, pl.ds(128*at,128), :], pan_sem.at[slot])
+
+    def block(weights, start, width):
+        h = dot(s_ref[...], weights)
+        gate, up = h[:, :width], h[:, width:]
+        @pl.when(j == 0)
+        def _():
+            for l in loads: l.wait()
+        prod = right_product(c_ref[:, :PANEL], down[0, pl.ds(start,width), :])
+        for c in range(1,4):
+            prod += right_product(c_ref[:, c*PANEL:(c+1)*PANEL], down[c, pl.ds(start,width), :])
+        sig = 1.0/(1.0+jnp.exp(-gate))
+        silu = gate*sig
+        act = (silu*up).astype(BF)
+        grad = jnp.concatenate([(prod*up*sig*(1.0+gate*(1.0-sig))).astype(BF),(prod*silu).astype(BF)],axis=1)
+        ggu_ref[:, :2*width] = grad
+        act_ref[:, :width] = act
+        for c in range(4):
+            gdown[c, pl.ds(start,width), :] = left_product(act, c_ref[:, c*PANEL:(c+1)*PANEL]).astype(BF)
+        return dot(st_ref[...], grad).astype(BF)
+
+    @pl.when(j < 5)
+    def _():
+        slot = lax.rem(j, 2)
+        g = block(panel_ref[...].reshape(2048, PANEL), pl.multiple_of(256*j, 256), 256)
+        @pl.when(j >= 2)
+        def _():
+            panel_out(slot, j-2).wait()
+        gpan[slot] = g.reshape(16,128,PANEL)
+        panel_out(slot, j).start()
+
+    @pl.when(j == 5)
+    def _():
+        for t in tails: t.wait()
+        g = block(tail[...].reshape(2048,256), 1280, 128)
+        gtail[...] = g.reshape(16,128,256)
+        outs = [pltpu.make_async_copy(gtail.at[:, pl.ds(64*h,64), :], send.at[:, pl.ds(640,64), pl.ds(256*h,256)], tail_sem.at[h]) for h in range(2)]
+        outs += [pltpu.make_async_copy(gdown.at[c, pl.ds(352*y,352), :], send.at[4*c+y, pl.ds(704,352), :], out_sem.at[4*c+y]) for c in range(4) for y in range(4)]
+        for o in outs: o.start()
+        panel_out(1, 3).wait()
+        panel_out(0, 4).wait()
+        for o in outs: o.wait()
+
+def whole(shape):
+    return pl.BlockSpec(shape, lambda j: (0,)*len(shape), pipeline_mode=pl.Buffered(1))
+
+def mlp_grads(s, st, cot, full):
+    return pl.pallas_call(
+        mlp_kernel, grid=(6,),
+        in_specs=[whole((512,2048)), whole((2048,512)), whole((512,2048)),
+                  pl.BlockSpec((16,128,PANEL), lambda j: (0, jnp.minimum(j,4), 0)),
+                  pl.BlockSpec(memory_space=pl.ANY)],
+        out_specs=[pl.BlockSpec((512,512), lambda j: (0,j)), pl.BlockSpec((512,256), lambda j:(0,j)), pl.BlockSpec(memory_space=pl.ANY)],
+        out_shape=[jax.ShapeDtypeStruct((512,3072),BF), jax.ShapeDtypeStruct((512,1536),BF), jax.ShapeDtypeStruct((16,1056,PANEL),BF)],
+        scratch_shapes=[pltpu.VMEM((4,FW,PANEL),BF), pltpu.VMEM((16,128,256),BF), pltpu.VMEM((2,16,128,PANEL),BF),
+                        pltpu.VMEM((16,128,256),BF), pltpu.VMEM((4,FW,PANEL),BF),
+                        pltpu.SemaphoreType.DMA((16,)), pltpu.SemaphoreType.DMA((2,)), pltpu.SemaphoreType.DMA((2,)), pltpu.SemaphoreType.DMA((16,))],
+        compiler_params=pltpu.CompilerParams(vmem_limit_bytes=58*2**20, dimension_semantics=("arbitrary",)),
+        cost_estimate=pl.CostEstimate(flops=18*10**9, bytes_accessed=45*10**6, transcendentals=10**6),
+        name="mlp_grads",
+    )(s, st, cot, full, full)
+
+def second_kernel(g_ref, panel_ref, full, out_ref, tail, tail_sem):
+    j = pl.program_id(0)
+    tails = tail_in(full, tail, tail_sem)
+    @pl.when(j == 0)
+    def _():
+        for t in tails: t.start()
+        out_ref[...] = right_product(g_ref[...], panel_ref[...].reshape(2048,PANEL))
+    @pl.when(jnp.logical_and(j > 0, j < 5))
+    def _():
+        out_ref[...] += right_product(g_ref[...], panel_ref[...].reshape(2048,PANEL))
+    @pl.when(j == 5)
+    def _():
+        for t in tails: t.wait()
+        out_ref[...] += right_product(g_ref[:, :256], tail[...].reshape(2048,256))
+
+def second_grad(ggu, full):
+    return pl.pallas_call(
+        second_kernel, grid=(6,),
+        in_specs=[pl.BlockSpec((512,512), lambda j:(0,j)), pl.BlockSpec((16,128,PANEL), lambda j: (0, jnp.minimum(j,4), 0)), pl.BlockSpec(memory_space=pl.ANY)],
+        out_specs=pl.BlockSpec((512,2048), lambda j:(0,0)),
+        out_shape=jax.ShapeDtypeStruct((512,2048),F32),
+        scratch_shapes=[pltpu.VMEM((16,128,256),BF), pltpu.SemaphoreType.DMA((2,))],
+        compiler_params=pltpu.CompilerParams(vmem_limit_bytes=40*2**20, dimension_semantics=("arbitrary",)),
+        cost_estimate=pl.CostEstimate(flops=6*10**9, bytes_accessed=20*10**6, transcendentals=0),
+        name="second_grad",
+    )(ggu, full, full)
+
+
 def rounded_gain(gain):
     return lax.optimization_barrier(gain.astype(BF)).astype(F32)
 
@@ -128,6 +242,22 @@
     half = HEAD_DIM // 2
     lane = lax.broadcasted_iota(jnp.int32, v.shape, v.ndim - 1) % HEAD_DIM
     return jnp.where(lane < half, -jnp.roll(v, -half, axis=-1), jnp.roll(v, half, axis=-1))
+
+
+def panels(gate, up):
+    blocks = []
+    for at in range(0, FW, 256):
+        blocks += [gate[:, at : at + 256], up[:, at : at + 256]]
+    return jnp.concatenate(blocks, axis=1)
+
+
+def unpanels(both):
+    gate, up = [], []
+    for at in range(0, FW, 256):
+        width = min(256, FW - at)
+        gate.append(both[:, 2 * at : 2 * at + width])
+        up.append(both[:, 2 * at + width : 2 * at + 2 * width])
+    return jnp.concatenate(gate, axis=1), jnp.concatenate(up, axis=1)
 
 
 def on_device(
@@ -161,29 +291,22 @@
     def mine(weight, width):
         return lax.dynamic_slice_in_dim(weight, member * width, width, 1).astype(BF)
 
-    out_block = turn(mine(output_weight, QW))
     attn_shard = jnp.concatenate(
-        [mine(query_weight, QW), mine(key_weight, KW), mine(value_weight, KW), out_block], axis=1
-    )
-    attn_full = plane_gather(pair_x(attn_shard, low))
+        [mine(query_weight, QW), mine(key_weight, KW), mine(value_weight, KW)], axis=1
+    )
+    attn_shard = jnp.concatenate(
+        [pair_x(attn_shard, low), turn_pair(mine(output_weight, QW), low)], axis=1
+    )
+    attn_full = plane_gather(attn_shard)
     qkv_full = attn_full[:, :QKVW]
     out_full = attn_full[:, QKVW:].reshape(4, QW, PANEL)
 
-    gu_shard = pair_x(
-        jnp.concatenate([mine(gate_weight, FW), mine(up_weight, FW)], axis=1), low
-    )
-    down_shard = pair_x(turn(mine(down_weight, PANEL)), low)
+    gu_shard = pair_x(panels(mine(gate_weight, FW), mine(up_weight, FW)), low)
     pieces = [gu_shard[:, j * PANEL : (j + 1) * PANEL] for j in range(5)]
     tail = gu_shard[:, 5 * PANEL :]
     pieces.append(jnp.concatenate([tail[:W_ROWS], tail[W_ROWS:]], axis=1))
-    pieces.append(down_shard)
+    pieces.append(turn_pair(mine(down_weight, PANEL), low))
     mlp_full = plane_gather(jnp.concatenate(pieces, axis=0)).reshape(16, 1056, PANEL)
-    gu_panels = [mlp_full[:, j * 128 : (j + 1) * 128].reshape(D, PANEL) for j in range(5)]
-    last = mlp_full[:, 640:704]
-    gu_panels.append(
-        jnp.stack([last[:, :, :256], last[:, :, 256:]], axis=1).reshape(D, 256)
-    )
-    down_full = mlp_full[:, 704:].reshape(4, FW, PANEL)
 
     places = jnp.stack([segment_ids, positions, padding])
     places = group_gather(places[None])
@@ -234,33 +357,14 @@
     second_low = (middle * inverse_rms(middle) * second_gain).astype(BF)
     second_all = group_gather(second_low)
 
-    gu = jnp.concatenate([dot(second_all, panel) for panel in gu_panels], axis=1)
-    gate, up = gu[:, :FW], gu[:, FW:]
-    sig = 1.0 / (1.0 + jnp.exp(-gate))
-    silu = gate * sig
-    active = (silu * up).astype(BF)
-    down_part = jnp.concatenate([dot(active, down_full[c]) for c in range(4)], axis=1)
+    grad_gu, active, send = mlp_grads(second_all, second_all.T, grads_in, mlp_full)
+    mlp_sum = plane_scatter(send.reshape(16 * 1056, PANEL))
+    grad_second = second_grad(grad_gu, mlp_full)
+
+    down_full = mlp_full[:, 704:].reshape(4, FW, PANEL)
+    down_part = jnp.concatenate([dot(active[:, :FW], down_full[c]) for c in range(4)], axis=1)
     block_output = (middle + group_scatter(down_part)).astype(BF)
 
-    grad_product = sum(
-        right_product(grads_in[:, c * PANEL : (c + 1) * PANEL], down_full[c]) for c in range(4)
-    )
-    grad_gate = (grad_product * up * sig * (1.0 + gate * (1.0 - sig))).astype(BF)
-    grad_up = (grad_product * silu).astype(BF)
-    grad_gu = jnp.concatenate([grad_gate, grad_up], axis=1)
-
-    cuts = [grad_gu[:, j * PANEL : (j + 1) * PANEL] for j in range(5)] + [grad_gu[:, 5 * PANEL :]]
-    sends = [left_product(second_all, cut).astype(BF) for cut in cuts]
-    send = [block.reshape(16, 128, PANEL) for block in sends[:5]]
-    tail = sends[5].reshape(16, 2, W_ROWS, 256)
-    send.append(jnp.concatenate([tail[:, 0], tail[:, 1]], axis=2))
-    grad_down = jnp.concatenate(
-        [left_product(active, grads_in[:, c * PANEL : (c + 1) * PANEL]) for c in range(4)], axis=0
-    ).astype(BF)
-    send.append(grad_down.reshape(16, 2 * DOWN_ROWS, PANEL))
-    mlp_sum = plane_scatter(jnp.concatenate(send, axis=1).reshape(16 * 1056, PANEL))
-
-    grad_second = sum(right_product(cut, panel) for cut, panel in zip(cuts, gu_panels))
     grad_second = group_scatter(grad_second)
     back, n_second = norm_back(middle, second_gain, grad_second)
     mlp_gain_part = jnp.sum(grad_second * n_second, axis=0)
@@ -320,6 +424,36 @@
     gains = gains + swap_far(gains)
     gains = gains + swap_core(gains)
 
+    qkv_part = attn_sum[:, :QKVW]
+    out_part = turn(attn_sum[:, QKVW:])
+    both = jnp.concatenate([qkv_part, out_part], axis=1)
+    kept = jnp.where(low, both[:W_ROWS], both[W_ROWS:])
+    given = jnp.where(low, both[W_ROWS:], both[:W_ROWS])
+    own_total = kept.astype(F32) + swap_x(given).astype(F32)
+    far_total = swap_far(kept).astype(F32) + lax.ppermute(
+        given, ("grp", "dp"), SWAP_FAR_X
+    ).astype(F32)
+    totals = jnp.concatenate([own_total, far_total], axis=0).astype(BF)
+    totals = jnp.concatenate([totals, swap_core(totals)], axis=0).astype(F32)
+    own_moment = jnp.concatenate(
+        [query_moment, key_moment, value_moment, output_moment], axis=1
+    )
+    moments = group_gather(own_moment.astype(BF)).astype(F32)
+    own_moved = 0.5 * own_moment + 0.5 * own_total
+    query_momentum = own_moved[:, :QW]
+    key_momentum = own_moved[:, QW : QW + KW]
+    value_momentum = own_moved[:, QW + KW : QKVW]
+    output_momentum = own_moved[:, QKVW:]
+
+    mine_at = (member // 2) + 2 * (member % 2)
+
+    def in_order(slots):
+        return [
+            lax.dynamic_index_in_dim(slots, mine_at ^ at, 0, keepdims=False) for at in (0, 2, 1, 3)
+        ]
+
+    attn_moved = in_order((0.5 * moments + 0.5 * totals).reshape(MEMBERS, W_ROWS, QKVW + PANEL))
+
     gu_rows = sum_x(
         jnp.concatenate(
             [mlp_sum[j * 128 : (j + 1) * 128] for j in range(5)]
@@ -329,40 +463,22 @@
         low,
     )
     down_rows = turn(sum_x(mlp_sum[704:], low).astype(BF)).astype(F32)
-    attn_rows = sum_x(attn_sum, low)
-    out_rows = turn(attn_rows[:, QKVW:].astype(BF)).astype(F32)
-
-    def step(moment, total):
-        return 0.5 * moment + 0.5 * total
-
-    gate_momentum = step(gate_moment, gu_rows[:, :FW])
-    up_momentum = step(up_moment, gu_rows[:, FW:])
-    down_momentum = step(down_moment, down_rows)
-    query_momentum = step(query_moment, attn_rows[:, :QW])
-    key_momentum = step(key_moment, attn_rows[:, QW : QW + KW])
-    value_momentum = step(value_moment, attn_rows[:, QW + KW : QKVW])
-    output_momentum = step(output_moment, out_rows)
-
-    mine_at = (member // 2) + 2 * (member % 2)
-
-    def spread(momentum):
-        rows, width = momentum.shape
-        slots = group_gather(momentum.astype(BF)).reshape(MEMBERS, rows, width)
-        return [
-            lax.dynamic_index_in_dim(slots, mine_at ^ at, 0, keepdims=False) for at in (0, 2, 1, 3)
-        ]
+    gate_rows, up_rows = unpanels(gu_rows)
+    gate_momentum = 0.5 * gate_moment + 0.5 * gate_rows
+    up_momentum = 0.5 * up_moment + 0.5 * up_rows
+    down_momentum = 0.5 * down_moment + 0.5 * down_rows
+    gu_moved = in_order(
+        group_gather(jnp.concatenate([gate_momentum, up_momentum], axis=1).astype(BF)).reshape(
+            MEMBERS, W_ROWS, GUW
+        )
+    )
+    down_moved = in_order(
+        group_gather(down_momentum.astype(BF)).reshape(MEMBERS, DOWN_ROWS, PANEL)
+    )
 
     def updated(weight, columns, start, width):
         moved = jnp.concatenate([block[:, start : start + width] for block in columns], axis=1)
         return weight - learn_rate * moved.astype(F32)
-
-    attn_moved = spread(
-        jnp.concatenate(
-            [query_momentum, key_momentum, value_momentum, output_momentum], axis=1
-        )
-    )
-    gu_moved = spread(jnp.concatenate([gate_momentum, up_momentum], axis=1))
-    down_moved = spread(down_momentum)
 
     gains = 0.5 * jnp.stack([attn_moment, mlp_moment]) + 0.5 * gains
     return (

time: 632 us -> 617 us (0.976)
  matrix products: 113 us -> 36 us
  waiting for transfers between devices: 227 us -> 287 us
  Pallas kernels: 0 us -> 41.9 us
  other arithmetic: 86.5 us -> 58 us
  local copies, waits for them, and re-layouts: 83.2 us -> 60.3 us
  starting transfers between devices: 101 us -> 113 us
    reduce_scatter x2, waiting for transfers between devices: 51.9 us -> 110 us  [plane_scatter(): lax.psum_scatter(v, 'dp', scatter_dimension=0, tiled=True, axis_index_gro...]
    pallas_call x0 -> x2, Pallas kernels: none -> 41.9 us  [the longest x1 32.3 us: mlp_grads(): pl.pallas_call(mlp_kernel, grid=(6,), in_specs=[whole((512, 2048)), whole...]
    dot_general x15 -> x5, matrix products: 45.2 us -> 10 us  [right_product(): lax.dot_general(left, right, (((1,), (1,)), ((), ())), preferred_element_...]
    dot_general x15 -> x5, matrix products: 30.5 us -> 6.89 us  [left_product(): lax.dot_general(left, right, (((0,), (0,)), ((), ())), preferred_element_...]
    unnamed x256 -> x201, local copies, waits for them, and re-layouts: 39.6 us -> 19.3 us
    concatenate x6 -> x5, other arithmetic: 21.3 us -> 1.24 us  [the longest x1 0.74 us: on_device(): jnp.concatenate([pair_x(attn_shard, low), turn_pair(mine(output_weight, Q...]
    dot_general x15 -> x9, matrix products: 34.1 us -> 15.7 us  [dot(): return jnp.dot(left, right, preferred_element_type=F32)]
    ppermute x7 -> x6, waiting for transfers between devices: 22 us -> 5.92 us  [swap_x(): return lax.ppermute(v, 'dp', SWAP_X)]
  transfers between devices with their start and end apart: 47 -> 51, of which waited for: 30 -> 33; matrix products, arithmetic and copies ran while one was open for 25% -> 12% of each run, Pallas kernels for 0% -> 0%
where the time goes in v2:
time: 617 us; the launch traced here: 612 us
  waiting for transfers between devices  287 us (47%)
  starting transfers between devices  113 us (18%)
  local copies, waits for them, and re-layouts  60.3 us (10%)
  other arithmetic  58 us (9%)
  Pallas kernels  41.9 us (7%)
  matrix products  36 us (6%)
  between operations  16.1 us (3%)
    reduce_scatter x2, waiting for transfers between devices, plane_scatter(): lax.psum_scatter(v, 'dp', scatter_dimension=0, tiled=True, axis_index_gro...  110 us
    ppermute x14, waiting for transfers between devices, swap_far(): return lax.ppermute(v, 'grp', SWAP_FAR)  92 us
    all_gather x2, waiting for transfers between devices, plane_gather(): return lax.all_gather(v, 'dp', axis=0, tiled=True, axis_index_groups=PLANES)  59.4 us
    ppermute x14, starting transfers between devices, swap_far(): return lax.ppermute(v, 'grp', SWAP_FAR)  46.8 us
    pallas_call x1, Pallas kernels, mlp_grads(): pl.pallas_call(mlp_kernel, grid=(6,), in_specs=[whole((512, 2048)), whole...  32.3 us
    ppermute x14, starting transfers between devices, swap_core(): return lax.ppermute(v, 'grp', SWAP_CORE)  26.4 us
    unnamed x201, local copies, waits for them, and re-layouts  19.3 us
    ppermute x4, starting transfers between devices, turn(): return lax.ppermute(v, ('grp', 'dp'), TURN)  19.2 us
  transfers between devices with their start and end apart: 51, of which 33 were waited for; matrix products, arithmetic and copies ran while one was open for 12% of the time, Pallas kernels for 0%

profile of v2, /device:TPU:1, one launch (start us, length us, event | category | flops | bytes accessed | tf_op | source)
XLA Modules:
  0.0 612.3 jit_solution(10050107797626428087)
XLA Ops:
  8.2 4.9 collective-permute-start.3
  22.9 5.0 collective-permute-start.14
  35.4 14.4 %collective-permute-start = (bf16[128,2048]{1,0:T(8,128)(2,1)S(1)}, bf16[128,2048]{1,0:T(8,128)(2,1)S(1)}, u32[]{:S(2)}, u32[]{:S(2)}) collective-permute-start(bf16[128,2048]{1,0:T(8,128)(2,1)S(1)} %copy-done.1), channel_id=1, source_target_pairs={{0,64},{32,96},{64,0},{96,32},{1,65},{33,97},{65,1},{97,33},{2,66}... | collective-permute-start | bytes 1572872 | tf_op jit(solution)/shard_map/ppermute | solution.py:64
  50.5 11.6 %collective-permute-done = bf16[128,2048]{1,0:T(8,128)(2,1)S(1)} collective-permute-done((bf16[128,2048]{1,0:T(8,128)(2,1)S(1)}, bf16[128,2048]{1,0:T(8,128)(2,1)S(1)}, u32[]{:S(2)}, u32[]{:S(2)}) %collective-permute-start) | collective-permute-done | bytes 524320 | tf_op jit(solution)/shard_map/ppermute | solution.py:64
  66.6 19.7 %all-gather.3.cloned.1.call-done = bf16[2048,1152]{1,0:T(8,128)(2,1)} async-done(((bf16[128,1152]{1,0:T(8,128)(2,1)}), bf16[2048,1152]{1,0:T(8,128)(2,1)}) %all-gather.3.cloned.1.call-update) | async-done | bytes 4718608 | tf_op jit(solution)/shard_map/all_gather | solution.py:78
  118.4 11.7 %collective-permute-done.8 = bf16[128,2048]{1,0:T(8,128)(2,1)S(1)} collective-permute-done((bf16[128,2048]{1,0:T(8,128)(2,1)S(1)}, bf16[128,2048]{1,0:T(8,128)(2,1)S(1)}, u32[]{:S(2)}, u32[]{:S(2)}) %collective-permute-start.8) | collective-permute-done | bytes 524320 | tf_op jit(solution)/shard_map/ppermute | solution.py:64
  133.8 7.5 %collective-permute-done.11 = bf16[128,2048]{1,0:T(8,128)(2,1)S(1)} collective-permute-done((bf16[128,2048]{1,0:T(8,128)(2,1)S(1)}, bf16[128,2048]{1,0:T(8,128)(2,1)S(1)}, u32[]{:S(2)}, u32[]{:S(2)}) %collective-permute-start.11) | collective-permute-done | bytes 524320 | tf_op jit(solution)/shard_map/ppermute | solution.py:64
  143.4 9.0 %collective-permute-done.9 = bf16[128,2048]{1,0:T(8,128)(2,1)S(1)} collective-permute-done((bf16[128,2048]{1,0:T(8,128)(2,1)S(1)}, bf16[128,2048]{1,0:T(8,128)(2,1)S(1)}, u32[]{:S(2)}, u32[]{:S(2)}) %collective-permute-start.9) | collective-permute-done | bytes 524320 | tf_op jit(solution)/shard_map/ppermute | solution.py:64
  163.1 39.7 %all-gather.5.cloned.1.call-done = bf16[16896,512]{1,0:T(8,128)(2,1)} async-done(((bf16[1056,512]{1,0:T(8,128)(2,1)}), bf16[16896,512]{1,0:T(8,128)(2,1)}) %all-gather.5.cloned.1.call-update) | async-done | bytes 17301520 | tf_op jit(solution)/shard_map/all_gather | solution.py:78
  207.6 32.3 %mlp_grads.1 = (bf16[512,3072]{1,0:T(8,128)(2,1)}, bf16[512,1536]{1,0:T(8,128)(2,1)}, bf16[16,1056,512]{2,1,0:T(8,128)(2,1)}) custom-call(bf16[512,2048]{1,0:T(8,128)(2,1)} %get-tuple-element.85.s_ref, bf16[2048,512]{1,0:T(8,128)(2,1)} %copy.148.st_ref, bf16[512,2048]{1,0:T(8,128)(2,1)} %pad_maximum_fusion.4.c_ref, bf16[16,1056,512]{2,1,0:T(8,128)(2,1)} %bitcast.132, ...), custom_call_target="tpu_custom_call" | custom-call | flops 17999998976 | bytes 45000000 | tf_op jit(solution)/shard_map/mlp_grads/pallas_call | solution.py:183
  246.1 9.6 %second_grad.1 = f32[512,2048]{1,0:T(8,128)S(1)} custom-call(bf16[512,3072]{1,0:T(8,128)(2,1)S(1)} %copy-done, bf16[16,1056,512]{2,1,0:T(8,128)(2,1)} %bitcast.134, bf16[16,1056,512]{2,1,0:T(8,128)(2,1)} %bitcast.135), custom_call_target="tpu_custom_call" | custom-call | flops 6000000000 | bytes 20000000 | tf_op jit(solution)/shard_map/second_grad/pallas_call | solution.py:214
  264.3 9.7 %collective-permute-done.19 = bf16[128,2048]{1,0:T(8,128)(2,1)S(1)} collective-permute-done((bf16[128,2048]{1,0:T(8,128)(2,1)S(1)}, bf16[128,2048]{1,0:T(8,128)(2,1)S(1)}, u32[]{:S(2)}, u32[]{:S(2)}) %collective-permute-start.19) | collective-permute-done | bytes 524320 | tf_op jit(solution)/shard_map/ppermute | solution.py:64
  275.0 10.3 %collective-permute-done.17 = bf16[128,2048]{1,0:T(8,128)(2,1)S(1)} collective-permute-done((bf16[128,2048]{1,0:T(8,128)(2,1)S(1)}, bf16[128,2048]{1,0:T(8,128)(2,1)S(1)}, u32[]{:S(2)}, u32[]{:S(2)}) %collective-permute-start.17) | collective-permute-done | bytes 524320 | tf_op jit(solution)/shard_map/ppermute | solution.py:64
  289.7 11.0 %collective-permute-done.20 = bf16[128,2048]{1,0:T(8,128)(2,1)S(1)} collective-permute-done((bf16[128,2048]{1,0:T(8,128)(2,1)S(1)}, bf16[128,2048]{1,0:T(8,128)(2,1)S(1)}, u32[]{:S(2)}, u32[]{:S(2)}) %collective-permute-start.20) | collective-permute-done | bytes 524320 | tf_op jit(solution)/shard_map/ppermute | solution.py:64
  338.4 18.4 %maximum_maximum_fusion = bf16[2048,1152]{0,1:T(8,128)(2,1)} fusion(bf16[512,512]{0,1:T(8,128)(2,1)S(1)} %copy-done.36, bf16[512,512]{0,1:T(8,128)(2,1)S(1)} %copy-done.37, bf16[512,512]{0,1:T(8,128)(2,1)S(1)} %copy-done.38, bf16[512,512]{0,1:T(8,128)(2,1)S(1)} %copy-done.39, bf16[2048,640]{0,1:T(8,128)(2,1)S(1)} %convolution_convert_fusion), kind=kLoop, calls=%fused_computation.4 | loop fusion | flops 23592960 | bytes 9437184 | tf_op jit(solution)/shard_map/concatenate | solution.py:411
  356.8 6.7 %copy.208 = bf16[2048,1152]{1,0:T(8,128)(2,1)} copy(bf16[2048,1152]{0,1:T(8,128)(2,1)} %maximum_maximum_fusion) | data formatting | bytes 9437184
  400.7 10.7 %collective-permute-done.23 = bf16[128,2048]{1,0:T(8,128)(2,1)S(1)} collective-permute-done((bf16[128,2048]{1,0:T(8,128)(2,1)S(1)}, bf16[128,2048]{1,0:T(8,128)(2,1)S(1)}, u32[]{:S(2)}, u32[]{:S(2)}) %collective-permute-start.23) | collective-permute-done | bytes 524320 | tf_op jit(solution)/shard_map/ppermute | solution.py:64
  411.8 28.2 %reduce-scatter.7.cloned.1.call-done = bf16[128,1152]{1,0:T(8,128)(2,1)} async-done(((bf16[2048,1152]{1,0:T(8,128)(2,1)}), bf16[128,1152]{1,0:T(8,128)(2,1)}) %reduce-scatter.7.cloned.1.call-update) | async-done | bytes 294928 | tf_op jit(solution)/shard_map/reduce_scatter | solution.py:82
  440.9 5.0 collective-permute-start.33
  452.8 5.7 collective-permute-start.41
  464.3 6.1 collective-permute-start.42
  475.1 82.1 %reduce-scatter.5.cloned.1.call-done = bf16[1056,512]{1,0:T(8,128)(2,1)} async-done(((bf16[16896,512]{1,0:T(8,128)(2,1)}), bf16[1056,512]{1,0:T(8,128)(2,1)}) %reduce-scatter.5.cloned.1.call-update) | async-done | bytes 1081360 | tf_op jit(solution)/shard_map/reduce_scatter | solution.py:82
  574.8 10.2 %collective-permute-start.45 = (bf16[176,512]{1,0:T(8,128)(2,1)S(1)}, bf16[176,512]{1,0:T(8,128)(2,1)S(1)}, u32[]{:S(2)}, u32[]{:S(2)}) collective-permute-start(bf16[176,512]{1,0:T(8,128)(2,1)S(1)} %get-tuple-element.68), channel_id=1, source_target_pairs={{0,64},{32,96},{64,0},{96,32},{1,65},{33,97},{65,1},{97,33},{2,66}... | collective-permute-start | bytes 540680 | tf_op jit(solution)/shard_map/ppermute | solution.py:64
  591.9 5.3 collective-permute-done.43
  (470 shorter events, 221.3 us)
Async XLA Ops:
  7.2 79.2 %all-gather.3.cloned.1.call-start = ((), (), s32[]{:S(2)}) async-start(), calls=%async_computation.2 | async-start | bytes 5013504 | tf_op jit(solution)/shard_map/all_gather | solution.py:78
  20.2 182.6 %all-gather.5.cloned.1.call-start = ((), (), s32[]{:S(2)}) async-start(), calls=%async_computation.3 | async-start | bytes 18382848 | tf_op jit(solution)/shard_map/all_gather | solution.py:78
  21.5 10.5 %collective-permute-start.13 = (bf16[64,2816]{1,0:T(8,128)(2,1)S(1)}, bf16[64,2816]{1,0:T(8,128)(2,1)S(1)}, u32[]{:S(2)}, u32[]{:S(2)}) collective-permute-start(bf16[64,2816]{1,0:T(8,128)(2,1)S(1)} %constant_dynamic-update-slice_fusion), channel_id=1, source_target_pairs={{0,1},{1,0},{2,3},{3,2},{4,5},{5,4},{6,7},{7,6},{8,9},{9,8},{10,11... | collective-permute-start | bytes 1081352 | tf_op jit(solution)/shard_map/ppermute | solution.py:56
  22.9 9.3 %collective-permute-start.14 = (bf16[176,512]{1,0:T(8,128)(2,1)S(1)}, bf16[176,512]{1,0:T(8,128)(2,1)S(1)}, u32[]{:S(2)}, u32[]{:S(2)}) collective-permute-start(bf16[176,512]{1,0:T(8,128)(2,1)S(1)} %dynamic-slice_convert_fusion), channel_id=1, source_target_pairs={{0,0},{1,1},{2,2},{3,3},{4,4},{5,5},{6,6},{7,7},{8,32},{9,33},{10,... | collective-permute-start | bytes 540680 | tf_op jit(solution)/shard_map/ppermute | solution.py:68
  35.4 404.7 %reduce-scatter.7.cloned.1.call-start = ((), (), s32[]{:S(2)}) async-start(), calls=%async_computation.5 | async-start | bytes 5013504 | tf_op jit(solution)/shard_map/reduce_scatter | solution.py:82
  35.4 26.7 %collective-permute-start = (bf16[128,2048]{1,0:T(8,128)(2,1)S(1)}, bf16[128,2048]{1,0:T(8,128)(2,1)S(1)}, u32[]{:S(2)}, u32[]{:S(2)}) collective-permute-start(bf16[128,2048]{1,0:T(8,128)(2,1)S(1)} %copy-done.1), channel_id=1, source_target_pairs={{0,64},{32,96},{64,0},{96,32},{1,65},{33,97},{65,1},{97,33},{2,66}... | collective-permute-start | bytes 1572872 | tf_op jit(solution)/shard_map/ppermute | solution.py:64
  49.8 13.7 %collective-permute-start.5 = (s32[1,3,128]{2,1,0:T(4,128)S(1)}, s32[1,3,128]{2,1,0:T(4,128)S(1)}, u32[]{:S(2)}, u32[]{:S(2)}) collective-permute-start(s32[1,3,128]{2,1,0:T(4,128)S(1)} %add_bitcast_fusion), channel_id=1, source_target_pairs={{0,64},{32,96},{64,0},{96,32},{1,65},{33,97},{65,1},{97,33},{2,66}... | collective-permute-start | bytes 4616 | tf_op jit(solution)/shard_map/ppermute | solution.py:64
  115.3 14.7 %collective-permute-start.8 = (bf16[128,2048]{1,0:T(8,128)(2,1)S(1)}, bf16[128,2048]{1,0:T(8,128)(2,1)S(1)}, u32[]{:S(2)}, u32[]{:S(2)}) collective-permute-start(bf16[128,2048]{1,0:T(8,128)(2,1)S(1)} %slice.828), channel_id=1, source_target_pairs={{0,64},{32,96},{64,0},{96,32},{1,65},{33,97},{65,1},{97,33},{2,66}... | collective-permute-start | bytes 1572872 | tf_op jit(solution)/shard_map/ppermute | solution.py:64
  118.0 23.2 %collective-permute-start.11 = (bf16[128,2048]{1,0:T(8,128)(2,1)S(1)}, bf16[128,2048]{1,0:T(8,128)(2,1)S(1)}, u32[]{:S(2)}, u32[]{:S(2)}) collective-permute-start(bf16[128,2048]{1,0:T(8,128)(2,1)S(1)} %copy-done.15), channel_id=1, source_target_pairs={{0,64},{32,96},{64,0},{96,32},{1,65},{33,97},{65,1},{97,33},{2,66}... | collective-permute-start | bytes 1572872 | tf_op jit(solution)/shard_map/ppermute | solution.py:64
  131.0 21.4 %collective-permute-start.9 = (bf16[128,2048]{1,0:T(8,128)(2,1)S(1)}, bf16[128,2048]{1,0:T(8,128)(2,1)S(1)}, u32[]{:S(2)}, u32[]{:S(2)}) collective-permute-start(bf16[128,2048]{1,0:T(8,128)(2,1)S(1)} %multiply_convert_fusion), channel_id=1, source_target_pairs={{0,64},{32,96},{64,0},{96,32},{1,65},{33,97},{65,1},{97,33},{2,66}... | collective-permute-start | bytes 1572872 | tf_op jit(solution)/shard_map/ppermute | solution.py:64
  141.4 12.9 %collective-permute-start.12 = (bf16[256,2048]{1,0:T(8,128)(2,1)S(1)}, bf16[256,2048]{1,0:T(8,128)(2,1)S(1)}, u32[]{:S(2)}, u32[]{:S(2)}) collective-permute-start(bf16[256,2048]{1,0:T(8,128)(2,1)S(1)} %pad_maximum_fusion.9), channel_id=1, source_target_pairs={{0,32},{32,0},{64,96},{96,64},{1,33},{33,1},{65,97},{97,65},{2,34}... | collective-permute-start | bytes 3145736 | tf_op jit(solution)/shard_map/ppermute | solution.py:60
  259.3 14.7 %collective-permute-start.19 = (bf16[128,2048]{1,0:T(8,128)(2,1)S(1)}, bf16[128,2048]{1,0:T(8,128)(2,1)S(1)}, u32[]{:S(2)}, u32[]{:S(2)}) collective-permute-start(bf16[128,2048]{1,0:T(8,128)(2,1)S(1)} %slice.826), channel_id=1, source_target_pairs={{0,64},{32,96},{64,0},{96,32},{1,65},{33,97},{65,1},{97,33},{2,66}... | collective-permute-start | bytes 1572872 | tf_op jit(solution)/shard_map/ppermute | solution.py:64
  262.5 22.7 %collective-permute-start.17 = (bf16[128,2048]{1,0:T(8,128)(2,1)S(1)}, bf16[128,2048]{1,0:T(8,128)(2,1)S(1)}, u32[]{:S(2)}, u32[]{:S(2)}) collective-permute-start(bf16[128,2048]{1,0:T(8,128)(2,1)S(1)} %slice.827), channel_id=1, source_target_pairs={{0,64},{32,96},{64,0},{96,32},{1,65},{33,97},{65,1},{97,33},{2,66}... | collective-permute-start | bytes 1572872 | tf_op jit(solution)/shard_map/ppermute | solution.py:64
  287.0 13.7 %collective-permute-start.20 = (bf16[128,2048]{1,0:T(8,128)(2,1)S(1)}, bf16[128,2048]{1,0:T(8,128)(2,1)S(1)}, u32[]{:S(2)}, u32[]{:S(2)}) collective-permute-start(bf16[128,2048]{1,0:T(8,128)(2,1)S(1)} %get-tuple-element.76), channel_id=1, source_target_pairs={{0,64},{32,96},{64,0},{96,32},{1,65},{33,97},{65,1},{97,33},{2,66}... | collective-permute-start | bytes 1572872 | tf_op jit(solution)/shard_map/ppermute | solution.py:64
  363.5 193.7 %reduce-scatter.5.cloned.1.call-start = ((), (), s32[]{:S(2)}) async-start(), calls=%async_computation.4 | async-start | bytes 18382848 | tf_op jit(solution)/shard_map/reduce_scatter | solution.py:82
  378.8 15.3 %collective-permute-start.22 = (bf16[256,2048]{1,0:T(8,128)(2,1)S(1)}, bf16[256,2048]{1,0:T(8,128)(2,1)}, u32[]{:S(2)}, u32[]{:S(2)}) collective-permute-start(bf16[256,2048]{1,0:T(8,128)(2,1)S(1)} %slice.821), channel_id=1, source_target_pairs={{0,32},{32,0},{64,96},{96,64},{1,33},{33,1},{65,97},{97,65},{2,34}... | collective-permute-start | bytes 3145736 | tf_op jit(solution)/shard_map/ppermute | solution.py:60
  396.4 15.1 %collective-permute-start.23 = (bf16[128,2048]{1,0:T(8,128)(2,1)S(1)}, bf16[128,2048]{1,0:T(8,128)(2,1)S(1)}, u32[]{:S(2)}, u32[]{:S(2)}) collective-permute-start(bf16[128,2048]{1,0:T(8,128)(2,1)S(1)} %slice.825), channel_id=1, source_target_pairs={{0,64},{32,96},{64,0},{96,32},{1,65},{33,97},{65,1},{97,33},{2,66}... | collective-permute-start | bytes 1572872 | tf_op jit(solution)/shard_map/ppermute | solution.py:64
  448.9 9.6 %collective-permute-start.34 = (bf16[64,1152]{1,0:T(8,128)(2,1)S(1)}, bf16[64,1152]{1,0:T(8,128)(2,1)S(1)}, u32[]{:S(2)}, u32[]{:S(2)}) collective-permute-start(bf16[64,1152]{1,0:T(8,128)(2,1)S(1)} %broadcast_select_fusion.4), channel_id=1, source_target_pairs={{0,1},{1,0},{2,3},{3,2},{4,5},{5,4},{6,7},{7,6},{8,9},{9,8},{10,11... | collective-permute-start | bytes 442376 | tf_op jit(solution)/shard_map/ppermute | solution.py:56
  452.8 9.0 %collective-permute-start.41 = (bf16[64,1152]{1,0:T(8,128)(2,1)S(1)}, bf16[64,1152]{1,0:T(8,128)(2,1)S(1)}, u32[]{:S(2)}, u32[]{:S(2)}) collective-permute-start(bf16[64,1152]{1,0:T(8,128)(2,1)S(1)} %broadcast_select_fusion.4), channel_id=1, source_target_pairs={{0,65},{1,64},{2,67},{3,66},{4,69},{5,68},{6,71},{7,70},{8,73},{9,... | collective-permute-start | bytes 442376 | tf_op jit(solution)/shard_map/ppermute | solution.py:433
  459.9 10.5 %collective-permute-start.38 = (bf16[64,1152]{1,0:T(8,128)(2,1)S(1)}, bf16[64,1152]{1,0:T(8,128)(2,1)S(1)}, u32[]{:S(2)}, u32[]{:S(2)}) collective-permute-start(bf16[64,1152]{1,0:T(8,128)(2,1)S(1)} %get-tuple-element.150), channel_id=1, source_target_pairs={{0,64},{32,96},{64,0},{96,32},{1,65},{33,97},{65,1},{97,33},{2,66}... | collective-permute-start | bytes 442376 | tf_op jit(solution)/shard_map/ppermute | solution.py:64
  564.8 20.2 %collective-permute-start.35 = (bf16[64,2816]{1,0:T(8,128)(2,1)S(1)}, bf16[64,2816]{1,0:T(8,128)(2,1)S(1)}, u32[]{:S(2)}, u32[]{:S(2)}) collective-permute-start(bf16[64,2816]{1,0:T(8,128)(2,1)S(1)} %broadcast_select_fusion), channel_id=1, source_target_pairs={{0,1},{1,0},{2,3},{3,2},{4,5},{5,4},{6,7},{7,6},{8,9},{9,8},{10,11... | collective-permute-start | bytes 1081352 | tf_op jit(solution)/shard_map/ppermute | solution.py:56
  574.8 14.2 %collective-permute-start.45 = (bf16[176,512]{1,0:T(8,128)(2,1)S(1)}, bf16[176,512]{1,0:T(8,128)(2,1)S(1)}, u32[]{:S(2)}, u32[]{:S(2)}) collective-permute-start(bf16[176,512]{1,0:T(8,128)(2,1)S(1)} %get-tuple-element.68), channel_id=1, source_target_pairs={{0,64},{32,96},{64,0},{96,32},{1,65},{33,97},{65,1},{97,33},{2,66}... | collective-permute-start | bytes 540680 | tf_op jit(solution)/shard_map/ppermute | solution.py:64
  586.9 10.4 %collective-permute-start.43 = (bf16[64,2816]{1,0:T(8,128)(2,1)S(1)}, bf16[64,2816]{1,0:T(8,128)(2,1)S(1)}, u32[]{:S(2)}, u32[]{:S(2)}) collective-permute-start(bf16[64,2816]{1,0:T(8,128)(2,1)S(1)} %pad_maximum_fusion.14), channel_id=1, source_target_pairs={{0,64},{32,96},{64,0},{96,32},{1,65},{33,97},{65,1},{97,33},{2,66}... | collective-permute-start | bytes 1081352 | tf_op jit(solution)/shard_map/ppermute | solution.py:64
  589.1 10.3 %collective-permute-start.46 = (bf16[352,512]{1,0:T(8,128)(2,1)S(1)}, bf16[352,512]{1,0:T(8,128)(2,1)S(1)}, u32[]{:S(2)}, u32[]{:S(2)}) collective-permute-start(bf16[352,512]{1,0:T(8,128)(2,1)S(1)} %pad_maximum_fusion.15), channel_id=1, source_target_pairs={{0,32},{32,0},{64,96},{96,64},{1,33},{33,1},{65,97},{97,65},{2,34}... | collective-permute-start | bytes 1081352 | tf_op jit(solution)/shard_map/ppermute | solution.py:60
  (116 other events, 1045.5 us)
Sparse Core Ops, SparseCore 0:
  20.3 66.0 all-gather.2
  89.1 113.6 all-gather.4
  363.6 76.3 reduce-scatter.6
  443.3 113.8 reduce-scatter.4

commit v3 on v2

--- a/solution.py
+++ b/solution.py
@@ -18,7 +18,6 @@
 GUW = 2 * FW
 PANEL = 512
 DOWN_ROWS = 176
-OUT_ROWS = 64
 W_ROWS = 64
 
 epsilon = 1e-05
@@ -28,20 +27,22 @@
 BF = jnp.bfloat16
 F32 = jnp.float32
 
-
-def dp_index(z, y, x):
-    return z * 8 + y * 2 + x
-
-
-PLANES = [[dp_index(z, y, x) for z in range(4) for y in range(4)] for x in range(2)]
+PLANES = [[z * 8 + y * 2 + x for z in range(4) for y in range(4)] for x in range(2)]
 SWAP_X = [(i, i ^ 1) for i in range(32)]
 SWAP_CORE = [(m, m ^ 1) for m in range(4)]
 SWAP_FAR = [(m, m ^ 2) for m in range(4)]
-TURN = [
-    (m * 32 + z * 8 + q, z * 32 + m * 8 + q) for m in range(4) for z in range(4) for q in range(8)
-]
-TURN_X = [(a, b ^ 1) for a, b in TURN]
 SWAP_FAR_X = [(m * 32 + i, (m ^ 2) * 32 + (i ^ 1)) for m in range(4) for i in range(32)]
+MZQ = [(m, z, q) for m in range(4) for z in range(4) for q in range(8)]
+
+
+def spot(m, z, q):
+    return m * 32 + z * 8 + q
+
+
+TURN = [(spot(m, z, q), spot(z, m, q)) for m, z, q in MZQ]
+TURN_X = [(spot(m, z, q), spot(z, m, q ^ 1)) for m, z, q in MZQ]
+TURN_OUT = [[(spot(m, z, q), spot(z, (m + k) % 4, q)) for m, z, q in MZQ] for k in range(4)]
+TURN_IN = [[(spot(m, z, q), spot((z + k) % 4, m, q)) for m, z, q in MZQ] for k in range(4)]
 
 
 def ring(place, k):
@@ -64,14 +65,8 @@
     return lax.ppermute(v, "grp", SWAP_FAR)
 
 
-def turn(v):
-    return lax.ppermute(v, ("grp", "dp"), TURN)
-
-
-def turn_pair(v, low):
-    own = turn(v)
-    other = lax.ppermute(v, ("grp", "dp"), TURN_X)
-    return jnp.concatenate([jnp.where(low, own, other), jnp.where(low, other, own)], axis=0)
+def everywhere(v, pairs):
+    return lax.ppermute(v, ("grp", "dp"), pairs)
 
 
 def plane_gather(v):
@@ -82,6 +77,27 @@
     return lax.psum_scatter(
         v, "dp", scatter_dimension=0, tiled=True, axis_index_groups=PLANES
     )
+
+
+def ring_gather(v, pairs, at):
+    rows = v.shape[0]
+    out = jnp.zeros((4 * rows,) + v.shape[1:], v.dtype)
+    for k, part in enumerate([v] + [lax.ppermute(v, "dp", p) for p in pairs]):
+        out = lax.dynamic_update_slice_in_dim(out, part, lax.rem(at + 4 - k, 4) * rows, 0)
+    return out
+
+
+def ring_scatter(v, pairs, at, extra=None):
+    rows = v.shape[0] // 4
+
+    def chunk(k):
+        part = lax.dynamic_slice_in_dim(v, lax.rem(at + k, 4) * rows, rows, 0)
+        return part if extra is None else jnp.concatenate([part, extra], axis=1)
+
+    total = chunk(0).astype(F32)
+    for k, p in enumerate(pairs):
+        total = total + lax.ppermute(chunk(k + 1), "dp", p).astype(F32)
+    return total
 
 
 def group_gather(v):
@@ -95,16 +111,31 @@
     return near[:ROWS] + swap_far(near[ROWS:].astype(BF)).astype(F32)
 
 
+def in_order(own, other, low):
+    return jnp.concatenate([jnp.where(low, own, other), jnp.where(low, other, own)], axis=0)
+
+
 def pair_x(v, low):
-    other = swap_x(v)
-    return jnp.concatenate([jnp.where(low, v, other), jnp.where(low, other, v)], axis=0)
-
-
-def sum_x(v, low):
+    return in_order(v, swap_x(v), low)
+
+
+def turn_pair(v, low):
+    return in_order(everywhere(v, TURN), everywhere(v, TURN_X), low)
+
+
+def halves(v, low):
     rows = v.shape[0] // 2
-    mine = jnp.where(low, v[:rows], v[rows:])
-    theirs = jnp.where(low, v[rows:], v[:rows])
-    return mine.astype(F32) + swap_x(theirs).astype(F32)
+    return jnp.where(low, v[:rows], v[rows:]), jnp.where(low, v[rows:], v[:rows])
+
+
+def two_parts(v):
+    high = lax.reduce_precision(v, 8, 7)
+    return jnp.concatenate([high.astype(BF), (v - high).astype(BF)], axis=0)
+
+
+def one_part(v):
+    rows = v.shape[0] // 2
+    return v[:rows].astype(F32) + v[rows:].astype(F32)
 
 
 def dot(left, right):
@@ -223,6 +254,150 @@
     )(ggu, full, full)
 
 
+def down_kernel(act_ref, down_ref, out_ref):
+    out_ref[...] = dot(act_ref[...], down_ref[...].reshape(FW, PANEL))
+
+
+def down_product(active, full):
+    return pl.pallas_call(
+        down_kernel,
+        grid=(4,),
+        in_specs=[whole((SLOTS, FW)), pl.BlockSpec((4, 352, PANEL), lambda c: (c, 2, 0))],
+        out_specs=pl.BlockSpec((SLOTS, PANEL), lambda c: (0, c)),
+        out_shape=jax.ShapeDtypeStruct((SLOTS, D), F32),
+        compiler_params=pltpu.CompilerParams(vmem_limit_bytes=32 * 2**20),
+        cost_estimate=pl.CostEstimate(
+            flops=3 * 10**9, bytes_accessed=12 * 10**6, transcendentals=0
+        ),
+        name="down_product",
+    )(active, full)
+
+
+LANES = 128
+
+
+def lanes_of(v):
+    return lax.broadcasted_iota(jnp.int32, v.shape, v.ndim - 1)
+
+
+def quarter_turn(v):
+    first = lanes_of(v) % HEAD_DIM < HEAD_DIM // 2
+    return jnp.where(first, -pltpu.roll(v, 96, 1), pltpu.roll(v, 32, 1))
+
+
+def doubled(v):
+    left = lanes_of(v) < HEAD_DIM
+    other = pltpu.roll(v, HEAD_DIM, 1)
+    return jnp.where(left, v, other), jnp.where(left, other, v)
+
+
+def head_rows(ref):
+    blocks = []
+    for g in range(GROUPS // 2):
+        v = ref[:, g * LANES : (g + 1) * LANES].astype(F32)
+        left = lanes_of(v) < HEAD_DIM
+        blocks += [jnp.where(left, v, 0.0), jnp.where(left, 0.0, v)]
+    return jnp.concatenate(blocks, axis=0).astype(BF)
+
+
+def pair_columns(v, g):
+    even = v[2 * g * ROWS : (2 * g + 1) * ROWS]
+    odd = v[(2 * g + 1) * ROWS : (2 * g + 2) * ROWS]
+    return jnp.where(lanes_of(even) < HEAD_DIM, even, odd)
+
+
+def softmax_rows(heads, key2, mask):
+    scores = right_product(heads, key2).reshape(GROUPS, ROWS, ROWS) * score_scale
+    masked = jnp.where(mask[None] > 0.0, scores, -1e30)
+    top = jnp.max(masked, axis=-1, keepdims=True)
+    total = top + jnp.log(jnp.sum(jnp.exp(masked - top), axis=-1, keepdims=True))
+    return jnp.exp(masked - total).reshape(GROUPS * ROWS, ROWS)
+
+
+def attention_kernel(qkv_ref, cos_ref, sin_ref, mask_ref, query_ref, kv_ref, out_ref):
+    cosine, sine = cos_ref[...], sin_ref[...]
+    for g in range(GROUPS // 2):
+        v = qkv_ref[:, g * LANES : (g + 1) * LANES]
+        query_ref[:, g * LANES : (g + 1) * LANES] = (v * cosine + quarter_turn(v) * sine).astype(BF)
+    v = qkv_ref[:, QW:]
+    kv = jnp.where(lanes_of(v) < HEAD_DIM, v * cosine + quarter_turn(v) * sine, v)
+    kv_ref[...] = kv.astype(BF)
+    key2, value2 = doubled(kv)
+    probs = softmax_rows(head_rows(query_ref), key2.astype(BF), mask_ref[0])
+    heads = dot(probs.astype(BF), value2.astype(BF))
+    for g in range(GROUPS // 2):
+        out_ref[:, g * LANES : (g + 1) * LANES] = pair_columns(heads, g).astype(BF)
+
+
+def attention_back_kernel(query_ref, kv_ref, grad_ref, cos_ref, sin_ref, mask_ref, out_ref):
+    cosine, sine = cos_ref[...], sin_ref[...]
+    key2, value2 = doubled(kv_ref[...].astype(F32))
+    key2, value2 = key2.astype(BF), value2.astype(BF)
+    heads, grads = head_rows(query_ref), head_rows(grad_ref)
+    probs = softmax_rows(heads, key2, mask_ref[0])
+    grad_value = left_product(probs.astype(BF), grads)
+    grad_value = grad_value + pltpu.roll(grad_value, HEAD_DIM, 1)
+    grad_probs = right_product(grads, value2)
+    inner = jnp.sum(grad_probs * probs, axis=-1, keepdims=True)
+    grad_scores = (probs * (grad_probs - inner)).astype(BF)
+    grad_query = dot(grad_scores, key2)
+    for g in range(GROUPS // 2):
+        v = pair_columns(grad_query, g) * score_scale
+        out_ref[:, g * LANES : (g + 1) * LANES] = (v * cosine - quarter_turn(v) * sine).astype(BF)
+    grad_key = left_product(grad_scores, heads)
+    v = (grad_key + pltpu.roll(grad_key, HEAD_DIM, 1)) * score_scale
+    grad_key = v * cosine - quarter_turn(v) * sine
+    out_ref[:, QW:] = jnp.where(lanes_of(v) < HEAD_DIM, grad_key, grad_value).astype(BF)
+
+
+def row_block(width):
+    return pl.BlockSpec((ROWS, width), lambda b: (b, 0))
+
+
+MASK_BLOCK = pl.BlockSpec((1, ROWS, ROWS), lambda b: (b, 0, 0))
+
+
+def attention(qkv, cosine, sine, mask):
+    return pl.pallas_call(
+        attention_kernel,
+        grid=(MEMBERS,),
+        in_specs=[row_block(QKVW), row_block(LANES), row_block(LANES), MASK_BLOCK],
+        out_specs=[row_block(QW), row_block(LANES), row_block(QW)],
+        out_shape=[
+            jax.ShapeDtypeStruct((SLOTS, QW), BF),
+            jax.ShapeDtypeStruct((SLOTS, LANES), BF),
+            jax.ShapeDtypeStruct((SLOTS, QW), BF),
+        ],
+        compiler_params=pltpu.CompilerParams(vmem_limit_bytes=32 * 2**20),
+        cost_estimate=pl.CostEstimate(
+            flops=3 * 10**8, bytes_accessed=4 * 10**6, transcendentals=10**6
+        ),
+        name="attention",
+    )(qkv, cosine, sine, mask)
+
+
+def attention_back(query, kv, grad, cosine, sine, mask):
+    return pl.pallas_call(
+        attention_back_kernel,
+        grid=(MEMBERS,),
+        in_specs=[
+            row_block(QW),
+            row_block(LANES),
+            row_block(QW),
+            row_block(LANES),
+            row_block(LANES),
+            MASK_BLOCK,
+        ],
+        out_specs=row_block(QKVW),
+        out_shape=jax.ShapeDtypeStruct((SLOTS, QKVW), BF),
+        compiler_params=pltpu.CompilerParams(vmem_limit_bytes=32 * 2**20),
+        cost_estimate=pl.CostEstimate(
+            flops=8 * 10**8, bytes_accessed=4 * 10**6, transcendentals=10**6
+        ),
+        name="attention_back",
+    )(query, kv, grad, cosine, sine, mask)
+
+
 def rounded_gain(gain):
     return lax.optimization_barrier(gain.astype(BF)).astype(F32)
 
@@ -236,12 +411,6 @@
     n = v * r
     scaled = grad * gain
     return r * (scaled - n * jnp.mean(scaled * n, axis=-1, keepdims=True)), n
-
-
-def turned(v):
-    half = HEAD_DIM // 2
-    lane = lax.broadcasted_iota(jnp.int32, v.shape, v.ndim - 1) % HEAD_DIM
-    return jnp.where(lane < half, -jnp.roll(v, -half, axis=-1), jnp.roll(v, half, axis=-1))
 
 
 def panels(gate, up):
@@ -286,20 +455,11 @@
     down_moment,
 ):
     member = lax.axis_index("grp")
-    low = (lax.axis_index("dp") % 2) == 0
+    place = lax.axis_index("dp")
+    z, y, low = place // 8, (place // 2) % 4, (place % 2) == 0
 
     def mine(weight, width):
         return lax.dynamic_slice_in_dim(weight, member * width, width, 1).astype(BF)
-
-    attn_shard = jnp.concatenate(
-        [mine(query_weight, QW), mine(key_weight, KW), mine(value_weight, KW)], axis=1
-    )
-    attn_shard = jnp.concatenate(
-        [pair_x(attn_shard, low), turn_pair(mine(output_weight, QW), low)], axis=1
-    )
-    attn_full = plane_gather(attn_shard)
-    qkv_full = attn_full[:, :QKVW]
-    out_full = attn_full[:, QKVW:].reshape(4, QW, PANEL)
 
     gu_shard = pair_x(panels(mine(gate_weight, FW), mine(up_weight, FW)), low)
     pieces = [gu_shard[:, j * PANEL : (j + 1) * PANEL] for j in range(5)]
@@ -308,6 +468,18 @@
     pieces.append(turn_pair(mine(down_weight, PANEL), low))
     mlp_full = plane_gather(jnp.concatenate(pieces, axis=0)).reshape(16, 1056, PANEL)
 
+    qkv_shard = jnp.concatenate(
+        [mine(query_weight, QW), mine(key_weight, KW), mine(value_weight, KW)], axis=1
+    )
+    qkv_full = ring_gather(ring_gather(pair_x(qkv_shard, low), RING_Y, y), RING_Z, z)
+    out_shard = mine(output_weight, QW)
+    out_rows = jnp.zeros((W_ROWS, D), BF)
+    for k in range(4):
+        out_rows = lax.dynamic_update_slice_in_dim(
+            out_rows, everywhere(out_shard, TURN_OUT[k]), lax.rem(z + 4 - k, 4) * PANEL, 1
+        )
+    out_full = ring_gather(pair_x(out_rows, low), RING_Y, y)
+
     places = jnp.stack([segment_ids, positions, padding])
     places = group_gather(places[None])
     segments, spots, pads = places[:, 0], places[:, 1], places[:, 2]
@@ -320,21 +492,10 @@
     n_first = inputs * inverse_rms(inputs)
     first_low = (n_first * first_gain).astype(BF)
 
-    qkv = dot(first_low, qkv_full)
     half = HEAD_DIM // 2
     freq = 10000.0 ** (-(jnp.arange(half, dtype=F32) * 2.0 / HEAD_DIM))
-    angles = spots.reshape(SLOTS, 1).astype(F32) * jnp.tile(freq, 2)[None]
+    angles = spots.reshape(SLOTS, 1).astype(F32) * jnp.tile(freq, LANES // half)[None]
     cosine, sine = jnp.cos(angles), jnp.sin(angles)
-    cosine_q, sine_q = jnp.tile(cosine, (1, GROUPS)), jnp.tile(sine, (1, GROUPS))
-
-    q_lin, k_lin = qkv[:, :QW], qkv[:, QW : QW + KW]
-    query_rot = (q_lin * cosine_q + turned(q_lin) * sine_q).astype(BF)
-    key_rot = (k_lin * cosine + turned(k_lin) * sine).astype(BF)
-    value_low = qkv[:, QW + KW :].astype(BF)
-    query_rot = query_rot.reshape(MEMBERS, ROWS, GROUPS, HEAD_DIM)
-    key_rot = key_rot.reshape(MEMBERS, ROWS, HEAD_DIM)
-    value_low = value_low.reshape(MEMBERS, ROWS, HEAD_DIM)
-
     column = jnp.arange(ROWS, dtype=jnp.int32)
     allowed = jnp.logical_and(
         jnp.logical_and(
@@ -342,99 +503,56 @@
             (column[None, :] <= column[:, None])[None],
         ),
         jnp.logical_or(pads[:, None, :] == 1, (column[None, :] == column[:, None])[None]),
-    )
-    scores = jnp.einsum("bqgd,bsd->bgqs", query_rot, key_rot, preferred_element_type=F32)
-    masked = jnp.where(allowed[:, None], scores * score_scale, -1e30)
-    row_max = jnp.max(masked, axis=-1, keepdims=True)
-    log_total = row_max + jnp.log(jnp.sum(jnp.exp(masked - row_max), axis=-1, keepdims=True))
-    probs = jnp.exp(masked - log_total)
-    probs_low = probs.astype(BF)
-    attended = jnp.einsum("bgqs,bsd->bqgd", probs_low, value_low, preferred_element_type=F32)
-    attended_low = attended.reshape(SLOTS, QW).astype(BF)
-
-    out_part = jnp.concatenate([dot(attended_low, out_full[c]) for c in range(4)], axis=1)
-    middle = tokens.astype(F32) + group_scatter(out_part)
+    ).astype(F32)
+
+    query_rot, kv, attended = attention(dot(first_low, qkv_full), cosine, sine, allowed)
+    middle = tokens.astype(F32) + group_scatter(dot(attended, out_full))
     second_low = (middle * inverse_rms(middle) * second_gain).astype(BF)
     second_all = group_gather(second_low)
 
     grad_gu, active, send = mlp_grads(second_all, second_all.T, grads_in, mlp_full)
     mlp_sum = plane_scatter(send.reshape(16 * 1056, PANEL))
-    grad_second = second_grad(grad_gu, mlp_full)
-
-    down_full = mlp_full[:, 704:].reshape(4, FW, PANEL)
-    down_part = jnp.concatenate([dot(active[:, :FW], down_full[c]) for c in range(4)], axis=1)
-    block_output = (middle + group_scatter(down_part)).astype(BF)
-
-    grad_second = group_scatter(grad_second)
+    grad_second = group_scatter(second_grad(grad_gu, mlp_full))
     back, n_second = norm_back(middle, second_gain, grad_second)
     mlp_gain_part = jnp.sum(grad_second * n_second, axis=0)
     grad_middle = cotangent.astype(F32) + back
     middle_all = group_gather(grad_middle.astype(BF))
 
-    grad_out = jnp.concatenate(
-        [
-            left_product(attended_low, middle_all[:, c * PANEL : (c + 1) * PANEL])
-            for c in range(4)
-        ],
-        axis=0,
-    )
-    grad_attended = sum(
-        right_product(middle_all[:, c * PANEL : (c + 1) * PANEL], out_full[c]) for c in range(4)
-    ).astype(BF)
-    grad_attended = grad_attended.reshape(MEMBERS, ROWS, GROUPS, HEAD_DIM)
-
-    grad_value = jnp.einsum(
-        "bgqs,bqgd->bsd", probs_low, grad_attended, preferred_element_type=F32
-    )
-    grad_probs = jnp.einsum(
-        "bqgd,bsd->bgqs", grad_attended, value_low, preferred_element_type=F32
-    )
-    grad_scores = (
-        probs * (grad_probs - jnp.sum(grad_probs * probs, axis=-1, keepdims=True))
-    ).astype(BF)
-    grad_query = (
-        jnp.einsum("bgqs,bsd->bqgd", grad_scores, key_rot, preferred_element_type=F32) * score_scale
-    ).reshape(SLOTS, QW)
-    grad_key = (
-        jnp.einsum("bgqs,bqgd->bsd", grad_scores, query_rot, preferred_element_type=F32)
-        * score_scale
-    ).reshape(SLOTS, KW)
-    grad_query = grad_query * cosine_q - turned(grad_query) * sine_q
-    grad_key = grad_key * cosine - turned(grad_key) * sine
-    grad_qkv = jnp.concatenate(
-        [grad_query.astype(BF), grad_key.astype(BF), grad_value.reshape(SLOTS, KW).astype(BF)],
-        axis=1,
-    )
-
-    qkv_send = left_product(first_low, grad_qkv)
-    attn_sum = plane_scatter(
-        jnp.concatenate([qkv_send.astype(BF), grad_out.astype(BF)], axis=1)
-    )
-
+    grad_attended = right_product(middle_all, out_full).astype(BF)
+    grad_qkv = attention_back(query_rot, kv, grad_attended, cosine, sine, allowed)
+    grad_qkv, active = lax.optimization_barrier((grad_qkv, active))
+
+    qkv_part = ring_scatter(left_product(first_low, grad_qkv).astype(BF), RING_Z, z)
+    out_part = ring_scatter(left_product(attended, middle_all).astype(BF), RING_Y, y).astype(BF)
+    out_part = sum(
+        everywhere(
+            lax.dynamic_slice_in_dim(out_part, lax.rem(z + k, 4) * PANEL, PANEL, 1), TURN_IN[k]
+        ).astype(F32)
+        for k in range(4)
+    )
     grad_first = right_product(grad_qkv, qkv_full)
     attn_gain_part = jnp.sum(grad_first * n_first, axis=0)
-    grad_first = group_scatter(grad_first)
-    back, _ = norm_back(tokens.astype(F32), first_gain, grad_first)
-    input_grad = grad_middle + back
-
-    gains = jnp.stack([attn_gain_part, mlp_gain_part])
-    for ring in (RING_Z, RING_Y):
-        gains = gains + sum(lax.ppermute(gains, "dp", pairs) for pairs in ring)
-    gains = gains + swap_x(gains)
-    gains = gains + swap_far(gains)
-    gains = gains + swap_core(gains)
-
-    qkv_part = attn_sum[:, :QKVW]
-    out_part = turn(attn_sum[:, QKVW:])
-    both = jnp.concatenate([qkv_part, out_part], axis=1)
-    kept = jnp.where(low, both[:W_ROWS], both[W_ROWS:])
-    given = jnp.where(low, both[W_ROWS:], both[:W_ROWS])
-    own_total = kept.astype(F32) + swap_x(given).astype(F32)
-    far_total = swap_far(kept).astype(F32) + lax.ppermute(
-        given, ("grp", "dp"), SWAP_FAR_X
-    ).astype(F32)
+    gains = jnp.stack([attn_gain_part, mlp_gain_part]).reshape(32, LANES)
+    gains = gains + sum(lax.ppermute(gains, "dp", p) for p in RING_Z)
+    rider = jnp.concatenate([two_parts(gains), jnp.zeros((W_ROWS, LANES), BF)], axis=0)
+    qkv_part = ring_scatter(qkv_part.astype(BF), RING_Y, y, rider)
+    gains = two_parts(one_part(qkv_part[:W_ROWS, QKVW:]))
+
+    both = jnp.concatenate([qkv_part[:, :QKVW], out_part], axis=1).astype(BF)
+    kept, given = halves(both, low)
+    width = QKVW + PANEL
+    near = swap_x(jnp.concatenate([given, gains], axis=1))
+    far = swap_far(jnp.concatenate([kept, gains], axis=1))
+    far_x = everywhere(jnp.concatenate([given, gains], axis=1), SWAP_FAR_X)
+    own_total = kept.astype(F32) + near[:, :width].astype(F32)
+    far_total = far[:, :width].astype(F32) + far_x[:, :width].astype(F32)
+    gains = sum(one_part(part) for part in (gains, near[:, width:], far[:, width:], far_x[:, width:]))
     totals = jnp.concatenate([own_total, far_total], axis=0).astype(BF)
-    totals = jnp.concatenate([totals, swap_core(totals)], axis=0).astype(F32)
+    rider = jnp.concatenate([two_parts(gains), jnp.zeros((W_ROWS, LANES), BF)], axis=0)
+    other = swap_core(jnp.concatenate([totals, rider], axis=1))
+    gains = gains + one_part(other[:W_ROWS, width:])
+    totals = jnp.concatenate([totals, other[:, :width]], axis=0).astype(F32)
+
     own_moment = jnp.concatenate(
         [query_moment, key_moment, value_moment, output_moment], axis=1
     )
@@ -447,40 +565,44 @@
 
     mine_at = (member // 2) + 2 * (member % 2)
 
-    def in_order(slots):
+    def by_member(slots):
         return [
             lax.dynamic_index_in_dim(slots, mine_at ^ at, 0, keepdims=False) for at in (0, 2, 1, 3)
         ]
 
-    attn_moved = in_order((0.5 * moments + 0.5 * totals).reshape(MEMBERS, W_ROWS, QKVW + PANEL))
-
-    gu_rows = sum_x(
-        jnp.concatenate(
-            [mlp_sum[j * 128 : (j + 1) * 128] for j in range(5)]
-            + [jnp.concatenate([mlp_sum[640:704, :256], mlp_sum[640:704, 256:]], axis=0)],
-            axis=1,
-        ),
-        low,
-    )
-    down_rows = turn(sum_x(mlp_sum[704:], low).astype(BF)).astype(F32)
-    gate_rows, up_rows = unpanels(gu_rows)
+    attn_moved = by_member((0.5 * moments + 0.5 * totals).reshape(MEMBERS, W_ROWS, width))
+
+    gu_part = jnp.concatenate(
+        [mlp_sum[j * 128 : (j + 1) * 128] for j in range(5)]
+        + [jnp.concatenate([mlp_sum[640:704, :256], mlp_sum[640:704, 256:]], axis=0)],
+        axis=1,
+    )
+    kept, given = halves(gu_part, low)
+    gate_rows, up_rows = unpanels(kept.astype(F32) + swap_x(given).astype(F32))
+    kept, given = halves(mlp_sum[704:], low)
+    down_rows = (kept.astype(F32) + swap_x(given).astype(F32)).astype(BF)
+    down_rows = everywhere(down_rows, TURN).astype(F32)
     gate_momentum = 0.5 * gate_moment + 0.5 * gate_rows
     up_momentum = 0.5 * up_moment + 0.5 * up_rows
     down_momentum = 0.5 * down_moment + 0.5 * down_rows
-    gu_moved = in_order(
+    gu_moved = by_member(
         group_gather(jnp.concatenate([gate_momentum, up_momentum], axis=1).astype(BF)).reshape(
             MEMBERS, W_ROWS, GUW
         )
     )
-    down_moved = in_order(
+    down_moved = by_member(
         group_gather(down_momentum.astype(BF)).reshape(MEMBERS, DOWN_ROWS, PANEL)
     )
 
-    def updated(weight, columns, start, width):
-        moved = jnp.concatenate([block[:, start : start + width] for block in columns], axis=1)
+    def updated(weight, columns, start, size):
+        moved = jnp.concatenate([block[:, start : start + size] for block in columns], axis=1)
         return weight - learn_rate * moved.astype(F32)
 
-    gains = 0.5 * jnp.stack([attn_moment, mlp_moment]) + 0.5 * gains
+    block_output = (middle + group_scatter(down_product(active, mlp_full))).astype(BF)
+    back, _ = norm_back(tokens.astype(F32), first_gain, group_scatter(grad_first))
+    input_grad = grad_middle + back
+
+    gains = 0.5 * jnp.stack([attn_moment, mlp_moment]) + 0.5 * gains.reshape(2, D)
     return (
         block_output,
         input_grad,
@@ -510,9 +632,9 @@
     flat = P(("grp", "dp"))
     weight = P("dp", None)
     moment = P("dp", "grp")
-    whole = P()
-    weights = (whole,) + (weight,) * 4 + (whole,) + (weight,) * 3
-    moments = (whole,) + (moment,) * 4 + (whole,) + (moment,) * 3
+    everyone = P()
+    weights = (everyone,) + (weight,) * 4 + (everyone,) + (weight,) * 3
+    moments = (everyone,) + (moment,) * 4 + (everyone,) + (moment,) * 3
     return jax.shard_map(
         on_device,
         mesh=mesh,

time: 617 us -> 495 us (0.80)
  waiting for transfers between devices: 287 us -> 220 us
  local copies, waits for them, and re-layouts: 60.3 us -> 28.1 us
  other arithmetic: 58 us -> 29.8 us
  matrix products: 36 us -> 14.9 us
  Pallas kernels: 41.9 us -> 57.7 us
  starting transfers between devices: 113 us -> 120 us
    ppermute x13 -> x33, waiting for transfers between devices: 11.3 us -> 131 us  [the longest x9 62.2 us: ring_gather(): lax.ppermute(v, 'dp', p)]
    reduce_scatter x2 -> x1, waiting for transfers between devices: 110 us -> 0.02 us  [plane_scatter(): lax.psum_scatter(v, 'dp', scatter_dimension=0, tiled=True, axis_index_gro...]
    all_gather x2 -> x1, waiting for transfers between devices: 59.4 us -> 0.01 us  [plane_gather(): return lax.all_gather(v, 'dp', axis=0, tiled=True, axis_index_groups=PLANES)]
    ppermute x14 -> x13, waiting for transfers between devices: 92 us -> 62.5 us  [swap_far(): return lax.ppermute(v, 'grp', SWAP_FAR)]
    ppermute x14 -> x13, starting transfers between devices: 46.8 us -> 22 us  [swap_far(): return lax.ppermute(v, 'grp', SWAP_FAR)]
    ppermute x13 -> x33, starting transfers between devices: 34.9 us -> 58.4 us  [the longest x12 33.4 us: everywhere(): return lax.ppermute(v, ('grp', 'dp'), pairs)]
    concatenate x5 -> x6, other arithmetic: 19.9 us -> 0.25 us  [the longest x2 0.13 us: in_order(): jnp.concatenate([jnp.where(low, own, other), jnp.where(low, other, own)],...]
    pallas_call x0 -> x3, Pallas kernels: none -> 15.3 us  [the longest x1 6.11 us: down_product(): pl.pallas_call(down_kernel, grid=(4,), in_specs=[whole((SLOTS, FW)), pl.B...]
  transfers between devices with their start and end apart: 51 -> 67, of which waited for: 33 -> 37; matrix products, arithmetic and copies ran while one was open for 12% -> 13% of each run, Pallas kernels for 0% -> 5%
where the time goes in v3:
time: 495 us; the launch traced here: 487 us
  waiting for transfers between devices  220 us (44%)
  starting transfers between devices  120 us (24%)
  Pallas kernels  57.7 us (12%)
  other arithmetic  29.8 us (6%)
  local copies, waits for them, and re-layouts  28.1 us (6%)
  between operations  16.4 us (3%)
  matrix products  14.9 us (3%)
    ppermute x13, waiting for transfers between devices, swap_far(): return lax.ppermute(v, 'grp', SWAP_FAR)  62.5 us
    ppermute x9, waiting for transfers between devices, ring_gather(): lax.ppermute(v, 'dp', p)  62.2 us
    ppermute x9, waiting for transfers between devices, ring_scatter(): total = total + lax.ppermute(chunk(k + 1), 'dp', p).astype(F32)  37.6 us
    ppermute x12, starting transfers between devices, everywhere(): return lax.ppermute(v, ('grp', 'dp'), pairs)  33.4 us
    pallas_call x1, Pallas kernels, mlp_grads(): pl.pallas_call(mlp_kernel, grid=(6,), in_specs=[whole((512, 2048)), whole...  32.5 us
    ppermute x12, waiting for transfers between devices, everywhere(): return lax.ppermute(v, ('grp', 'dp'), pairs)  31 us
    ppermute x13, starting transfers between devices, swap_core(): return lax.ppermute(v, 'grp', SWAP_CORE)  30.5 us
    ppermute x13, starting transfers between devices, swap_far(): return lax.ppermute(v, 'grp', SWAP_FAR)  22 us
  transfers between devices with their start and end apart: 67, of which 37 were waited for; matrix products, arithmetic and copies ran while one was open for 13% of the time, Pallas kernels for 5%

profile of v3, /device:TPU:1, one launch (start us, length us, event | category | flops | bytes accessed | tf_op | source)
XLA Modules:
  0.0 487.3 jit_solution(7610353292789341430)
XLA Ops:
  19.5 6.1 %collective-permute-done.27 = bf16[176,512]{1,0:T(8,128)(2,1)S(1)} collective-permute-done((bf16[176,512]{1,0:T(8,128)(2,1)S(1)}, bf16[176,512]{1,0:T(8,128)(2,1)S(1)}, u32[]{:S(2)}, u32[]{:S(2)}) %collective-permute-start.27) | collective-permute-done | bytes 180256 | tf_op jit(solution)/shard_map/ppermute | solution.py:69
  29.7 11.7 %collective-permute-start.12 = (bf16[64,512]{1,0:T(8,128)(2,1)S(1)}, bf16[64,512]{1,0:T(8,128)(2,1)S(1)}, u32[]{:S(2)}, u32[]{:S(2)}) collective-permute-start(bf16[64,512]{1,0:T(8,128)(2,1)S(1)} %dynamic-slice_convert_fusion.3), channel_id=1, source_target_pairs={{0,8},{1,9},{2,10},{3,11},{4,12},{5,13},{6,14},{7,15},{8,40},{9,41... | collective-permute-start | bytes 196616 | tf_op jit(solution)/shard_map/ppermute | solution.py:69
  64.7 6.2 %collective-permute-done.15 = bf16[64,2048]{1,0:T(8,128)(2,1)S(1)} collective-permute-done((bf16[64,2048]{1,0:T(8,128)(2,1)S(1)}, bf16[64,2048]{1,0:T(8,128)(2,1)S(1)}, u32[]{:S(2)}, u32[]{:S(2)}) %collective-permute-start.15) | collective-permute-done | bytes 262176 | tf_op jit(solution)/shard_map/ppermute | solution.py:57
  79.5 9.5 %collective-permute-done.16 = bf16[128,2048]{1,0:T(8,128)(2,1)S(1)} collective-permute-done((bf16[128,2048]{1,0:T(8,128)(2,1)S(1)}, bf16[128,2048]{1,0:T(8,128)(2,1)S(1)}, u32[]{:S(2)}, u32[]{:S(2)}) %collective-permute-start.16) | collective-permute-done | bytes 524320 | tf_op jit(solution)/shard_map/ppermute | solution.py:85
  89.1 5.5 %collective-permute-start.1 = (bf16[256,2048]{1,0:T(8,128)(2,1)S(1)}, bf16[256,2048]{1,0:T(8,128)(2,1)S(1)}, u32[]{:S(2)}, u32[]{:S(2)}) collective-permute-start(bf16[256,2048]{1,0:T(8,128)(2,1)S(1)} %pad_maximum_fusion.5), channel_id=1, source_target_pairs={{0,32},{32,0},{64,96},{96,64},{1,33},{33,1},{65,97},{97,65},{2,34}... | collective-permute-start | bytes 3145736 | tf_op jit(solution)/shard_map/ppermute | solution.py:61
  94.6 18.8 %collective-permute-done.17 = bf16[128,2048]{1,0:T(8,128)(2,1)S(1)} collective-permute-done((bf16[128,2048]{1,0:T(8,128)(2,1)S(1)}, bf16[128,2048]{1,0:T(8,128)(2,1)S(1)}, u32[]{:S(2)}, u32[]{:S(2)}) %collective-permute-start.17) | collective-permute-done | bytes 524320 | tf_op jit(solution)/shard_map/ppermute | solution.py:85
  123.8 19.0 %collective-permute-done.8 = bf16[512,640]{1,0:T(8,128)(2,1)S(1)} collective-permute-done((bf16[512,640]{1,0:T(8,128)(2,1)S(1)}, bf16[512,640]{1,0:T(8,128)(2,1)S(1)}, u32[]{:S(2)}, u32[]{:S(2)}) %collective-permute-start.8) | collective-permute-done | bytes 655392 | tf_op jit(solution)/shard_map/ppermute | solution.py:85
  150.2 5.8 %collective-permute-start.19 = (bf16[256,2048]{1,0:T(8,128)(2,1)S(1)}, bf16[256,2048]{1,0:T(8,128)(2,1)S(1)}, u32[]{:S(2)}, u32[]{:S(2)}) collective-permute-start(bf16[256,2048]{1,0:T(8,128)(2,1)S(1)} %slice.683), channel_id=1, source_target_pairs={{0,32},{32,0},{64,96},{96,64},{1,33},{33,1},{65,97},{97,65},{2,34}... | collective-permute-start | bytes 3145736 | tf_op jit(solution)/shard_map/ppermute | solution.py:61
  161.7 11.7 %collective-permute-done.20 = bf16[128,2048]{1,0:T(8,128)(2,1)S(1)} collective-permute-done((bf16[128,2048]{1,0:T(8,128)(2,1)S(1)}, bf16[128,2048]{1,0:T(8,128)(2,1)S(1)}, u32[]{:S(2)}, u32[]{:S(2)}) %collective-permute-start.20) | collective-permute-done | bytes 524320 | tf_op jit(solution)/shard_map/ppermute | solution.py:65
  176.9 7.8 %collective-permute-done.23 = bf16[128,2048]{1,0:T(8,128)(2,1)S(1)} collective-permute-done((bf16[128,2048]{1,0:T(8,128)(2,1)S(1)}, bf16[128,2048]{1,0:T(8,128)(2,1)S(1)}, u32[]{:S(2)}, u32[]{:S(2)}) %collective-permute-start.23) | collective-permute-done | bytes 524320 | tf_op jit(solution)/shard_map/ppermute | solution.py:65
  186.8 9.1 %collective-permute-done.21 = bf16[128,2048]{1,0:T(8,128)(2,1)S(1)} collective-permute-done((bf16[128,2048]{1,0:T(8,128)(2,1)S(1)}, bf16[128,2048]{1,0:T(8,128)(2,1)S(1)}, u32[]{:S(2)}, u32[]{:S(2)}) %collective-permute-start.21) | collective-permute-done | bytes 524320 | tf_op jit(solution)/shard_map/ppermute | solution.py:65
  204.1 32.5 %mlp_grads.1 = (bf16[512,3072]{1,0:T(8,128)(2,1)}, bf16[512,1536]{1,0:T(8,128)(2,1)}, bf16[16,1056,512]{2,1,0:T(8,128)(2,1)}) custom-call(bf16[512,2048]{1,0:T(8,128)(2,1)} %get-tuple-element.101.s_ref, bf16[2048,512]{1,0:T(8,128)(2,1)} %copy.73.st_ref, bf16[512,2048]{1,0:T(8,128)(2,1)} %pad_maximum_fusion.2.c_ref, bf16[16,1056,512]{2,1,0:T(8,128)(2,1)} %bitcast.55, ...), custom_call_target="tpu_custom_call" | custom-call | flops 17999998976 | bytes 45000000 | tf_op jit(solution)/shard_map/mlp_grads/pallas_call | solution.py:214
  238.5 9.9 %second_grad.1 = f32[512,2048]{1,0:T(8,128)S(1)} custom-call(bf16[512,3072]{1,0:T(8,128)(2,1)S(1)} %copy-done, bf16[16,1056,512]{2,1,0:T(8,128)(2,1)} %bitcast.57, bf16[16,1056,512]{2,1,0:T(8,128)(2,1)} %bitcast.58), custom_call_target="tpu_custom_call" | custom-call | flops 6000000000 | bytes 20000000 | tf_op jit(solution)/shard_map/second_grad/pallas_call | solution.py:245
  254.1 12.4 %collective-permute-done.29 = bf16[128,2048]{1,0:T(8,128)(2,1)S(1)} collective-permute-done((bf16[128,2048]{1,0:T(8,128)(2,1)S(1)}, bf16[128,2048]{1,0:T(8,128)(2,1)S(1)}, u32[]{:S(2)}, u32[]{:S(2)}) %collective-permute-start.29) | collective-permute-done | bytes 524320 | tf_op jit(solution)/shard_map/ppermute | solution.py:65
  271.3 11.5 %collective-permute-done.30 = bf16[128,2048]{1,0:T(8,128)(2,1)S(1)} collective-permute-done((bf16[128,2048]{1,0:T(8,128)(2,1)S(1)}, bf16[128,2048]{1,0:T(8,128)(2,1)S(1)}, u32[]{:S(2)}, u32[]{:S(2)}) %collective-permute-start.30) | collective-permute-done | bytes 524320 | tf_op jit(solution)/shard_map/ppermute | solution.py:65
  292.1 5.9 %attention_back.1 = bf16[512,640]{1,0:T(8,128)(2,1)S(1)} custom-call(bf16[512,512]{1,0:T(8,128)(2,1)S(1)} %copy-done.9, bf16[512,128]{1,0:T(8,128)(2,1)S(1)} %get-tuple-element.30.kv_ref, bf16[512,512]{1,0:T(8,128)(2,1)S(1)} %convolution_convert_fusion.2.grad_ref, f32[512,128]{1,0:T(8,128)S(1)} %copy-done.3, f32[512,128]{1,0:T(8,128)S(1)} %get-tuple-element.185.sin_ref, ...), custom_call_target="tpu_custom_call" | custom-call | flops 800000000 | bytes 4000000 | tf_op jit(solution)/shard_map/attention_back/pallas_call | solution.py:380
  314.5 12.8 %collective-permute-done.47 = bf16[128,2048]{1,0:T(8,128)(2,1)S(1)} collective-permute-done((bf16[128,2048]{1,0:T(8,128)(2,1)S(1)}, bf16[128,2048]{1,0:T(8,128)(2,1)S(1)}, u32[]{:S(2)}, u32[]{:S(2)}) %collective-permute-start.47) | collective-permute-done | bytes 524320 | tf_op jit(solution)/shard_map/ppermute | solution.py:99
  328.2 11.6 %collective-permute-done.45 = bf16[128,2048]{1,0:T(8,128)(2,1)S(1)} collective-permute-done((bf16[128,2048]{1,0:T(8,128)(2,1)S(1)}, bf16[128,2048]{1,0:T(8,128)(2,1)S(1)}, u32[]{:S(2)}, u32[]{:S(2)}) %collective-permute-start.45) | collective-permute-done | bytes 524320 | tf_op jit(solution)/shard_map/ppermute | solution.py:99
  345.8 6.2 %collective-permute-start.48 = (bf16[128,512]{1,0:T(8,128)(2,1)S(1)}, bf16[128,512]{1,0:T(8,128)(2,1)S(1)}, u32[]{:S(2)}, u32[]{:S(2)}) collective-permute-start(bf16[128,512]{1,0:T(8,128)(2,1)S(1)} %get-tuple-element.134), channel_id=1, source_target_pairs={{0,0},{1,1},{2,2},{3,3},{4,4},{5,5},{6,6},{7,7},{8,32},{9,33},{10,... | collective-permute-start | bytes 393224 | tf_op jit(solution)/shard_map/ppermute | solution.py:69
  365.6 6.1 %collective-permute-done.42 = bf16[128,768]{1,0:T(8,128)(2,1)S(1)} collective-permute-done((bf16[128,768]{1,0:T(8,128)(2,1)S(1)}, bf16[128,768]{1,0:T(8,128)(2,1)S(1)}, u32[]{:S(2)}, u32[]{:S(2)}) %collective-permute-start.42) | collective-permute-done | bytes 196640 | tf_op jit(solution)/shard_map/ppermute | solution.py:99
  376.7 6.1 %down_product.1 = f32[512,2048]{1,0:T(8,128)S(1)} custom-call(bf16[512,1536]{1,0:T(8,128)(2,1)S(1)} %copy-done.1, bf16[16,1056,512]{2,1,0:T(8,128)(2,1)} %bitcast.59), custom_call_target="tpu_custom_call" | custom-call | flops 3000000000 | bytes 12000000 | tf_op jit(solution)/shard_map/down_product/pallas_call | solution.py:262
  391.6 17.1 %collective-permute-done.54 = bf16[64,1280]{1,0:T(8,128)(2,1)S(1)} collective-permute-done((bf16[64,1280]{1,0:T(8,128)(2,1)S(1)}, bf16[64,1280]{1,0:T(8,128)(2,1)S(1)}, u32[]{:S(2)}, u32[]{:S(2)}) %collective-permute-start.54) | collective-permute-done | bytes 163872 | tf_op jit(solution)/shard_map/ppermute | solution.py:69
  420.0 7.5 %collective-permute-done.35 = bf16[128,2048]{1,0:T(8,128)(2,1)S(1)} collective-permute-done((bf16[128,2048]{1,0:T(8,128)(2,1)}, bf16[128,2048]{1,0:T(8,128)(2,1)S(1)}, u32[]{:S(2)}, u32[]{:S(2)}) %collective-permute-start.35) | collective-permute-done | bytes 524320 | tf_op jit(solution)/shard_map/ppermute | solution.py:65
  437.6 8.8 %collective-permute-done.57 = bf16[176,512]{1,0:T(8,128)(2,1)S(1)} collective-permute-done((bf16[176,512]{1,0:T(8,128)(2,1)S(1)}, bf16[176,512]{1,0:T(8,128)(2,1)S(1)}, u32[]{:S(2)}, u32[]{:S(2)}) %collective-permute-start.57) | collective-permute-done | bytes 180256 | tf_op jit(solution)/shard_map/ppermute | solution.py:57
  (451 shorter events, 211.1 us)
Async XLA Ops:
  7.2 196.9 %all-gather.2.cloned.1.call-start = ((), (), s32[]{:S(2)}) async-start(), calls=%async_computation.1 | async-start | bytes 18382848 | tf_op jit(solution)/shard_map/all_gather | solution.py:73
  26.8 401.2 %reduce-scatter.2.cloned.1.call-start = ((), (), s32[]{:S(2)}) async-start(), calls=%async_computation.2 | async-start | bytes 18382848 | tf_op jit(solution)/shard_map/reduce_scatter | solution.py:77
  27.7 23.6 %collective-permute-start.11 = (bf16[64,512]{1,0:T(8,128)(2,1)S(1)}, bf16[64,512]{1,0:T(8,128)(2,1)S(1)}, u32[]{:S(2)}, u32[]{:S(2)}) collective-permute-start(bf16[64,512]{1,0:T(8,128)(2,1)S(1)} %dynamic-slice_convert_fusion.3), channel_id=1, source_target_pairs={{0,0},{1,1},{2,2},{3,3},{4,4},{5,5},{6,6},{7,7},{8,32},{9,33},{10,... | collective-permute-start | bytes 196616 | tf_op jit(solution)/shard_map/ppermute | solution.py:69
  29.7 22.9 %collective-permute-start.12 = (bf16[64,512]{1,0:T(8,128)(2,1)S(1)}, bf16[64,512]{1,0:T(8,128)(2,1)S(1)}, u32[]{:S(2)}, u32[]{:S(2)}) collective-permute-start(bf16[64,512]{1,0:T(8,128)(2,1)S(1)} %dynamic-slice_convert_fusion.3), channel_id=1, source_target_pairs={{0,8},{1,9},{2,10},{3,11},{4,12},{5,13},{6,14},{7,15},{8,40},{9,41... | collective-permute-start | bytes 196616 | tf_op jit(solution)/shard_map/ppermute | solution.py:69
  51.3 27.0 %collective-permute-start = (bf16[128,2048]{1,0:T(8,128)(2,1)S(1)}, bf16[128,2048]{1,0:T(8,128)(2,1)S(1)}, u32[]{:S(2)}, u32[]{:S(2)}) collective-permute-start(bf16[128,2048]{1,0:T(8,128)(2,1)S(1)} %copy-done.12), channel_id=1, source_target_pairs={{0,64},{32,96},{64,0},{96,32},{1,65},{33,97},{65,1},{97,33},{2,66}... | collective-permute-start | bytes 1572872 | tf_op jit(solution)/shard_map/ppermute | solution.py:65
  72.8 46.6 %collective-permute-start.6 = (bf16[512,640]{1,0:T(8,128)(2,1)S(1)}, bf16[512,640]{1,0:T(8,128)(2,1)S(1)}, u32[]{:S(2)}, u32[]{:S(2)}) collective-permute-start(bf16[512,640]{1,0:T(8,128)(2,1)S(1)} %constant_dynamic-update-slice_fusion.38), channel_id=1, source_target_pairs={{0,8},{1,9},{2,10},{3,11},{4,12},{5,13},{6,14},{7,15},{8,16},{9,17... | collective-permute-start | bytes 1966088 | tf_op jit(solution)/shard_map/ppermute | solution.py:85
  73.2 50.5 %collective-permute-start.7 = (bf16[512,640]{1,0:T(8,128)(2,1)S(1)}, bf16[512,640]{1,0:T(8,128)(2,1)S(1)}, u32[]{:S(2)}, u32[]{:S(2)}) collective-permute-start(bf16[512,640]{1,0:T(8,128)(2,1)S(1)} %constant_dynamic-update-slice_fusion.38), channel_id=1, source_target_pairs={{0,16},{1,17},{2,18},{3,19},{4,20},{5,21},{6,22},{7,23},{8,24},{9,... | collective-permute-start | bytes 1966088 | tf_op jit(solution)/shard_map/ppermute | solution.py:85
  75.3 38.0 %collective-permute-start.17 = (bf16[128,2048]{1,0:T(8,128)(2,1)S(1)}, bf16[128,2048]{1,0:T(8,128)(2,1)S(1)}, u32[]{:S(2)}, u32[]{:S(2)}) collective-permute-start(bf16[128,2048]{1,0:T(8,128)(2,1)S(1)} %get-tuple-element.139), channel_id=1, source_target_pairs={{0,4},{1,5},{2,6},{3,7},{4,0},{5,1},{6,2},{7,3},{8,12},{9,13},{10,... | collective-permute-start | bytes 1572872 | tf_op jit(solution)/shard_map/ppermute | solution.py:85
  78.3 41.0 %collective-permute-start.18 = (bf16[128,2048]{1,0:T(8,128)(2,1)S(1)}, bf16[128,2048]{1,0:T(8,128)(2,1)S(1)}, u32[]{:S(2)}, u32[]{:S(2)}) collective-permute-start(bf16[128,2048]{1,0:T(8,128)(2,1)S(1)} %get-tuple-element.139), channel_id=1, source_target_pairs={{0,6},{1,7},{2,0},{3,1},{4,2},{5,3},{6,4},{7,5},{8,14},{9,15},{10,... | collective-permute-start | bytes 1572872 | tf_op jit(solution)/shard_map/ppermute | solution.py:85
  89.1 53.9 %collective-permute-start.1 = (bf16[256,2048]{1,0:T(8,128)(2,1)S(1)}, bf16[256,2048]{1,0:T(8,128)(2,1)S(1)}, u32[]{:S(2)}, u32[]{:S(2)}) collective-permute-start(bf16[256,2048]{1,0:T(8,128)(2,1)S(1)} %pad_maximum_fusion.5), channel_id=1, source_target_pairs={{0,32},{32,0},{64,96},{96,64},{1,33},{33,1},{65,97},{97,65},{2,34}... | collective-permute-start | bytes 3145736 | tf_op jit(solution)/shard_map/ppermute | solution.py:61
  113.4 29.5 %collective-permute-start.8 = (bf16[512,640]{1,0:T(8,128)(2,1)S(1)}, bf16[512,640]{1,0:T(8,128)(2,1)S(1)}, u32[]{:S(2)}, u32[]{:S(2)}) collective-permute-start(bf16[512,640]{1,0:T(8,128)(2,1)S(1)} %constant_dynamic-update-slice_fusion.38), channel_id=1, source_target_pairs={{0,24},{1,25},{2,26},{3,27},{4,28},{5,29},{6,30},{7,31},{8,0},{9,1... | collective-permute-start | bytes 1966088 | tf_op jit(solution)/shard_map/ppermute | solution.py:85
  161.0 23.6 %collective-permute-start.23 = (bf16[128,2048]{1,0:T(8,128)(2,1)S(1)}, bf16[128,2048]{1,0:T(8,128)(2,1)S(1)}, u32[]{:S(2)}, u32[]{:S(2)}) collective-permute-start(bf16[128,2048]{1,0:T(8,128)(2,1)S(1)} %copy-done.21), channel_id=1, source_target_pairs={{0,64},{32,96},{64,0},{96,32},{1,65},{33,97},{65,1},{97,33},{2,66}... | collective-permute-start | bytes 1572872 | tf_op jit(solution)/shard_map/ppermute | solution.py:65
  174.4 21.4 %collective-permute-start.21 = (bf16[128,2048]{1,0:T(8,128)(2,1)S(1)}, bf16[128,2048]{1,0:T(8,128)(2,1)S(1)}, u32[]{:S(2)}, u32[]{:S(2)}) collective-permute-start(bf16[128,2048]{1,0:T(8,128)(2,1)S(1)} %multiply_convert_fusion), channel_id=1, source_target_pairs={{0,64},{32,96},{64,0},{96,32},{1,65},{33,97},{65,1},{97,33},{2,66}... | collective-permute-start | bytes 1572872 | tf_op jit(solution)/shard_map/ppermute | solution.py:65
  308.4 18.9 %collective-permute-start.47 = (bf16[128,2048]{1,0:T(8,128)(2,1)S(1)}, bf16[128,2048]{1,0:T(8,128)(2,1)S(1)}, u32[]{:S(2)}, u32[]{:S(2)}) collective-permute-start(bf16[128,2048]{1,0:T(8,128)(2,1)S(1)} %get-tuple-element.98), channel_id=1, source_target_pairs={{0,6},{1,7},{2,0},{3,1},{4,2},{5,3},{6,4},{7,5},{8,14},{9,15},{10,... | collective-permute-start | bytes 1572872 | tf_op jit(solution)/shard_map/ppermute | solution.py:99
  308.5 19.7 %collective-permute-start.46 = (bf16[128,2048]{1,0:T(8,128)(2,1)S(1)}, bf16[128,2048]{1,0:T(8,128)(2,1)S(1)}, u32[]{:S(2)}, u32[]{:S(2)}) collective-permute-start(bf16[128,2048]{1,0:T(8,128)(2,1)S(1)} %get-tuple-element.99), channel_id=1, source_target_pairs={{0,4},{1,5},{2,6},{3,7},{4,0},{5,1},{6,2},{7,3},{8,12},{9,13},{10,... | collective-permute-start | bytes 1572872 | tf_op jit(solution)/shard_map/ppermute | solution.py:99
  311.8 28.1 %collective-permute-start.45 = (bf16[128,2048]{1,0:T(8,128)(2,1)S(1)}, bf16[128,2048]{1,0:T(8,128)(2,1)S(1)}, u32[]{:S(2)}, u32[]{:S(2)}) collective-permute-start(bf16[128,2048]{1,0:T(8,128)(2,1)S(1)} %get-tuple-element.97), channel_id=1, source_target_pairs={{0,2},{1,3},{2,4},{3,5},{4,6},{5,7},{6,0},{7,1},{8,10},{9,11},{10,... | collective-permute-start | bytes 1572872 | tf_op jit(solution)/shard_map/ppermute | solution.py:99
  312.2 32.9 %collective-permute-start.38 = (bf16[512,640]{1,0:T(8,128)(2,1)S(1)}, bf16[512,640]{1,0:T(8,128)(2,1)S(1)}, u32[]{:S(2)}, u32[]{:S(2)}) collective-permute-start(bf16[512,640]{1,0:T(8,128)(2,1)S(1)} %get-tuple-element.95), channel_id=1, source_target_pairs={{0,24},{1,25},{2,26},{3,27},{4,28},{5,29},{6,30},{7,31},{8,0},{9,1... | collective-permute-start | bytes 1966088 | tf_op jit(solution)/shard_map/ppermute | solution.py:99
  313.0 32.8 %collective-permute-start.37 = (bf16[512,640]{1,0:T(8,128)(2,1)S(1)}, bf16[512,640]{1,0:T(8,128)(2,1)S(1)}, u32[]{:S(2)}, u32[]{:S(2)}) collective-permute-start(bf16[512,640]{1,0:T(8,128)(2,1)S(1)} %get-tuple-element.96), channel_id=1, source_target_pairs={{0,16},{1,17},{2,18},{3,19},{4,20},{5,21},{6,22},{7,23},{8,24},{9,... | collective-permute-start | bytes 1966088 | tf_op jit(solution)/shard_map/ppermute | solution.py:99
  327.3 24.7 %collective-permute-start.36 = (bf16[512,640]{1,0:T(8,128)(2,1)S(1)}, bf16[512,640]{1,0:T(8,128)(2,1)S(1)}, u32[]{:S(2)}, u32[]{:S(2)}) collective-permute-start(bf16[512,640]{1,0:T(8,128)(2,1)S(1)} %get-tuple-element.94), channel_id=1, source_target_pairs={{0,8},{1,9},{2,10},{3,11},{4,12},{5,13},{6,14},{7,15},{8,16},{9,17... | collective-permute-start | bytes 1966088 | tf_op jit(solution)/shard_map/ppermute | solution.py:99
  383.8 26.1 %collective-permute-start.34 = (bf16[256,2048]{1,0:T(8,128)(2,1)S(1)}, bf16[256,2048]{1,0:T(8,128)(2,1)S(1)}, u32[]{:S(2)}, u32[]{:S(2)}) collective-permute-start(bf16[256,2048]{1,0:T(8,128)(2,1)S(1)} %slice.680), channel_id=1, source_target_pairs={{0,32},{32,0},{64,96},{96,64},{1,33},{33,1},{65,97},{97,65},{2,34}... | collective-permute-start | bytes 3145736 | tf_op jit(solution)/shard_map/ppermute | solution.py:61
  383.9 24.8 %collective-permute-start.54 = (bf16[64,1280]{1,0:T(8,128)(2,1)S(1)}, bf16[64,1280]{1,0:T(8,128)(2,1)S(1)}, u32[]{:S(2)}, u32[]{:S(2)}) collective-permute-start(bf16[64,1280]{1,0:T(8,128)(2,1)S(1)} %fusion.22), channel_id=1, source_target_pairs={{0,65},{1,64},{2,67},{3,66},{4,69},{5,68},{6,71},{7,70},{8,73},{9,... | collective-permute-start | bytes 491528 | tf_op jit(solution)/shard_map/ppermute | solution.py:69
  384.1 24.6 %collective-permute-start.53 = (bf16[64,1280]{1,0:T(8,128)(2,1)S(1)}, bf16[64,1280]{1,0:T(8,128)(2,1)S(1)}, u32[]{:S(2)}, u32[]{:S(2)}) collective-permute-start(bf16[64,1280]{1,0:T(8,128)(2,1)S(1)} %fusion.21), channel_id=1, source_target_pairs={{0,64},{32,96},{64,0},{96,32},{1,65},{33,97},{65,1},{97,33},{2,66}... | collective-permute-start | bytes 491528 | tf_op jit(solution)/shard_map/ppermute | solution.py:65
  385.9 26.6 %collective-permute-start.59 = (bf16[64,1152]{1,0:T(8,128)(2,1)S(1)}, bf16[64,1152]{1,0:T(8,128)(2,1)S(1)}, u32[]{:S(2)}, u32[]{:S(2)}) collective-permute-start(bf16[64,1152]{1,0:T(8,128)(2,1)S(1)} %get-tuple-element.169), channel_id=1, source_target_pairs={{0,64},{32,96},{64,0},{96,32},{1,65},{33,97},{65,1},{97,33},{2,66}... | collective-permute-start | bytes 442376 | tf_op jit(solution)/shard_map/ppermute | solution.py:65
  389.9 77.6 %collective-permute-start.33 = (bf16[128,2048]{1,0:T(8,128)(2,1)}, bf16[128,2048]{1,0:T(8,128)(2,1)}, u32[]{:S(2)}, u32[]{:S(2)}) collective-permute-start(bf16[128,2048]{1,0:T(8,128)(2,1)} %slice.685), channel_id=1, source_target_pairs={{0,64},{32,96},{64,0},{96,32},{1,65},{33,97},{65,1},{97,33},{2,66}... | collective-permute-start | bytes 1572872 | tf_op jit(solution)/shard_map/ppermute | solution.py:65
  (116 other events, 1343.9 us)
Sparse Core Ops, SparseCore 0:
  26.9 148.4 all-gather.1
  236.8 138.1 reduce-scatter.1

commit v4 on v3

--- a/solution.py
+++ b/solution.py
@@ -14,6 +14,7 @@
 QW = 512
 KW = 64
 QKVW = QW + 2 * KW
+SPLIT = 384
 FW = 1408
 GUW = 2 * FW
 PANEL = 512
@@ -79,11 +80,11 @@
     )
 
 
-def ring_gather(v, pairs, at):
-    rows = v.shape[0]
-    out = jnp.zeros((4 * rows,) + v.shape[1:], v.dtype)
+def ring_gather(v, pairs, at, axis=0):
+    rows = v.shape[axis]
+    out = jnp.zeros(v.shape[:axis] + (4 * rows,) + v.shape[axis + 1 :], v.dtype)
     for k, part in enumerate([v] + [lax.ppermute(v, "dp", p) for p in pairs]):
-        out = lax.dynamic_update_slice_in_dim(out, part, lax.rem(at + 4 - k, 4) * rows, 0)
+        out = lax.dynamic_update_slice_in_dim(out, part, lax.rem(at + 4 - k, 4) * rows, axis)
     return out
 
 
@@ -314,12 +315,12 @@
     return jnp.exp(masked - total).reshape(GROUPS * ROWS, ROWS)
 
 
-def attention_kernel(qkv_ref, cos_ref, sin_ref, mask_ref, query_ref, kv_ref, out_ref):
+def attention_kernel(qkv_a, qkv_b, cos_ref, sin_ref, mask_ref, query_ref, kv_ref, out_ref):
     cosine, sine = cos_ref[...], sin_ref[...]
     for g in range(GROUPS // 2):
-        v = qkv_ref[:, g * LANES : (g + 1) * LANES]
+        v = qkv_a[:, g * LANES : (g + 1) * LANES] if g < 3 else qkv_b[:, :LANES]
         query_ref[:, g * LANES : (g + 1) * LANES] = (v * cosine + quarter_turn(v) * sine).astype(BF)
-    v = qkv_ref[:, QW:]
+    v = qkv_b[:, QW - SPLIT :]
     kv = jnp.where(lanes_of(v) < HEAD_DIM, v * cosine + quarter_turn(v) * sine, v)
     kv_ref[...] = kv.astype(BF)
     key2, value2 = doubled(kv)
@@ -357,11 +358,17 @@
 MASK_BLOCK = pl.BlockSpec((1, ROWS, ROWS), lambda b: (b, 0, 0))
 
 
-def attention(qkv, cosine, sine, mask):
+def attention(qkv_a, qkv_b, cosine, sine, mask):
     return pl.pallas_call(
         attention_kernel,
         grid=(MEMBERS,),
-        in_specs=[row_block(QKVW), row_block(LANES), row_block(LANES), MASK_BLOCK],
+        in_specs=[
+            row_block(SPLIT),
+            row_block(QKVW - SPLIT),
+            row_block(LANES),
+            row_block(LANES),
+            MASK_BLOCK,
+        ],
         out_specs=[row_block(QW), row_block(LANES), row_block(QW)],
         out_shape=[
             jax.ShapeDtypeStruct((SLOTS, QW), BF),
@@ -373,7 +380,7 @@
             flops=3 * 10**8, bytes_accessed=4 * 10**6, transcendentals=10**6
         ),
         name="attention",
-    )(qkv, cosine, sine, mask)
+    )(qkv_a, qkv_b, cosine, sine, mask)
 
 
 def attention_back(query, kv, grad, cosine, sine, mask):
@@ -418,15 +425,6 @@
     for at in range(0, FW, 256):
         blocks += [gate[:, at : at + 256], up[:, at : at + 256]]
     return jnp.concatenate(blocks, axis=1)
-
-
-def unpanels(both):
-    gate, up = [], []
-    for at in range(0, FW, 256):
-        width = min(256, FW - at)
-        gate.append(both[:, 2 * at : 2 * at + width])
-        up.append(both[:, 2 * at + width : 2 * at + 2 * width])
-    return jnp.concatenate(gate, axis=1), jnp.concatenate(up, axis=1)
 
 
 def on_device(
@@ -471,20 +469,31 @@
     qkv_shard = jnp.concatenate(
         [mine(query_weight, QW), mine(key_weight, KW), mine(value_weight, KW)], axis=1
     )
-    qkv_full = ring_gather(ring_gather(pair_x(qkv_shard, low), RING_Y, y), RING_Z, z)
-    out_shard = mine(output_weight, QW)
+    qkv_shard = pair_x(qkv_shard, low)
+    qkv_a = ring_gather(qkv_shard[:, :SPLIT], RING_Y, y)
+    qkv_b = ring_gather(qkv_shard[:, SPLIT:], RING_Z, z).reshape(4, 128, QKVW - SPLIT)
+    qkv_a, qkv_b, out_shard = lax.optimization_barrier((qkv_a, qkv_b, mine(output_weight, QW)))
+    qkv_a = ring_gather(qkv_a, RING_Z, z)
+    qkv_b = ring_gather(qkv_b, RING_Y, y, 1).reshape(D, QKVW - SPLIT)
     out_rows = jnp.zeros((W_ROWS, D), BF)
     for k in range(4):
         out_rows = lax.dynamic_update_slice_in_dim(
             out_rows, everywhere(out_shard, TURN_OUT[k]), lax.rem(z + 4 - k, 4) * PANEL, 1
         )
-    out_full = ring_gather(pair_x(out_rows, low), RING_Y, y)
+    out_rows = pair_x(out_rows, low)
+    qkv_a, qkv_b, out_rows = lax.optimization_barrier((qkv_a, qkv_b, out_rows))
+    out_full = ring_gather(out_rows, RING_Y, y)
 
     places = jnp.stack([segment_ids, positions, padding])
     places = group_gather(places[None])
     segments, spots, pads = places[:, 0], places[:, 1], places[:, 2]
     rows_in = group_gather(tokens)
     grads_in = group_gather(cotangent)
+    own_moment = jnp.concatenate(
+        [query_moment, key_moment, value_moment, output_moment], axis=1
+    )
+    grads_in, moments = lax.optimization_barrier((grads_in, group_gather(own_moment.astype(BF))))
+    moments = moments.astype(F32)
 
     first_gain = rounded_gain(attn_gain)
     second_gain = rounded_gain(mlp_gain)
@@ -505,7 +514,9 @@
         jnp.logical_or(pads[:, None, :] == 1, (column[None, :] == column[:, None])[None]),
     ).astype(F32)
 
-    query_rot, kv, attended = attention(dot(first_low, qkv_full), cosine, sine, allowed)
+    query_rot, kv, attended = attention(
+        dot(first_low, qkv_a), dot(first_low, qkv_b), cosine, sine, allowed
+    )
     middle = tokens.astype(F32) + group_scatter(dot(attended, out_full))
     second_low = (middle * inverse_rms(middle) * second_gain).astype(BF)
     second_all = group_gather(second_low)
@@ -518,20 +529,31 @@
     grad_middle = cotangent.astype(F32) + back
     middle_all = group_gather(grad_middle.astype(BF))
 
+    down_part, middle_all = lax.optimization_barrier(
+        (down_product(active, mlp_full), middle_all)
+    )
     grad_attended = right_product(middle_all, out_full).astype(BF)
-    grad_qkv = attention_back(query_rot, kv, grad_attended, cosine, sine, allowed)
-    grad_qkv, active = lax.optimization_barrier((grad_qkv, active))
-
-    qkv_part = ring_scatter(left_product(first_low, grad_qkv).astype(BF), RING_Z, z)
-    out_part = ring_scatter(left_product(attended, middle_all).astype(BF), RING_Y, y).astype(BF)
+    grad_out = left_product(attended, middle_all).astype(BF)
+    grad_attended, grad_out = lax.optimization_barrier((grad_attended, grad_out))
+    block_output = (middle + group_scatter(down_part)).astype(BF)
+    out_part = ring_scatter(grad_out, RING_Y, y).astype(BF)
     out_part = sum(
         everywhere(
             lax.dynamic_slice_in_dim(out_part, lax.rem(z + k, 4) * PANEL, PANEL, 1), TURN_IN[k]
         ).astype(F32)
         for k in range(4)
     )
-    grad_first = right_product(grad_qkv, qkv_full)
+    grad_qkv = attention_back(query_rot, kv, grad_attended, cosine, sine, allowed)
+    qkv_part = left_product(first_low, grad_qkv).astype(BF)
+    qkv_part, grad_qkv = lax.optimization_barrier((qkv_part, grad_qkv))
+    qkv_part = ring_scatter(qkv_part, RING_Z, z)
+    grad_first = right_product(grad_qkv[:, :SPLIT], qkv_a) + right_product(
+        grad_qkv[:, SPLIT:], qkv_b
+    )
     attn_gain_part = jnp.sum(grad_first * n_first, axis=0)
+    back, _ = norm_back(tokens.astype(F32), first_gain, group_scatter(grad_first))
+    input_grad = grad_middle + back
+
     gains = jnp.stack([attn_gain_part, mlp_gain_part]).reshape(32, LANES)
     gains = gains + sum(lax.ppermute(gains, "dp", p) for p in RING_Z)
     rider = jnp.concatenate([two_parts(gains), jnp.zeros((W_ROWS, LANES), BF)], axis=0)
@@ -539,6 +561,7 @@
     gains = two_parts(one_part(qkv_part[:W_ROWS, QKVW:]))
 
     both = jnp.concatenate([qkv_part[:, :QKVW], out_part], axis=1).astype(BF)
+    both, mlp_sum = lax.optimization_barrier((both, mlp_sum))
     kept, given = halves(both, low)
     width = QKVW + PANEL
     near = swap_x(jnp.concatenate([given, gains], axis=1))
@@ -553,10 +576,6 @@
     gains = gains + one_part(other[:W_ROWS, width:])
     totals = jnp.concatenate([totals, other[:, :width]], axis=0).astype(F32)
 
-    own_moment = jnp.concatenate(
-        [query_moment, key_moment, value_moment, output_moment], axis=1
-    )
-    moments = group_gather(own_moment.astype(BF)).astype(F32)
     own_moved = 0.5 * own_moment + 0.5 * own_total
     query_momentum = own_moved[:, :QW]
     key_momentum = own_moved[:, QW : QW + KW]
@@ -572,16 +591,20 @@
 
     attn_moved = by_member((0.5 * moments + 0.5 * totals).reshape(MEMBERS, W_ROWS, width))
 
-    gu_part = jnp.concatenate(
-        [mlp_sum[j * 128 : (j + 1) * 128] for j in range(5)]
-        + [jnp.concatenate([mlp_sum[640:704, :256], mlp_sum[640:704, 256:]], axis=0)],
-        axis=1,
-    )
-    kept, given = halves(gu_part, low)
-    gate_rows, up_rows = unpanels(kept.astype(F32) + swap_x(given).astype(F32))
+    body = mlp_sum[:640].reshape(5, 2, W_ROWS, PANEL)
+    tail = jnp.pad(mlp_sum[640:704].reshape(W_ROWS, 2, 256), ((0, 0), (0, 0), (0, 256)))
+    first = jnp.concatenate([body[:, 0], tail[None, :, 0]], axis=0)
+    second = jnp.concatenate([body[:, 1], tail[None, :, 1]], axis=0)
+    kept, given = jnp.where(low, first, second), jnp.where(low, second, first)
+    gu_total = kept.astype(F32) + swap_x(given).astype(F32)
+    gate_rows = jnp.concatenate(
+        [gu_total[j, :, :256] for j in range(5)] + [gu_total[5, :, :128]], axis=1
+    )
+    up_rows = jnp.concatenate(
+        [gu_total[j, :, 256:] for j in range(5)] + [gu_total[5, :, 128:256]], axis=1
+    )
     kept, given = halves(mlp_sum[704:], low)
-    down_rows = (kept.astype(F32) + swap_x(given).astype(F32)).astype(BF)
-    down_rows = everywhere(down_rows, TURN).astype(F32)
+    down_rows = everywhere(kept, TURN).astype(F32) + everywhere(given, TURN_X).astype(F32)
     gate_momentum = 0.5 * gate_moment + 0.5 * gate_rows
     up_momentum = 0.5 * up_moment + 0.5 * up_rows
     down_momentum = 0.5 * down_moment + 0.5 * down_rows
@@ -597,10 +620,6 @@
     def updated(weight, columns, start, size):
         moved = jnp.concatenate([block[:, start : start + size] for block in columns], axis=1)
         return weight - learn_rate * moved.astype(F32)
-
-    block_output = (middle + group_scatter(down_product(active, mlp_full))).astype(BF)
-    back, _ = norm_back(tokens.astype(F32), first_gain, group_scatter(grad_first))
-    input_grad = grad_middle + back
 
     gains = 0.5 * jnp.stack([attn_moment, mlp_moment]) + 0.5 * gains.reshape(2, D)
     return (

time: 495 us -> 531 us (1.073)
  waiting for transfers between devices: 220 us -> 245 us
  other arithmetic: 29.8 us -> 41.8 us
    ppermute x13, waiting for transfers between devices: 62.5 us -> 90.2 us  [swap_far(): return lax.ppermute(v, 'grp', SWAP_FAR)]
    ppermute x9 -> x15, waiting for transfers between devices: 62.2 us -> 89.1 us  [ring_gather(): lax.ppermute(v, 'dp', p)]
    ppermute x12 -> x13, waiting for transfers between devices: 31 us -> 14.2 us  [everywhere(): return lax.ppermute(v, ('grp', 'dp'), pairs)]
    ppermute x6 -> x5, waiting for transfers between devices: 18.1 us -> 2.13 us  [swap_x(): return lax.ppermute(v, 'dp', SWAP_X)]
    ppermute x13, starting transfers between devices: 22 us -> 37.7 us  [swap_far(): return lax.ppermute(v, 'grp', SWAP_FAR)]
    ppermute x13, starting transfers between devices: 30.5 us -> 17.5 us  [swap_core(): return lax.ppermute(v, 'grp', SWAP_CORE)]
    ppermute x12 -> x13, starting transfers between devices: 33.4 us -> 23.4 us  [everywhere(): return lax.ppermute(v, ('grp', 'dp'), pairs)]
    ppermute x9 -> x15, starting transfers between devices: 13.3 us -> 21.5 us  [ring_gather(): lax.ppermute(v, 'dp', p)]
  transfers between devices with their start and end apart: 67 -> 73, of which waited for: 37 -> 37; matrix products, arithmetic and copies ran while one was open for 13% -> 14% of each run, Pallas kernels for 5% -> 5%
where the time goes in v4:
time: 531 us; the launch traced here: 522 us
  waiting for transfers between devices  245 us (46%)
  starting transfers between devices  119 us (22%)
  Pallas kernels  57.8 us (11%)
  other arithmetic  41.8 us (8%)
  local copies, waits for them, and re-layouts  28 us (5%)
  between operations  16.4 us (3%)
  matrix products  13.7 us (3%)
    ppermute x13, waiting for transfers between devices, swap_far(): return lax.ppermute(v, 'grp', SWAP_FAR)  90.2 us
    ppermute x15, waiting for transfers between devices, ring_gather(): lax.ppermute(v, 'dp', p)  89.1 us
    ppermute x9, waiting for transfers between devices, ring_scatter(): total = total + lax.ppermute(chunk(k + 1), 'dp', p).astype(F32)  42.7 us
    ppermute x13, starting transfers between devices, swap_far(): return lax.ppermute(v, 'grp', SWAP_FAR)  37.7 us
    pallas_call x1, Pallas kernels, mlp_grads(): pl.pallas_call(mlp_kernel, grid=(6,), in_specs=[whole((512, 2048)), whole...  32.3 us
    ppermute x13, starting transfers between devices, everywhere(): return lax.ppermute(v, ('grp', 'dp'), pairs)  23.4 us
    ppermute x15, starting transfers between devices, ring_gather(): lax.ppermute(v, 'dp', p)  21.5 us
    ppermute x13, starting transfers between devices, swap_core(): return lax.ppermute(v, 'grp', SWAP_CORE)  17.5 us
  transfers between devices with their start and end apart: 73, of which 37 were waited for; matrix products, arithmetic and copies ran while one was open for 14% of the time, Pallas kernels for 5%

profile of v4, /device:TPU:1, one launch (start us, length us, event | category | flops | bytes accessed | tf_op | source)
XLA Modules:
  0.0 521.9 jit_solution(5612792421105764824)
XLA Ops:
  19.5 6.1 %collective-permute-done.35 = bf16[176,512]{1,0:T(8,128)(2,1)S(1)} collective-permute-done((bf16[176,512]{1,0:T(8,128)(2,1)S(1)}, bf16[176,512]{1,0:T(8,128)(2,1)S(1)}, u32[]{:S(2)}, u32[]{:S(2)}) %collective-permute-start.35) | collective-permute-done | bytes 180256 | tf_op jit(solution)/shard_map/ppermute | solution.py:70
  29.8 8.8 %collective-permute-start = (bf16[128,2048]{1,0:T(8,128)(2,1)S(1)}, bf16[128,2048]{1,0:T(8,128)(2,1)S(1)}, u32[]{:S(2)}, u32[]{:S(2)}) collective-permute-start(bf16[128,2048]{1,0:T(8,128)(2,1)S(1)} %copy-done.14), channel_id=1, source_target_pairs={{0,64},{32,96},{64,0},{96,32},{1,65},{33,97},{65,1},{97,33},{2,66}... | collective-permute-start | bytes 1572872 | tf_op jit(solution)/shard_map/ppermute | solution.py:66
  40.4 11.5 %collective-permute-done.20 = s32[1,3,128]{2,1,0:T(4,128)S(1)} collective-permute-done((s32[1,3,128]{2,1,0:T(4,128)S(1)}, s32[1,3,128]{2,1,0:T(4,128)S(1)}, u32[]{:S(2)}, u32[]{:S(2)}) %collective-permute-start.20) | collective-permute-done | bytes 1568 | tf_op jit(solution)/shard_map/ppermute | solution.py:66
  72.6 6.1 %collective-permute-start.16 = (bf16[64,512]{1,0:T(8,128)(2,1)}, bf16[64,512]{1,0:T(8,128)(2,1)S(1)}, u32[]{:S(2)}, u32[]{:S(2)}) collective-permute-start(bf16[64,512]{1,0:T(8,128)(2,1)} %dynamic-slice_convert_fusion.3), channel_id=1, source_target_pairs={{0,8},{1,9},{2,10},{3,11},{4,12},{5,13},{6,14},{7,15},{8,40},{9,41... | collective-permute-start | bytes 196616 | tf_op jit(solution)/shard_map/ppermute | solution.py:70
  87.5 6.9 %collective-permute-done.12 = bf16[4,128,256]{2,1,0:T(8,128)(2,1)S(1)} collective-permute-done((bf16[4,128,256]{2,1,0:T(8,128)(2,1)S(1)}, bf16[4,128,256]{2,1,0:T(8,128)(2,1)S(1)}, u32[]{:S(2)}, u32[]{:S(2)}) %collective-permute-start.12) | collective-permute-done | bytes 262176 | tf_op jit(solution)/shard_map/ppermute | solution.py:86
  94.4 11.8 %collective-permute-done.13 = bf16[4,128,256]{2,1,0:T(8,128)(2,1)S(1)} collective-permute-done((bf16[4,128,256]{2,1,0:T(8,128)(2,1)S(1)}, bf16[4,128,256]{2,1,0:T(8,128)(2,1)S(1)}, u32[]{:S(2)}, u32[]{:S(2)}) %collective-permute-start.13) | collective-permute-done | bytes 262176 | tf_op jit(solution)/shard_map/ppermute | solution.py:86
  110.3 17.2 %collective-permute-done.10 = bf16[512,384]{1,0:T(8,128)(2,1)S(1)} collective-permute-done((bf16[512,384]{1,0:T(8,128)(2,1)S(1)}, bf16[512,384]{1,0:T(8,128)(2,1)S(1)}, u32[]{:S(2)}, u32[]{:S(2)}) %collective-permute-start.10) | collective-permute-done | bytes 393248 | tf_op jit(solution)/shard_map/ppermute | solution.py:86
  127.6 13.6 %collective-permute-done.11 = bf16[512,384]{1,0:T(8,128)(2,1)S(1)} collective-permute-done((bf16[512,384]{1,0:T(8,128)(2,1)S(1)}, bf16[512,384]{1,0:T(8,128)(2,1)S(1)}, u32[]{:S(2)}, u32[]{:S(2)}) %collective-permute-start.11) | collective-permute-done | bytes 393248 | tf_op jit(solution)/shard_map/ppermute | solution.py:86
  149.1 17.4 %collective-permute-done.22 = bf16[128,2048]{1,0:T(8,128)(2,1)S(1)} collective-permute-done((bf16[128,2048]{1,0:T(8,128)(2,1)S(1)}, bf16[128,2048]{1,0:T(8,128)(2,1)S(1)}, u32[]{:S(2)}, u32[]{:S(2)}) %collective-permute-start.22) | collective-permute-done | bytes 524320 | tf_op jit(solution)/shard_map/ppermute | solution.py:86
  166.5 14.9 %collective-permute-done.23 = bf16[128,2048]{1,0:T(8,128)(2,1)S(1)} collective-permute-done((bf16[128,2048]{1,0:T(8,128)(2,1)S(1)}, bf16[128,2048]{1,0:T(8,128)(2,1)S(1)}, u32[]{:S(2)}, u32[]{:S(2)}) %collective-permute-start.23) | collective-permute-done | bytes 524320 | tf_op jit(solution)/shard_map/ppermute | solution.py:86
  196.7 11.6 %collective-permute-done.26 = bf16[128,2048]{1,0:T(8,128)(2,1)S(1)} collective-permute-done((bf16[128,2048]{1,0:T(8,128)(2,1)S(1)}, bf16[128,2048]{1,0:T(8,128)(2,1)S(1)}, u32[]{:S(2)}, u32[]{:S(2)}) %collective-permute-start.26) | collective-permute-done | bytes 524320 | tf_op jit(solution)/shard_map/ppermute | solution.py:66
  213.1 6.5 %collective-permute-done.29 = bf16[128,2048]{1,0:T(8,128)(2,1)S(1)} collective-permute-done((bf16[128,2048]{1,0:T(8,128)(2,1)S(1)}, bf16[128,2048]{1,0:T(8,128)(2,1)S(1)}, u32[]{:S(2)}, u32[]{:S(2)}) %collective-permute-start.29) | collective-permute-done | bytes 524320 | tf_op jit(solution)/shard_map/ppermute | solution.py:66
  246.0 32.3 %mlp_grads.1 = (bf16[512,3072]{1,0:T(8,128)(2,1)}, bf16[512,1536]{1,0:T(8,128)(2,1)}, bf16[16,1056,512]{2,1,0:T(8,128)(2,1)}) custom-call(bf16[512,2048]{1,0:T(8,128)(2,1)} %get-tuple-element.93.s_ref, bf16[2048,512]{1,0:T(8,128)(2,1)} %copy.47.st_ref, bf16[512,2048]{1,0:T(8,128)(2,1)} %pad_maximum_fusion.2.c_ref, bf16[16,1056,512]{2,1,0:T(8,128)(2,1)} %bitcast.128, ...), custom_call_target="tpu_custom_call" | custom-call | flops 17999998976 | bytes 45000000 | tf_op jit(solution)/shard_map/mlp_grads/pallas_call | solution.py:215
  280.2 10.2 %second_grad.1 = f32[512,2048]{1,0:T(8,128)S(1)} custom-call(bf16[512,3072]{1,0:T(8,128)(2,1)S(1)} %copy-done.2, bf16[16,1056,512]{2,1,0:T(8,128)(2,1)} %bitcast.130, bf16[16,1056,512]{2,1,0:T(8,128)(2,1)} %bitcast.131), custom_call_target="tpu_custom_call" | custom-call | flops 6000000000 | bytes 20000000 | tf_op jit(solution)/shard_map/second_grad/pallas_call | solution.py:246
  296.3 12.2 %collective-permute-done.37 = bf16[128,2048]{1,0:T(8,128)(2,1)S(1)} collective-permute-done((bf16[128,2048]{1,0:T(8,128)(2,1)S(1)}, bf16[128,2048]{1,0:T(8,128)(2,1)S(1)}, u32[]{:S(2)}, u32[]{:S(2)}) %collective-permute-start.37) | collective-permute-done | bytes 524320 | tf_op jit(solution)/shard_map/ppermute | solution.py:66
  313.3 11.3 %collective-permute-done.38 = bf16[128,2048]{1,0:T(8,128)(2,1)S(1)} collective-permute-done((bf16[128,2048]{1,0:T(8,128)(2,1)S(1)}, bf16[128,2048]{1,0:T(8,128)(2,1)S(1)}, u32[]{:S(2)}, u32[]{:S(2)}) %collective-permute-start.38) | collective-permute-done | bytes 524320 | tf_op jit(solution)/shard_map/ppermute | solution.py:66
  327.9 6.1 %down_product.1 = f32[512,2048]{1,0:T(8,128)S(1)} custom-call(bf16[512,1536]{1,0:T(8,128)(2,1)S(1)} %copy-done.3, bf16[16,1056,512]{2,1,0:T(8,128)(2,1)} %bitcast.132), custom_call_target="tpu_custom_call" | custom-call | flops 3000000000 | bytes 12000000 | tf_op jit(solution)/shard_map/down_product/pallas_call | solution.py:263
  341.2 5.9 %attention_back.1 = bf16[512,640]{1,0:T(8,128)(2,1)S(1)} custom-call(bf16[512,512]{1,0:T(8,128)(2,1)S(1)} %copy-done.11, bf16[512,128]{1,0:T(8,128)(2,1)S(1)} %get-tuple-element.54.kv_ref, bf16[512,512]{1,0:T(8,128)(2,1)S(1)} %convolution_convert_fusion.2.grad_ref, f32[512,128]{1,0:T(8,128)S(1)} %copy-done.5, f32[512,128]{1,0:T(8,128)S(1)} %get-tuple-element.176.sin_ref, ...), custom_call_target="tpu_custom_call" | custom-call | flops 800000000 | bytes 4000000 | tf_op jit(solution)/shard_map/attention_back/pallas_call | solution.py:387
  371.0 11.3 %collective-permute-done.54 = bf16[128,2048]{1,0:T(8,128)(2,1)S(1)} collective-permute-done((bf16[128,2048]{1,0:T(8,128)(2,1)}, bf16[128,2048]{1,0:T(8,128)(2,1)S(1)}, u32[]{:S(2)}, u32[]{:S(2)}) %collective-permute-start.54) | collective-permute-done | bytes 524320 | tf_op jit(solution)/shard_map/ppermute | solution.py:100
  392.9 6.5 %collective-permute-done.45 = bf16[512,640]{1,0:T(8,128)(2,1)S(1)} collective-permute-done((bf16[512,640]{1,0:T(8,128)(2,1)S(1)}, bf16[512,640]{1,0:T(8,128)(2,1)S(1)}, u32[]{:S(2)}, u32[]{:S(2)}) %collective-permute-start.45) | collective-permute-done | bytes 655392 | tf_op jit(solution)/shard_map/ppermute | solution.py:100
  399.5 13.1 %collective-permute-done.46 = bf16[512,640]{1,0:T(8,128)(2,1)S(1)} collective-permute-done((bf16[512,640]{1,0:T(8,128)(2,1)S(1)}, bf16[512,640]{1,0:T(8,128)(2,1)S(1)}, u32[]{:S(2)}, u32[]{:S(2)}) %collective-permute-start.46) | collective-permute-done | bytes 655392 | tf_op jit(solution)/shard_map/ppermute | solution.py:100
  434.6 10.5 %collective-permute-done.43 = bf16[128,2048]{1,0:T(8,128)(2,1)S(1)} collective-permute-done((bf16[128,2048]{1,0:T(8,128)(2,1)S(1)}, bf16[128,2048]{1,0:T(8,128)(2,1)S(1)}, u32[]{:S(2)}, u32[]{:S(2)}) %collective-permute-start.43) | collective-permute-done | bytes 524320 | tf_op jit(solution)/shard_map/ppermute | solution.py:66
  445.5 10.9 %collective-permute-done.41 = bf16[128,2048]{1,0:T(8,128)(2,1)S(1)} collective-permute-done((bf16[128,2048]{1,0:T(8,128)(2,1)S(1)}, bf16[128,2048]{1,0:T(8,128)(2,1)S(1)}, u32[]{:S(2)}, u32[]{:S(2)}) %collective-permute-start.41) | collective-permute-done | bytes 524320 | tf_op jit(solution)/shard_map/ppermute | solution.py:66
  477.1 6.3 %collective-permute-start.69 = (bf16[176,512]{1,0:T(8,128)(2,1)S(1)}, bf16[176,512]{1,0:T(8,128)(2,1)S(1)}, u32[]{:S(2)}, u32[]{:S(2)}) collective-permute-start(bf16[176,512]{1,0:T(8,128)(2,1)S(1)} %get-tuple-element.66), channel_id=1, source_target_pairs={{0,64},{32,96},{64,0},{96,32},{1,65},{33,97},{65,1},{97,33},{2,66}... | collective-permute-start | bytes 540680 | tf_op jit(solution)/shard_map/ppermute | solution.py:66
  (476 shorter events, 236.5 us)
Async XLA Ops:
  7.2 238.8 %all-gather.2.cloned.1.call-start = ((), (), s32[]{:S(2)}) async-start(), calls=%async_computation.1 | async-start | bytes 18382848 | tf_op jit(solution)/shard_map/all_gather | solution.py:74
  26.8 432.0 %reduce-scatter.2.cloned.1.call-start = ((), (), s32[]{:S(2)}) async-start(), calls=%async_computation.2 | async-start | bytes 18382848 | tf_op jit(solution)/shard_map/reduce_scatter | solution.py:78
  28.7 26.4 %collective-permute-start.2 = (bf16[64,640]{1,0:T(8,128)(2,1)S(1)}, bf16[64,640]{1,0:T(8,128)(2,1)S(1)}, u32[]{:S(2)}, u32[]{:S(2)}) collective-permute-start(bf16[64,640]{1,0:T(8,128)(2,1)S(1)} %pad_maximum_fusion.25), channel_id=1, source_target_pairs={{0,1},{1,0},{2,3},{3,2},{4,5},{5,4},{6,7},{7,6},{8,9},{9,8},{10,11... | collective-permute-start | bytes 245768 | tf_op jit(solution)/shard_map/ppermute | solution.py:58
  29.8 111.6 %collective-permute-start = (bf16[128,2048]{1,0:T(8,128)(2,1)S(1)}, bf16[128,2048]{1,0:T(8,128)(2,1)S(1)}, u32[]{:S(2)}, u32[]{:S(2)}) collective-permute-start(bf16[128,2048]{1,0:T(8,128)(2,1)S(1)} %copy-done.14), channel_id=1, source_target_pairs={{0,64},{32,96},{64,0},{96,32},{1,65},{33,97},{65,1},{97,33},{2,66}... | collective-permute-start | bytes 1572872 | tf_op jit(solution)/shard_map/ppermute | solution.py:66
  81.9 24.3 %collective-permute-start.13 = (bf16[4,128,256]{2,1,0:T(8,128)(2,1)S(1)}, bf16[4,128,256]{2,1,0:T(8,128)(2,1)S(1)}, u32[]{:S(2)}, u32[]{:S(2)}) collective-permute-start(bf16[4,128,256]{2,1,0:T(8,128)(2,1)S(1)} %bitcast.143), channel_id=1, source_target_pairs={{0,4},{1,5},{2,6},{3,7},{4,0},{5,1},{6,2},{7,3},{8,12},{9,13},{10,... | collective-permute-start | bytes 786440 | tf_op jit(solution)/shard_map/ppermute | solution.py:86
  85.3 24.8 %collective-permute-start.14 = (bf16[4,128,256]{2,1,0:T(8,128)(2,1)S(1)}, bf16[4,128,256]{2,1,0:T(8,128)(2,1)S(1)}, u32[]{:S(2)}, u32[]{:S(2)}) collective-permute-start(bf16[4,128,256]{2,1,0:T(8,128)(2,1)S(1)} %bitcast.144), channel_id=1, source_target_pairs={{0,6},{1,7},{2,0},{3,1},{4,2},{5,3},{6,4},{7,5},{8,14},{9,15},{10,... | collective-permute-start | bytes 786440 | tf_op jit(solution)/shard_map/ppermute | solution.py:86
  87.4 22.9 %collective-permute-start.9 = (bf16[512,384]{1,0:T(8,128)(2,1)S(1)}, bf16[512,384]{1,0:T(8,128)(2,1)S(1)}, u32[]{:S(2)}, u32[]{:S(2)}) collective-permute-start(bf16[512,384]{1,0:T(8,128)(2,1)S(1)} %constant_dynamic-update-slice_fusion.45), channel_id=1, source_target_pairs={{0,8},{1,9},{2,10},{3,11},{4,12},{5,13},{6,14},{7,15},{8,16},{9,17... | collective-permute-start | bytes 1179656 | tf_op jit(solution)/shard_map/ppermute | solution.py:86
  110.0 31.2 %collective-permute-start.11 = (bf16[512,384]{1,0:T(8,128)(2,1)S(1)}, bf16[512,384]{1,0:T(8,128)(2,1)S(1)}, u32[]{:S(2)}, u32[]{:S(2)}) collective-permute-start(bf16[512,384]{1,0:T(8,128)(2,1)S(1)} %constant_dynamic-update-slice_fusion.45), channel_id=1, source_target_pairs={{0,24},{1,25},{2,26},{3,27},{4,28},{5,29},{6,30},{7,31},{8,0},{9,1... | collective-permute-start | bytes 1179656 | tf_op jit(solution)/shard_map/ppermute | solution.py:86
  141.3 25.2 %collective-permute-start.22 = (bf16[128,2048]{1,0:T(8,128)(2,1)S(1)}, bf16[128,2048]{1,0:T(8,128)(2,1)S(1)}, u32[]{:S(2)}, u32[]{:S(2)}) collective-permute-start(bf16[128,2048]{1,0:T(8,128)(2,1)S(1)} %pad_maximum_fusion.12), channel_id=1, source_target_pairs={{0,2},{1,3},{2,4},{3,5},{4,6},{5,7},{6,0},{7,1},{8,10},{9,11},{10,... | collective-permute-start | bytes 1572872 | tf_op jit(solution)/shard_map/ppermute | solution.py:86
  141.5 40.1 %collective-permute-start.1 = (bf16[256,2048]{1,0:T(8,128)(2,1)S(1)}, bf16[256,2048]{1,0:T(8,128)(2,1)S(1)}, u32[]{:S(2)}, u32[]{:S(2)}) collective-permute-start(bf16[256,2048]{1,0:T(8,128)(2,1)S(1)} %pad_maximum_fusion.5), channel_id=1, source_target_pairs={{0,32},{32,0},{64,96},{96,64},{1,33},{33,1},{65,97},{97,65},{2,34}... | collective-permute-start | bytes 3145736 | tf_op jit(solution)/shard_map/ppermute | solution.py:62
  145.4 36.1 %collective-permute-start.23 = (bf16[128,2048]{1,0:T(8,128)(2,1)S(1)}, bf16[128,2048]{1,0:T(8,128)(2,1)S(1)}, u32[]{:S(2)}, u32[]{:S(2)}) collective-permute-start(bf16[128,2048]{1,0:T(8,128)(2,1)S(1)} %pad_maximum_fusion.12), channel_id=1, source_target_pairs={{0,4},{1,5},{2,6},{3,7},{4,0},{5,1},{6,2},{7,3},{8,12},{9,13},{10,... | collective-permute-start | bytes 1572872 | tf_op jit(solution)/shard_map/ppermute | solution.py:86
  145.5 36.0 %collective-permute-start.24 = (bf16[128,2048]{1,0:T(8,128)(2,1)S(1)}, bf16[128,2048]{1,0:T(8,128)(2,1)S(1)}, u32[]{:S(2)}, u32[]{:S(2)}) collective-permute-start(bf16[128,2048]{1,0:T(8,128)(2,1)S(1)} %pad_maximum_fusion.12), channel_id=1, source_target_pairs={{0,6},{1,7},{2,0},{3,1},{4,2},{5,3},{6,4},{7,5},{8,14},{9,15},{10,... | collective-permute-start | bytes 1572872 | tf_op jit(solution)/shard_map/ppermute | solution.py:86
  196.4 23.2 %collective-permute-start.29 = (bf16[128,2048]{1,0:T(8,128)(2,1)S(1)}, bf16[128,2048]{1,0:T(8,128)(2,1)S(1)}, u32[]{:S(2)}, u32[]{:S(2)}) collective-permute-start(bf16[128,2048]{1,0:T(8,128)(2,1)S(1)} %copy-done.25), channel_id=1, source_target_pairs={{0,64},{32,96},{64,0},{96,32},{1,65},{33,97},{65,1},{97,33},{2,66}... | collective-permute-start | bytes 1572872 | tf_op jit(solution)/shard_map/ppermute | solution.py:66
  340.7 28.3 %collective-permute-start.53 = (bf16[128,2048]{1,0:T(8,128)(2,1)}, bf16[128,2048]{1,0:T(8,128)(2,1)}, u32[]{:S(2)}, u32[]{:S(2)}) collective-permute-start(bf16[128,2048]{1,0:T(8,128)(2,1)} %get-tuple-element.89), channel_id=1, source_target_pairs={{0,2},{1,3},{2,4},{3,5},{4,6},{5,7},{6,0},{7,1},{8,10},{9,11},{10,... | collective-permute-start | bytes 1572872 | tf_op jit(solution)/shard_map/ppermute | solution.py:100
  361.9 26.8 %collective-permute-start.55 = (bf16[128,2048]{1,0:T(8,128)(2,1)S(1)}, bf16[128,2048]{1,0:T(8,128)(2,1)S(1)}, u32[]{:S(2)}, u32[]{:S(2)}) collective-permute-start(bf16[128,2048]{1,0:T(8,128)(2,1)S(1)} %get-tuple-element.90), channel_id=1, source_target_pairs={{0,6},{1,7},{2,0},{3,1},{4,2},{5,3},{6,4},{7,5},{8,14},{9,15},{10,... | collective-permute-start | bytes 1572872 | tf_op jit(solution)/shard_map/ppermute | solution.py:100
  367.1 25.8 %collective-permute-start.44 = (bf16[512,640]{1,0:T(8,128)(2,1)S(1)}, bf16[512,640]{1,0:T(8,128)(2,1)S(1)}, u32[]{:S(2)}, u32[]{:S(2)}) collective-permute-start(bf16[512,640]{1,0:T(8,128)(2,1)S(1)} %get-tuple-element.86), channel_id=1, source_target_pairs={{0,8},{1,9},{2,10},{3,11},{4,12},{5,13},{6,14},{7,15},{8,16},{9,17... | collective-permute-start | bytes 1966088 | tf_op jit(solution)/shard_map/ppermute | solution.py:100
  367.5 32.0 %collective-permute-start.45 = (bf16[512,640]{1,0:T(8,128)(2,1)S(1)}, bf16[512,640]{1,0:T(8,128)(2,1)S(1)}, u32[]{:S(2)}, u32[]{:S(2)}) collective-permute-start(bf16[512,640]{1,0:T(8,128)(2,1)S(1)} %get-tuple-element.88), channel_id=1, source_target_pairs={{0,16},{1,17},{2,18},{3,19},{4,20},{5,21},{6,22},{7,23},{8,24},{9,... | collective-permute-start | bytes 1966088 | tf_op jit(solution)/shard_map/ppermute | solution.py:100
  368.9 43.6 %collective-permute-start.46 = (bf16[512,640]{1,0:T(8,128)(2,1)S(1)}, bf16[512,640]{1,0:T(8,128)(2,1)S(1)}, u32[]{:S(2)}, u32[]{:S(2)}) collective-permute-start(bf16[512,640]{1,0:T(8,128)(2,1)S(1)} %get-tuple-element.87), channel_id=1, source_target_pairs={{0,24},{1,25},{2,26},{3,27},{4,28},{5,29},{6,30},{7,31},{8,0},{9,1... | collective-permute-start | bytes 1966088 | tf_op jit(solution)/shard_map/ppermute | solution.py:100
  382.3 48.3 %collective-permute-start.42 = (bf16[256,2048]{1,0:T(8,128)(2,1)S(1)}, bf16[256,2048]{1,0:T(8,128)(2,1)S(1)}, u32[]{:S(2)}, u32[]{:S(2)}) collective-permute-start(bf16[256,2048]{1,0:T(8,128)(2,1)S(1)} %slice.695), channel_id=1, source_target_pairs={{0,32},{32,0},{64,96},{96,64},{1,33},{33,1},{65,97},{97,65},{2,34}... | collective-permute-start | bytes 3145736 | tf_op jit(solution)/shard_map/ppermute | solution.py:62
  390.6 26.0 %collective-permute-start.56 = (bf16[128,512]{1,0:T(8,128)(2,1)S(1)}, bf16[128,512]{1,0:T(8,128)(2,1)S(1)}, u32[]{:S(2)}, u32[]{:S(2)}) collective-permute-start(bf16[128,512]{1,0:T(8,128)(2,1)S(1)} %get-tuple-element.128), channel_id=1, source_target_pairs={{0,0},{1,1},{2,2},{3,3},{4,4},{5,5},{6,6},{7,7},{8,32},{9,33},{10,... | collective-permute-start | bytes 393224 | tf_op jit(solution)/shard_map/ppermute | solution.py:70
  392.8 23.8 %collective-permute-start.57 = (bf16[128,512]{1,0:T(8,128)(2,1)S(1)}, bf16[128,512]{1,0:T(8,128)(2,1)S(1)}, u32[]{:S(2)}, u32[]{:S(2)}) collective-permute-start(bf16[128,512]{1,0:T(8,128)(2,1)S(1)} %get-tuple-element.131), channel_id=1, source_target_pairs={{0,32},{1,33},{2,34},{3,35},{4,36},{5,37},{6,38},{7,39},{8,64},{9,... | collective-permute-start | bytes 393224 | tf_op jit(solution)/shard_map/ppermute | solution.py:70
  434.5 21.9 %collective-permute-start.41 = (bf16[128,2048]{1,0:T(8,128)(2,1)S(1)}, bf16[128,2048]{1,0:T(8,128)(2,1)S(1)}, u32[]{:S(2)}, u32[]{:S(2)}) collective-permute-start(bf16[128,2048]{1,0:T(8,128)(2,1)S(1)} %slice.700), channel_id=1, source_target_pairs={{0,64},{32,96},{64,0},{96,32},{1,65},{33,97},{65,1},{97,33},{2,66}... | collective-permute-start | bytes 1572872 | tf_op jit(solution)/shard_map/ppermute | solution.py:66
  461.9 21.5 %collective-permute-start.62 = (bf16[64,1280]{1,0:T(8,128)(2,1)S(1)}, bf16[64,1280]{1,0:T(8,128)(2,1)S(1)}, u32[]{:S(2)}, u32[]{:S(2)}) collective-permute-start(bf16[64,1280]{1,0:T(8,128)(2,1)S(1)} %fusion.22), channel_id=1, source_target_pairs={{0,65},{1,64},{2,67},{3,66},{4,69},{5,68},{6,71},{7,70},{8,73},{9,... | collective-permute-start | bytes 491528 | tf_op jit(solution)/shard_map/ppermute | solution.py:70
  468.5 24.4 %collective-permute-start.64 = (bf16[6,64,512]{2,1,0:T(8,128)(2,1)S(1)}, bf16[6,64,512]{2,1,0:T(8,128)(2,1)S(1)}, u32[]{:S(2)}, u32[]{:S(2)}) collective-permute-start(bf16[6,64,512]{2,1,0:T(8,128)(2,1)S(1)} %broadcast_select_fusion), channel_id=1, source_target_pairs={{0,1},{1,0},{2,3},{3,2},{4,5},{5,4},{6,7},{7,6},{8,9},{9,8},{10,11... | collective-permute-start | bytes 1179656 | tf_op jit(solution)/shard_map/ppermute | solution.py:58
  (122 other events, 1357.3 us)
Sparse Core Ops, SparseCore 0:
  26.9 146.6 all-gather.1
  278.5 144.7 reduce-scatter.1

commit v5 on v3

--- a/solution.py
+++ b/solution.py
@@ -41,8 +41,9 @@
 
 TURN = [(spot(m, z, q), spot(z, m, q)) for m, z, q in MZQ]
 TURN_X = [(spot(m, z, q), spot(z, m, q ^ 1)) for m, z, q in MZQ]
-TURN_OUT = [[(spot(m, z, q), spot(z, (m + k) % 4, q)) for m, z, q in MZQ] for k in range(4)]
 TURN_IN = [[(spot(m, z, q), spot((z + k) % 4, m, q)) for m, z, q in MZQ] for k in range(4)]
+OWNED = [(spot(m, z, q), spot(z, m, (q & 3) * 2 + (q >> 2))) for m, z, q in MZQ]
+RETURN = [(b, a) for a, b in OWNED]
 
 
 def ring(place, k):
@@ -77,14 +78,6 @@
     return lax.psum_scatter(
         v, "dp", scatter_dimension=0, tiled=True, axis_index_groups=PLANES
     )
-
-
-def ring_gather(v, pairs, at):
-    rows = v.shape[0]
-    out = jnp.zeros((4 * rows,) + v.shape[1:], v.dtype)
-    for k, part in enumerate([v] + [lax.ppermute(v, "dp", p) for p in pairs]):
-        out = lax.dynamic_update_slice_in_dim(out, part, lax.rem(at + 4 - k, 4) * rows, 0)
-    return out
 
 
 def ring_scatter(v, pairs, at, extra=None):
@@ -105,10 +98,38 @@
     return jnp.concatenate([pair, swap_core(pair)], axis=0)
 
 
+def group_scatter_near(partial):
+    half = 2 * ROWS
+    return partial[:half] + swap_core(partial[half:].astype(BF)).astype(F32)
+
+
+def group_scatter_far(near):
+    return near[:ROWS] + swap_far(near[ROWS:].astype(BF)).astype(F32)
+
+
 def group_scatter(partial):
-    half = 2 * ROWS
-    near = partial[:half] + swap_core(partial[half:].astype(BF)).astype(F32)
-    return near[:ROWS] + swap_far(near[ROWS:].astype(BF)).astype(F32)
+    return group_scatter_far(group_scatter_near(partial))
+
+
+def far_x(v):
+    return everywhere(v, SWAP_FAR_X)
+
+
+def row_gather(v):
+    four = jnp.concatenate([v, swap_x(v), swap_far(v), far_x(v)], axis=0)
+    return jnp.concatenate([four, swap_core(four)], axis=0)
+
+
+def row_scatter(near):
+    low_part, far_part, far_x_part = (
+        near[k * ROWS : (k + 1) * ROWS].astype(BF) for k in (1, 2, 3)
+    )
+    return (
+        near[:ROWS]
+        + swap_x(low_part).astype(F32)
+        + swap_far(far_part).astype(F32)
+        + far_x(far_x_part).astype(F32)
+    )
 
 
 def in_order(own, other, low):
@@ -150,121 +171,219 @@
     return lax.dot_general(left, right, (((1,), (1,)), ((), ())), preferred_element_type=F32)
 
 
-def tail_in(full, tail, sems):
-    return [pltpu.make_async_copy(full.at[:, pl.ds(640,64), pl.ds(256*h,256)], tail.at[:, pl.ds(64*h,64), :], sems.at[h]) for h in range(2)]
+ALL = 1024
+UNITS = 704
+LAST = 192
+SHARD = 528
+
+
+TAIL = [(256, 64, 256 * h, 64 * h, 0, 256) for h in range(2)]
+TAIL += [(320, 32, 128 * h, 32 * h, 256, 128) for h in range(4)]
+
+
+def tail_pieces(shard):
+    for row, rows, column, at, start, width in TAIL:
+        yield (
+            shard.at[:, pl.ds(row, rows), pl.ds(column, width)],
+            (slice(None), pl.ds(at, rows), pl.ds(start, width)),
+        )
+
+
+def tail_loads(full, tail, sems):
+    return [
+        pltpu.make_async_copy(src, tail.at[at], sems.at[i])
+        for i, (src, at) in enumerate(tail_pieces(full))
+    ]
+
+
+def down_blocks(shard, down):
+    return [
+        (shard.at[4 * c + j, pl.ds(352, 176), :], down.at[c, pl.ds(176 * j, 176), :])
+        for c in range(4)
+        for j in range(4)
+    ]
+
 
 def mlp_kernel(s_ref, st_ref, c_ref, panel_ref, full, ggu_ref, act_ref, send,
                down, tail, gpan, gtail, gdown, in_sem, tail_sem, pan_sem, out_sem):
-    j = pl.program_id(0)
-    loads = [pltpu.make_async_copy(full.at[4*c+y, pl.ds(704,352), :], down.at[c, pl.ds(352*y,352), :], in_sem.at[4*c+y]) for c in range(4) for y in range(4)]
-    tails = tail_in(full, tail, tail_sem)
-    @pl.when(j == 0)
+    step = pl.program_id(0)
+    loads = [
+        pltpu.make_async_copy(src, dst, in_sem.at[i])
+        for i, (src, dst) in enumerate(down_blocks(full, down))
+    ]
+    tails = tail_loads(full, tail, tail_sem)
+
+    @pl.when(step == 0)
     def _():
-        for l in loads: l.start()
-        for t in tails: t.start()
-
-    def panel_out(slot, at):
-        return pltpu.make_async_copy(gpan.at[slot], send.at[:, pl.ds(128*at,128), :], pan_sem.at[slot])
-
-    def block(weights, start, width):
+        for copy in loads + tails:
+            copy.start()
+
+    def panel_out(at):
+        return pltpu.make_async_copy(
+            gpan.at[at], send.at[:, pl.ds(128 * at, 128), :], pan_sem.at[at]
+        )
+
+    def block(weights, start, width, store):
         h = dot(s_ref[...], weights)
         gate, up = h[:, :width], h[:, width:]
-        @pl.when(j == 0)
+
+        @pl.when(step == 0)
         def _():
-            for l in loads: l.wait()
-        prod = right_product(c_ref[:, :PANEL], down[0, pl.ds(start,width), :])
-        for c in range(1,4):
-            prod += right_product(c_ref[:, c*PANEL:(c+1)*PANEL], down[c, pl.ds(start,width), :])
-        sig = 1.0/(1.0+jnp.exp(-gate))
-        silu = gate*sig
-        act = (silu*up).astype(BF)
-        grad = jnp.concatenate([(prod*up*sig*(1.0+gate*(1.0-sig))).astype(BF),(prod*silu).astype(BF)],axis=1)
-        ggu_ref[:, :2*width] = grad
+            for copy in loads:
+                copy.wait()
+
+        prod = right_product(c_ref[:, :PANEL], down[0, pl.ds(start, width), :])
+        for c in range(1, 4):
+            prod += right_product(
+                c_ref[:, c * PANEL : (c + 1) * PANEL], down[c, pl.ds(start, width), :]
+            )
+        sig = 1.0 / (1.0 + jnp.exp(-gate))
+        silu = gate * sig
+        act = (silu * up).astype(BF)
+        ggu_ref[:, :width] = (prod * up * sig * (1.0 + gate * (1.0 - sig))).astype(BF)
+        ggu_ref[:, width : 2 * width] = (prod * silu).astype(BF)
         act_ref[:, :width] = act
         for c in range(4):
-            gdown[c, pl.ds(start,width), :] = left_product(act, c_ref[:, c*PANEL:(c+1)*PANEL]).astype(BF)
-        return dot(st_ref[...], grad).astype(BF)
-
-    @pl.when(j < 5)
+            gdown[c, pl.ds(start, width), :] = left_product(
+                act, c_ref[:, c * PANEL : (c + 1) * PANEL]
+            ).astype(BF)
+        store(dot(st_ref[...], ggu_ref[:, : 2 * width]).astype(BF))
+
+    @pl.when(step < 2)
     def _():
-        slot = lax.rem(j, 2)
-        g = block(panel_ref[...].reshape(2048, PANEL), pl.multiple_of(256*j, 256), 256)
-        @pl.when(j >= 2)
-        def _():
-            panel_out(slot, j-2).wait()
-        gpan[slot] = g.reshape(16,128,PANEL)
-        panel_out(slot, j).start()
-
-    @pl.when(j == 5)
+        def store(grads):
+            gpan[step] = grads.reshape(16, 128, PANEL)
+
+        block(panel_ref[...].reshape(D, PANEL), pl.multiple_of(256 * step, 256), 256, store)
+        panel_out(step).start()
+
+    @pl.when(step == 2)
     def _():
-        for t in tails: t.wait()
-        g = block(tail[...].reshape(2048,256), 1280, 128)
-        gtail[...] = g.reshape(16,128,256)
-        outs = [pltpu.make_async_copy(gtail.at[:, pl.ds(64*h,64), :], send.at[:, pl.ds(640,64), pl.ds(256*h,256)], tail_sem.at[h]) for h in range(2)]
-        outs += [pltpu.make_async_copy(gdown.at[c, pl.ds(352*y,352), :], send.at[4*c+y, pl.ds(704,352), :], out_sem.at[4*c+y]) for c in range(4) for y in range(4)]
-        for o in outs: o.start()
-        panel_out(1, 3).wait()
-        panel_out(0, 4).wait()
-        for o in outs: o.wait()
-
-def whole(shape):
-    return pl.BlockSpec(shape, lambda j: (0,)*len(shape), pipeline_mode=pl.Buffered(1))
+        def store(grads):
+            gtail[...] = grads.reshape(16, 128, 2 * LAST)
+
+        for copy in tails:
+            copy.wait()
+        block(tail[...].reshape(D, 2 * LAST), 512, LAST, store)
+        outs = [
+            pltpu.make_async_copy(gtail.at[at], dst, tail_sem.at[i])
+            for i, (dst, at) in enumerate(tail_pieces(send))
+        ]
+        outs += [
+            pltpu.make_async_copy(src, dst, out_sem.at[i])
+            for i, (dst, src) in enumerate(down_blocks(send, gdown))
+        ]
+        for copy in outs:
+            copy.start()
+        for copy in outs + [panel_out(0), panel_out(1)]:
+            copy.wait()
+
 
 def mlp_grads(s, st, cot, full):
     return pl.pallas_call(
-        mlp_kernel, grid=(6,),
-        in_specs=[whole((512,2048)), whole((2048,512)), whole((512,2048)),
-                  pl.BlockSpec((16,128,PANEL), lambda j: (0, jnp.minimum(j,4), 0)),
-                  pl.BlockSpec(memory_space=pl.ANY)],
-        out_specs=[pl.BlockSpec((512,512), lambda j: (0,j)), pl.BlockSpec((512,256), lambda j:(0,j)), pl.BlockSpec(memory_space=pl.ANY)],
-        out_shape=[jax.ShapeDtypeStruct((512,3072),BF), jax.ShapeDtypeStruct((512,1536),BF), jax.ShapeDtypeStruct((16,1056,PANEL),BF)],
-        scratch_shapes=[pltpu.VMEM((4,FW,PANEL),BF), pltpu.VMEM((16,128,256),BF), pltpu.VMEM((2,16,128,PANEL),BF),
-                        pltpu.VMEM((16,128,256),BF), pltpu.VMEM((4,FW,PANEL),BF),
-                        pltpu.SemaphoreType.DMA((16,)), pltpu.SemaphoreType.DMA((2,)), pltpu.SemaphoreType.DMA((2,)), pltpu.SemaphoreType.DMA((16,))],
-        compiler_params=pltpu.CompilerParams(vmem_limit_bytes=58*2**20, dimension_semantics=("arbitrary",)),
-        cost_estimate=pl.CostEstimate(flops=18*10**9, bytes_accessed=45*10**6, transcendentals=10**6),
+        mlp_kernel,
+        grid=(3,),
+        in_specs=[pl.BlockSpec(memory_space=pltpu.VMEM)] * 3
+        + [
+            pl.BlockSpec((16, 128, PANEL), lambda i: (0, jnp.minimum(i, 1), 0)),
+            pl.BlockSpec(memory_space=pl.ANY),
+        ],
+        out_specs=[
+            pl.BlockSpec((ALL, 512), lambda i: (0, i)),
+            pl.BlockSpec((ALL, 256), lambda i: (0, i)),
+            pl.BlockSpec(memory_space=pl.ANY),
+        ],
+        out_shape=[
+            jax.ShapeDtypeStruct((ALL, 1536), BF),
+            jax.ShapeDtypeStruct((ALL, 768), BF),
+            jax.ShapeDtypeStruct((16, SHARD, PANEL), BF),
+        ],
+        scratch_shapes=[
+            pltpu.VMEM((4, UNITS, PANEL), BF),
+            pltpu.VMEM((16, 128, 2 * LAST), BF),
+            pltpu.VMEM((2, 16, 128, PANEL), BF),
+            pltpu.VMEM((16, 128, 2 * LAST), BF),
+            pltpu.VMEM((4, UNITS, PANEL), BF),
+            pltpu.SemaphoreType.DMA((16,)),
+            pltpu.SemaphoreType.DMA((6,)),
+            pltpu.SemaphoreType.DMA((2,)),
+            pltpu.SemaphoreType.DMA((16,)),
+        ],
+        compiler_params=pltpu.CompilerParams(vmem_limit_bytes=44 * 2**20),
+        cost_estimate=pl.CostEstimate(
+            flops=18 * 10**9, bytes_accessed=45 * 10**6, transcendentals=10**6
+        ),
         name="mlp_grads",
     )(s, st, cot, full, full)
 
-def second_kernel(g_ref, panel_ref, full, out_ref, tail, tail_sem):
-    j = pl.program_id(0)
-    tails = tail_in(full, tail, tail_sem)
-    @pl.when(j == 0)
-    def _():
-        for t in tails: t.start()
-        out_ref[...] = right_product(g_ref[...], panel_ref[...].reshape(2048,PANEL))
-    @pl.when(jnp.logical_and(j > 0, j < 5))
-    def _():
-        out_ref[...] += right_product(g_ref[...], panel_ref[...].reshape(2048,PANEL))
-    @pl.when(j == 5)
-    def _():
-        for t in tails: t.wait()
-        out_ref[...] += right_product(g_ref[:, :256], tail[...].reshape(2048,256))
+
+def second_kernel(g_ref, panel_ref, last_refs, near_ref, core_ref, tail):
+    for row, rows, column, at, start, width in TAIL:
+        tail[:, at : at + rows, start : start + width] = last_refs[row][
+            :, :, column : column + width
+        ]
+    total = right_product(g_ref[:, :PANEL], panel_ref[:, :128].reshape(PANEL, PANEL))
+    total += right_product(
+        g_ref[:, PANEL : 2 * PANEL], panel_ref[:, 128:].reshape(PANEL, PANEL)
+    )
+    total += right_product(
+        g_ref[:, 2 * PANEL : 2 * PANEL + 2 * LAST], tail[...].reshape(PANEL, 2 * LAST)
+    )
+    near_ref[...] = total[: ALL // 2]
+    core_ref[...] = total[ALL // 2 :].astype(BF)
+
 
 def second_grad(ggu, full):
+    half = pl.BlockSpec((ALL // 2, PANEL), lambda i: (0, i))
+
+    def kernel(g_ref, panel_ref, wide_ref, narrow_ref, near_ref, core_ref, tail):
+        second_kernel(
+            g_ref, panel_ref, {256: wide_ref, 320: narrow_ref}, near_ref, core_ref, tail
+        )
+
     return pl.pallas_call(
-        second_kernel, grid=(6,),
-        in_specs=[pl.BlockSpec((512,512), lambda j:(0,j)), pl.BlockSpec((16,128,PANEL), lambda j: (0, jnp.minimum(j,4), 0)), pl.BlockSpec(memory_space=pl.ANY)],
-        out_specs=pl.BlockSpec((512,2048), lambda j:(0,0)),
-        out_shape=jax.ShapeDtypeStruct((512,2048),F32),
-        scratch_shapes=[pltpu.VMEM((16,128,256),BF), pltpu.SemaphoreType.DMA((2,))],
-        compiler_params=pltpu.CompilerParams(vmem_limit_bytes=40*2**20, dimension_semantics=("arbitrary",)),
-        cost_estimate=pl.CostEstimate(flops=6*10**9, bytes_accessed=20*10**6, transcendentals=0),
+        kernel,
+        grid=(4,),
+        in_specs=[
+            pl.BlockSpec(memory_space=pltpu.VMEM),
+            pl.BlockSpec((4, 256, PANEL), lambda i: (i, 0, 0)),
+            pl.BlockSpec((4, 64, PANEL), lambda i: (i, 4, 0)),
+            pl.BlockSpec((4, 32, PANEL), lambda i: (i, 10, 0)),
+        ],
+        out_specs=[half, half],
+        out_shape=[
+            jax.ShapeDtypeStruct((ALL // 2, D), F32),
+            jax.ShapeDtypeStruct((ALL // 2, D), BF),
+        ],
+        scratch_shapes=[pltpu.VMEM((4, 128, 2 * LAST), BF)],
+        compiler_params=pltpu.CompilerParams(vmem_limit_bytes=32 * 2**20),
+        cost_estimate=pl.CostEstimate(
+            flops=6 * 10**9, bytes_accessed=20 * 10**6, transcendentals=0
+        ),
         name="second_grad",
-    )(ggu, full, full)
-
-
-def down_kernel(act_ref, down_ref, out_ref):
-    out_ref[...] = dot(act_ref[...], down_ref[...].reshape(FW, PANEL))
+    )(ggu, full, full, full)
+
+
+def down_kernel(act_ref, down_ref, near_ref, core_ref):
+    part = dot(act_ref[:, :UNITS], down_ref[...].reshape(UNITS, PANEL))
+    near_ref[...] = part[: ALL // 2]
+    core_ref[...] = part[ALL // 2 :].astype(BF)
 
 
 def down_product(active, full):
+    half = pl.BlockSpec((ALL // 2, PANEL), lambda c: (0, c))
     return pl.pallas_call(
         down_kernel,
         grid=(4,),
-        in_specs=[whole((SLOTS, FW)), pl.BlockSpec((4, 352, PANEL), lambda c: (c, 2, 0))],
-        out_specs=pl.BlockSpec((SLOTS, PANEL), lambda c: (0, c)),
-        out_shape=jax.ShapeDtypeStruct((SLOTS, D), F32),
+        in_specs=[
+            pl.BlockSpec(memory_space=pltpu.VMEM),
+            pl.BlockSpec((4, 176, PANEL), lambda c: (c, 2, 0)),
+        ],
+        out_specs=[half, half],
+        out_shape=[
+            jax.ShapeDtypeStruct((ALL // 2, D), F32),
+            jax.ShapeDtypeStruct((ALL // 2, D), BF),
+        ],
         compiler_params=pltpu.CompilerParams(vmem_limit_bytes=32 * 2**20),
         cost_estimate=pl.CostEstimate(
             flops=3 * 10**9, bytes_accessed=12 * 10**6, transcendentals=0
@@ -415,17 +534,14 @@
 
 def panels(gate, up):
     blocks = []
-    for at in range(0, FW, 256):
+    for at in range(0, UNITS, 256):
         blocks += [gate[:, at : at + 256], up[:, at : at + 256]]
     return jnp.concatenate(blocks, axis=1)
 
 
-def unpanels(both):
-    gate, up = [], []
-    for at in range(0, FW, 256):
-        width = min(256, FW - at)
-        gate.append(both[:, 2 * at : 2 * at + width])
-        up.append(both[:, 2 * at + width : 2 * at + 2 * width])
+def unpanels(v):
+    gate = [v[:, :256], v[:, 512:768], v[:, 1024 : 1024 + LAST]]
+    up = [v[:, 256:512], v[:, 768:1024], v[:, 1024 + LAST :]]
     return jnp.concatenate(gate, axis=1), jnp.concatenate(up, axis=1)
 
 
@@ -461,30 +577,42 @@
     def mine(weight, width):
         return lax.dynamic_slice_in_dim(weight, member * width, width, 1).astype(BF)
 
-    gu_shard = pair_x(panels(mine(gate_weight, FW), mine(up_weight, FW)), low)
-    pieces = [gu_shard[:, j * PANEL : (j + 1) * PANEL] for j in range(5)]
-    tail = gu_shard[:, 5 * PANEL :]
-    pieces.append(jnp.concatenate([tail[:W_ROWS], tail[W_ROWS:]], axis=1))
-    pieces.append(turn_pair(mine(down_weight, PANEL), low))
-    mlp_full = plane_gather(jnp.concatenate(pieces, axis=0)).reshape(16, 1056, PANEL)
-
-    qkv_shard = jnp.concatenate(
+    attn_shard = jnp.concatenate(
         [mine(query_weight, QW), mine(key_weight, KW), mine(value_weight, KW)], axis=1
     )
-    qkv_full = ring_gather(ring_gather(pair_x(qkv_shard, low), RING_Y, y), RING_Z, z)
-    out_shard = mine(output_weight, QW)
-    out_rows = jnp.zeros((W_ROWS, D), BF)
-    for k in range(4):
-        out_rows = lax.dynamic_update_slice_in_dim(
-            out_rows, everywhere(out_shard, TURN_OUT[k]), lax.rem(z + 4 - k, 4) * PANEL, 1
-        )
-    out_full = ring_gather(pair_x(out_rows, low), RING_Y, y)
+    attn_shard = jnp.concatenate(
+        [pair_x(attn_shard, low), turn_pair(mine(output_weight, QW), low)], axis=1
+    )
+    attn_full = plane_gather(attn_shard)
+    qkv_full = attn_full[:, :QKVW]
+    out_full = attn_full[:, QKVW:].reshape(4, QW, PANEL).transpose(1, 0, 2).reshape(QW, D)
+
+    gate_mine, up_mine = mine(gate_weight, FW), mine(up_weight, FW)
+    first = panels(gate_mine[:, :UNITS], up_mine[:, :UNITS])
+    second = panels(gate_mine[:, UNITS:], up_mine[:, UNITS:])
+    kept, given = jnp.where(low, first, second), jnp.where(low, second, first)
+    gu_shard = in_order(kept, swap_x(given), low)
+    tail = gu_shard[:, 2 * PANEL :]
+    pieces = [
+        gu_shard[:, :PANEL],
+        gu_shard[:, PANEL : 2 * PANEL],
+        jnp.concatenate([tail[:W_ROWS, :256], tail[W_ROWS:, :256]], axis=1),
+        jnp.concatenate([tail[32 * h : 32 * h + 32, 256:] for h in range(4)], axis=1),
+        everywhere(mine(down_weight, PANEL), OWNED),
+    ]
+    mlp_full = plane_gather(jnp.concatenate(pieces, axis=0)).reshape(16, SHARD, PANEL)
 
     places = jnp.stack([segment_ids, positions, padding])
     places = group_gather(places[None])
     segments, spots, pads = places[:, 0], places[:, 1], places[:, 2]
     rows_in = group_gather(tokens)
-    grads_in = group_gather(cotangent)
+    own_moment = jnp.concatenate(
+        [query_moment, key_moment, value_moment, output_moment], axis=1
+    )
+    grads_in, moments = lax.optimization_barrier(
+        (row_gather(cotangent), group_gather(own_moment.astype(BF)))
+    )
+    moments = moments.astype(F32)
 
     first_gain = rounded_gain(attn_gain)
     second_gain = rounded_gain(mlp_gain)
@@ -508,55 +636,67 @@
     query_rot, kv, attended = attention(dot(first_low, qkv_full), cosine, sine, allowed)
     middle = tokens.astype(F32) + group_scatter(dot(attended, out_full))
     second_low = (middle * inverse_rms(middle) * second_gain).astype(BF)
-    second_all = group_gather(second_low)
+    second_all = row_gather(second_low)
 
     grad_gu, active, send = mlp_grads(second_all, second_all.T, grads_in, mlp_full)
-    mlp_sum = plane_scatter(send.reshape(16 * 1056, PANEL))
-    grad_second = group_scatter(second_grad(grad_gu, mlp_full))
+    mlp_sum = plane_scatter(send.reshape(16 * SHARD, PANEL))
+    second_near, second_core = second_grad(grad_gu, mlp_full)
+    grad_second = row_scatter(second_near + swap_core(second_core).astype(F32))
     back, n_second = norm_back(middle, second_gain, grad_second)
     mlp_gain_part = jnp.sum(grad_second * n_second, axis=0)
     grad_middle = cotangent.astype(F32) + back
     middle_all = group_gather(grad_middle.astype(BF))
+    down_near, down_core = down_product(active, mlp_full)
+    down_near = down_near + swap_core(down_core).astype(F32)
+    middle_all, down_near = lax.optimization_barrier((middle_all, down_near))
 
     grad_attended = right_product(middle_all, out_full).astype(BF)
+    grad_out = left_product(attended, middle_all).astype(BF)
+    grad_attended, grad_out = lax.optimization_barrier((grad_attended, grad_out))
     grad_qkv = attention_back(query_rot, kv, grad_attended, cosine, sine, allowed)
-    grad_qkv, active = lax.optimization_barrier((grad_qkv, active))
-
-    qkv_part = ring_scatter(left_product(first_low, grad_qkv).astype(BF), RING_Z, z)
-    out_part = ring_scatter(left_product(attended, middle_all).astype(BF), RING_Y, y).astype(BF)
+
+    qkv_part = left_product(first_low, grad_qkv).astype(BF)
+    qkv_part, grad_qkv = lax.optimization_barrier((qkv_part, grad_qkv))
+    qkv_part = ring_scatter(qkv_part, RING_Z, z)
+    out_part = ring_scatter(grad_out, RING_Y, y).astype(BF)
+    grad_first = right_product(grad_qkv, qkv_full)
+    attn_gain_part = jnp.sum(grad_first * n_first, axis=0)
+    gains = jnp.stack([attn_gain_part, mlp_gain_part]).reshape(32, LANES)
+    gains, out_part = lax.optimization_barrier((gains, out_part))
+    gains = gains + sum(lax.ppermute(gains, "dp", p) for p in RING_Z)
     out_part = sum(
         everywhere(
             lax.dynamic_slice_in_dim(out_part, lax.rem(z + k, 4) * PANEL, PANEL, 1), TURN_IN[k]
         ).astype(F32)
         for k in range(4)
     )
-    grad_first = right_product(grad_qkv, qkv_full)
-    attn_gain_part = jnp.sum(grad_first * n_first, axis=0)
-    gains = jnp.stack([attn_gain_part, mlp_gain_part]).reshape(32, LANES)
-    gains = gains + sum(lax.ppermute(gains, "dp", p) for p in RING_Z)
+    first_near = group_scatter_near(grad_first)
+    block_output = (middle + row_scatter(down_near)).astype(BF)
+    qkv_part, first_near, block_output = lax.optimization_barrier(
+        (qkv_part, first_near, block_output)
+    )
+    back, _ = norm_back(tokens.astype(F32), first_gain, group_scatter_far(first_near))
+    input_grad = grad_middle + back
     rider = jnp.concatenate([two_parts(gains), jnp.zeros((W_ROWS, LANES), BF)], axis=0)
     qkv_part = ring_scatter(qkv_part.astype(BF), RING_Y, y, rider)
     gains = two_parts(one_part(qkv_part[:W_ROWS, QKVW:]))
 
     both = jnp.concatenate([qkv_part[:, :QKVW], out_part], axis=1).astype(BF)
+    both, mlp_sum, input_grad = lax.optimization_barrier((both, mlp_sum, input_grad))
     kept, given = halves(both, low)
     width = QKVW + PANEL
     near = swap_x(jnp.concatenate([given, gains], axis=1))
     far = swap_far(jnp.concatenate([kept, gains], axis=1))
-    far_x = everywhere(jnp.concatenate([given, gains], axis=1), SWAP_FAR_X)
+    both_far = far_x(jnp.concatenate([given, gains], axis=1))
     own_total = kept.astype(F32) + near[:, :width].astype(F32)
-    far_total = far[:, :width].astype(F32) + far_x[:, :width].astype(F32)
-    gains = sum(one_part(part) for part in (gains, near[:, width:], far[:, width:], far_x[:, width:]))
+    far_total = far[:, :width].astype(F32) + both_far[:, :width].astype(F32)
+    gains = sum(one_part(part) for part in (gains, near[:, width:], far[:, width:], both_far[:, width:]))
     totals = jnp.concatenate([own_total, far_total], axis=0).astype(BF)
     rider = jnp.concatenate([two_parts(gains), jnp.zeros((W_ROWS, LANES), BF)], axis=0)
     other = swap_core(jnp.concatenate([totals, rider], axis=1))
     gains = gains + one_part(other[:W_ROWS, width:])
     totals = jnp.concatenate([totals, other[:, :width]], axis=0).astype(F32)
 
-    own_moment = jnp.concatenate(
-        [query_moment, key_moment, value_moment, output_moment], axis=1
-    )
-    moments = group_gather(own_moment.astype(BF)).astype(F32)
     own_moved = 0.5 * own_moment + 0.5 * own_total
     query_momentum = own_moved[:, :QW]
     key_momentum = own_moved[:, QW : QW + KW]
@@ -572,16 +712,23 @@
 
     attn_moved = by_member((0.5 * moments + 0.5 * totals).reshape(MEMBERS, W_ROWS, width))
 
+    wide, narrow = mlp_sum[256:320], mlp_sum[320:352]
     gu_part = jnp.concatenate(
-        [mlp_sum[j * 128 : (j + 1) * 128] for j in range(5)]
-        + [jnp.concatenate([mlp_sum[640:704, :256], mlp_sum[640:704, 256:]], axis=0)],
+        [
+            mlp_sum[:128],
+            mlp_sum[128:256],
+            jnp.concatenate([wide[:, :256], wide[:, 256:]], axis=0),
+            jnp.concatenate([narrow[:, h * LANES : (h + 1) * LANES] for h in range(4)], axis=0),
+        ],
         axis=1,
     )
     kept, given = halves(gu_part, low)
-    gate_rows, up_rows = unpanels(kept.astype(F32) + swap_x(given).astype(F32))
-    kept, given = halves(mlp_sum[704:], low)
-    down_rows = (kept.astype(F32) + swap_x(given).astype(F32)).astype(BF)
-    down_rows = everywhere(down_rows, TURN).astype(F32)
+    other = swap_x(given)
+    first = unpanels(jnp.where(low, kept, other))
+    second = unpanels(jnp.where(low, other, kept))
+    gate_rows = jnp.concatenate([first[0], second[0]], axis=1).astype(F32)
+    up_rows = jnp.concatenate([first[1], second[1]], axis=1).astype(F32)
+    down_rows = everywhere(mlp_sum[352:], RETURN).astype(F32)
     gate_momentum = 0.5 * gate_moment + 0.5 * gate_rows
     up_momentum = 0.5 * up_moment + 0.5 * up_rows
     down_momentum = 0.5 * down_moment + 0.5 * down_rows
@@ -597,10 +744,6 @@
     def updated(weight, columns, start, size):
         moved = jnp.concatenate([block[:, start : start + size] for block in columns], axis=1)
         return weight - learn_rate * moved.astype(F32)
-
-    block_output = (middle + group_scatter(down_product(active, mlp_full))).astype(BF)
-    back, _ = norm_back(tokens.astype(F32), first_gain, group_scatter(grad_first))
-    input_grad = grad_middle + back
 
     gains = 0.5 * jnp.stack([attn_moment, mlp_moment]) + 0.5 * gains.reshape(2, D)
     return (

time: 495 us -> 498 us (level)
  the two profiles are of different devices: /device:TPU:1 before, /device:TPU:81 now
where the time goes in v5:
time: 498 us; the launch traced here: 488 us
  waiting for transfers between devices  209 us (42%)
  starting transfers between devices  95.3 us (19%)
  local copies, waits for them, and re-layouts  51.7 us (10%)
  Pallas kernels  51.6 us (10%)
  other arithmetic  50.3 us (10%)
  between operations  15.8 us (3%)
  matrix products  14.8 us (3%)
    ppermute x13, waiting for transfers between devices, swap_far(): return lax.ppermute(v, 'grp', SWAP_FAR)  71.9 us
    ppermute x13, waiting for transfers between devices, everywhere(): return lax.ppermute(v, ('grp', 'dp'), pairs)  61 us
    ppermute x13, starting transfers between devices, everywhere(): return lax.ppermute(v, ('grp', 'dp'), pairs)  34.5 us
    pallas_call x1, Pallas kernels, mlp_grads(): pl.pallas_call(mlp_kernel, grid=(3,), in_specs=[pl.BlockSpec(memory_space...  29.6 us
    ppermute x3, waiting for transfers between devices, on_device(): gains = gains + sum((lax.ppermute(gains, 'dp', p) for p in RING_Z))  26.6 us
    ppermute x13, starting transfers between devices, swap_core(): return lax.ppermute(v, 'grp', SWAP_CORE)  26.3 us
    ppermute x9, waiting for transfers between devices, ring_scatter(): total = total + lax.ppermute(chunk(k + 1), 'dp', p).astype(F32)  20.3 us
    all_gather x2, waiting for transfers between devices, plane_gather(): return lax.all_gather(v, 'dp', axis=0, tiled=True, axis_index_groups=PLANES)  15.5 us
  transfers between devices with their start and end apart: 62, of which 24 were waited for; matrix products, arithmetic and copies ran while one was open for 20% of the time, Pallas kernels for 5%

profile of v5, /device:TPU:81, one launch (start us, length us, event | category | flops | bytes accessed | tf_op | source)
XLA Modules:
  0.0 488.4 jit_solution(6170086890957870775)
XLA Ops:
  8.2 4.8 collective-permute-start.3
  24.2 5.2 %collective-permute-start.20 = (bf16[176,512]{1,0:T(8,128)(2,1)S(1)}, bf16[176,512]{1,0:T(8,128)(2,1)S(1)}, u32[]{:S(2)}, u32[]{:S(2)}) collective-permute-start(bf16[176,512]{1,0:T(8,128)(2,1)S(1)} %dynamic-slice_convert_fusion), channel_id=1, source_target_pairs={{0,0},{1,2},{2,4},{3,6},{4,1},{5,3},{6,5},{7,7},{8,32},{9,34},{10,... | collective-permute-start | bytes 540680 | tf_op jit(solution)/shard_map/ppermute | solution.py:70
  29.7 7.3 %collective-permute-done.20 = bf16[176,512]{1,0:T(8,128)(2,1)S(1)} collective-permute-done((bf16[176,512]{1,0:T(8,128)(2,1)S(1)}, bf16[176,512]{1,0:T(8,128)(2,1)S(1)}, u32[]{:S(2)}, u32[]{:S(2)}) %collective-permute-start.20) | collective-permute-done | bytes 180256 | tf_op jit(solution)/shard_map/ppermute | solution.py:70
  37.9 10.9 %collective-permute-done = bf16[128,2048]{1,0:T(8,128)(2,1)S(1)} collective-permute-done((bf16[128,2048]{1,0:T(8,128)(2,1)S(1)}, bf16[128,2048]{1,0:T(8,128)(2,1)S(1)}, u32[]{:S(2)}, u32[]{:S(2)}) %collective-permute-start) | collective-permute-done | bytes 524320 | tf_op jit(solution)/shard_map/ppermute | solution.py:66
  50.0 4.9 %collective-permute-start.1 = (bf16[256,2048]{1,0:T(8,128)(2,1)}, bf16[256,2048]{1,0:T(8,128)(2,1)S(1)}, u32[]{:S(2)}, u32[]{:S(2)}) collective-permute-start(bf16[256,2048]{1,0:T(8,128)(2,1)} %pad_maximum_fusion.5), channel_id=1, source_target_pairs={{0,32},{32,0},{64,96},{96,64},{1,33},{33,1},{65,97},{97,65},{2,34}... | collective-permute-start | bytes 3145736 | tf_op jit(solution)/shard_map/ppermute | solution.py:62
  63.1 15.5 %all-gather.3.cloned.1.call-done = bf16[2048,1152]{1,0:T(8,128)(2,1)} async-done(((bf16[128,1152]{1,0:T(8,128)(2,1)}), bf16[2048,1152]{1,0:T(8,128)(2,1)}) %all-gather.3.cloned.1.call-update) | async-done | bytes 4718608 | tf_op jit(solution)/shard_map/all_gather | solution.py:74
  98.3 7.1 %collective-permute-done.13 = bf16[128,2048]{1,0:T(8,128)(2,1)S(1)} collective-permute-done((bf16[128,2048]{1,0:T(8,128)(2,1)S(1)}, bf16[128,2048]{1,0:T(8,128)(2,1)S(1)}, u32[]{:S(2)}, u32[]{:S(2)}) %collective-permute-start.13) | collective-permute-done | bytes 524320 | tf_op jit(solution)/shard_map/ppermute | solution.py:58
  105.4 13.3 %collective-permute-done.14 = bf16[128,2048]{1,0:T(8,128)(2,1)S(1)} collective-permute-done((bf16[128,2048]{1,0:T(8,128)(2,1)S(1)}, bf16[128,2048]{1,0:T(8,128)(2,1)S(1)}, u32[]{:S(2)}, u32[]{:S(2)}) %collective-permute-start.14) | collective-permute-done | bytes 524320 | tf_op jit(solution)/shard_map/ppermute | solution.py:66
  118.7 13.3 %collective-permute-done.15 = bf16[128,2048]{1,0:T(8,128)(2,1)S(1)} collective-permute-done((bf16[128,2048]{1,0:T(8,128)(2,1)S(1)}, bf16[128,2048]{1,0:T(8,128)(2,1)S(1)}, u32[]{:S(2)}, u32[]{:S(2)}) %collective-permute-start.15) | collective-permute-done | bytes 524320 | tf_op jit(solution)/shard_map/ppermute | solution.py:70
  144.0 22.5 %collective-permute-done.17 = bf16[64,1152]{1,0:T(8,128)(2,1)S(1)} collective-permute-done((bf16[64,1152]{1,0:T(8,128)(2,1)S(1)}, bf16[64,1152]{1,0:T(8,128)(2,1)S(1)}, u32[]{:S(2)}, u32[]{:S(2)}) %collective-permute-start.17) | collective-permute-done | bytes 147488 | tf_op jit(solution)/shard_map/ppermute | solution.py:66
  180.4 6.4 %copy.46.st_ref = bf16[2048,1024]{1,0:T(8,128)(2,1)} copy(bf16[2048,1024]{0,1:T(8,128)(2,1)} %bitcast.9) | data formatting | bytes 8388608 | tf_op jit(solution)/shard_map/transpose | solution.py:641
  186.8 29.6 %mlp_grads.1 = (bf16[1024,1536]{1,0:T(8,128)(2,1)S(1)}, bf16[1024,768]{1,0:T(8,128)(2,1)S(1)}, bf16[16,528,512]{2,1,0:T(8,128)(2,1)}) custom-call(bf16[1024,2048]{1,0:T(8,128)(2,1)} %constant_dynamic-update-slice_fusion.s_ref, bf16[2048,1024]{1,0:T(8,128)(2,1)} %copy.46.st_ref, bf16[1024,2048]{1,0:T(8,128)(2,1)} %copy-done.59, ...), custom_call_target="tpu_custom_call" | custom-call | flops 17999998976 | bytes 45000000 | tf_op jit(solution)/shard_map/mlp_grads/pallas_call | solution.py:283
  221.1 8.3 %second_grad.1 = (f32[512,2048]{1,0:T(8,128)S(1)}, bf16[512,2048]{1,0:T(8,128)(2,1)S(1)}) custom-call(bf16[1024,1536]{1,0:T(8,128)(2,1)S(1)} %get-tuple-element.50.g_ref, bf16[16,528,512]{2,1,0:T(8,128)(2,1)S(1)} %bitcast.60, bf16[16,528,512]{2,1,0:T(8,128)(2,1)S(1)} %bitcast.61, bf16[16,528,512]{2,1,0:T(8,128)(2,1)S(1)} %bitcast.62), custom_call_target="tpu_custom_call" | custom-call | flops 6000000000 | bytes 20000000 | tf_op jit(solution)/shard_map/second_grad/pallas_call | solution.py:344
  238.4 4.5 down_product.1
  244.2 16.4 %collective-permute-done.24 = bf16[128,2048]{1,0:T(8,128)(2,1)S(1)} collective-permute-done((bf16[128,2048]{1,0:T(8,128)(2,1)S(1)}, bf16[128,2048]{1,0:T(8,128)(2,1)S(1)}, u32[]{:S(2)}, u32[]{:S(2)}) %collective-permute-start.24) | collective-permute-done | bytes 524320 | tf_op jit(solution)/shard_map/ppermute | solution.py:70
  264.0 12.3 %collective-permute-done.25 = bf16[128,2048]{1,0:T(8,128)(2,1)S(1)} collective-permute-done((bf16[128,2048]{1,0:T(8,128)(2,1)S(1)}, bf16[128,2048]{1,0:T(8,128)(2,1)S(1)}, u32[]{:S(2)}, u32[]{:S(2)}) %collective-permute-start.25) | collective-permute-done | bytes 524320 | tf_op jit(solution)/shard_map/ppermute | solution.py:66
  290.9 5.9 %attention_back.1 = bf16[512,640]{1,0:T(8,128)(2,1)S(1)} custom-call(bf16[512,512]{1,0:T(8,128)(2,1)S(1)} %copy-done.9, bf16[512,128]{1,0:T(8,128)(2,1)S(1)} %get-tuple-element.47.kv_ref, bf16[512,512]{1,0:T(8,128)(2,1)S(1)} %convolution_convert_fusion.2.grad_ref, f32[512,128]{1,0:T(8,128)S(1)} %copy-done.5, f32[512,128]{1,0:T(8,128)S(1)} %get-tuple-element.207.sin_ref, ...), custom_call_target="tpu_custom_call" | custom-call | flops 800000000 | bytes 4000000 | tf_op jit(solution)/shard_map/attention_back/pallas_call | solution.py:499
  313.4 5.6 %collective-permute-done.37 = bf16[128,2048]{1,0:T(8,128)(2,1)} collective-permute-done((bf16[128,2048]{1,0:T(8,128)(2,1)}, bf16[128,2048]{1,0:T(8,128)(2,1)}, u32[]{:S(2)}, u32[]{:S(2)}) %collective-permute-start.37) | collective-permute-done | bytes 524320 | tf_op jit(solution)/shard_map/ppermute | solution.py:92
  320.7 12.7 %collective-permute-done.35 = bf16[128,2048]{1,0:T(8,128)(2,1)} collective-permute-done((bf16[128,2048]{1,0:T(8,128)(2,1)}, bf16[128,2048]{1,0:T(8,128)(2,1)}, u32[]{:S(2)}, u32[]{:S(2)}) %collective-permute-start.35) | collective-permute-done | bytes 524320 | tf_op jit(solution)/shard_map/ppermute | solution.py:92
  347.4 24.2 %collective-permute-done.38 = f32[32,128]{1,0:T(8,128)S(1)} collective-permute-done((f32[32,128]{1,0:T(8,128)S(1)}, f32[32,128]{1,0:T(8,128)S(1)}, u32[]{:S(2)}, u32[]{:S(2)}) %collective-permute-start.38) | collective-permute-done | bytes 16416 | tf_op jit(solution)/shard_map/ppermute | solution.py:666
  394.5 9.0 %collective-permute-done.48 = bf16[128,2048]{1,0:T(8,128)(2,1)S(1)} collective-permute-done((bf16[128,2048]{1,0:T(8,128)(2,1)S(1)}, bf16[128,2048]{1,0:T(8,128)(2,1)S(1)}, u32[]{:S(2)}, u32[]{:S(2)}) %collective-permute-start.48) | collective-permute-done | bytes 524320 | tf_op jit(solution)/shard_map/ppermute | solution.py:66
  413.3 5.5 %collective-permute-start.54 = (bf16[176,512]{1,0:T(8,128)(2,1)S(1)}, bf16[176,512]{1,0:T(8,128)(2,1)}, u32[]{:S(2)}, u32[]{:S(2)}) collective-permute-start(bf16[176,512]{1,0:T(8,128)(2,1)S(1)} %slice.487), channel_id=1, source_target_pairs={{0,0},{2,1},{4,2},{6,3},{1,4},{3,5},{5,6},{7,7},{32,8},{34,9},{36,... | collective-permute-start | bytes 540680 | tf_op jit(solution)/shard_map/ppermute | solution.py:70
  425.7 20.1 %collective-permute-done.54 = bf16[176,512]{1,0:T(8,128)(2,1)} collective-permute-done((bf16[176,512]{1,0:T(8,128)(2,1)S(1)}, bf16[176,512]{1,0:T(8,128)(2,1)}, u32[]{:S(2)}, u32[]{:S(2)}) %collective-permute-start.54) | collective-permute-done | bytes 180256 | tf_op jit(solution)/shard_map/ppermute | solution.py:70
  454.4 5.1 %collective-permute-start.58 = (bf16[352,512]{1,0:T(8,128)(2,1)}, bf16[352,512]{1,0:T(8,128)(2,1)}, u32[]{:S(2)}, u32[]{:S(2)}) collective-permute-start(bf16[352,512]{1,0:T(8,128)(2,1)} %pad_maximum_fusion.11), channel_id=1, source_target_pairs={{0,32},{32,0},{64,96},{96,64},{1,33},{33,1},{65,97},{97,65},{2,34}... | collective-permute-start | bytes 1081352 | tf_op jit(solution)/shard_map/ppermute | solution.py:62
  (444 shorter events, 202.1 us)
Async XLA Ops:
  7.2 71.5 %all-gather.3.cloned.1.call-start = ((), (), s32[]{:S(2)}) async-start(), calls=%async_computation.1 | async-start | bytes 5013504 | tf_op jit(solution)/shard_map/all_gather | solution.py:74
  21.3 165.5 %all-gather.5.cloned.1.call-start = ((), (), s32[]{:S(2)}) async-start(), calls=%async_computation.2 | async-start | bytes 9191424 | tf_op jit(solution)/shard_map/all_gather | solution.py:74
  37.8 367.8 %reduce-scatter.2.cloned.1.call-start = ((), (), s32[]{:S(2)}) async-start(), calls=%async_computation.3 | async-start | bytes 9191424 | tf_op jit(solution)/shard_map/reduce_scatter | solution.py:78
  93.6 25.0 %collective-permute-start.14 = (bf16[128,2048]{1,0:T(8,128)(2,1)S(1)}, bf16[128,2048]{1,0:T(8,128)(2,1)S(1)}, u32[]{:S(2)}, u32[]{:S(2)}) collective-permute-start(bf16[128,2048]{1,0:T(8,128)(2,1)S(1)} %copy-done.21), channel_id=1, source_target_pairs={{0,64},{32,96},{64,0},{96,32},{1,65},{33,97},{65,1},{97,33},{2,66}... | collective-permute-start | bytes 1572872 | tf_op jit(solution)/shard_map/ppermute | solution.py:66
  96.1 35.9 %collective-permute-start.15 = (bf16[128,2048]{1,0:T(8,128)(2,1)S(1)}, bf16[128,2048]{1,0:T(8,128)(2,1)S(1)}, u32[]{:S(2)}, u32[]{:S(2)}) collective-permute-start(bf16[128,2048]{1,0:T(8,128)(2,1)S(1)} %copy-done.21), channel_id=1, source_target_pairs={{0,65},{1,64},{2,67},{3,66},{4,69},{5,68},{6,71},{7,70},{8,73},{9,... | collective-permute-start | bytes 1572872 | tf_op jit(solution)/shard_map/ppermute | solution.py:70
  96.7 39.1 %collective-permute-start.8 = (bf16[128,2048]{1,0:T(8,128)(2,1)S(1)}, bf16[128,2048]{1,0:T(8,128)(2,1)S(1)}, u32[]{:S(2)}, u32[]{:S(2)}) collective-permute-start(bf16[128,2048]{1,0:T(8,128)(2,1)S(1)} %slice.672), channel_id=1, source_target_pairs={{0,64},{32,96},{64,0},{96,32},{1,65},{33,97},{65,1},{97,33},{2,66}... | collective-permute-start | bytes 1572872 | tf_op jit(solution)/shard_map/ppermute | solution.py:66
  133.5 39.4 %collective-permute-start.16 = (bf16[512,2048]{1,0:T(8,128)(2,1)}, bf16[512,2048]{1,0:T(8,128)(2,1)}, u32[]{:S(2)}, u32[]{:S(2)}) collective-permute-start(bf16[512,2048]{1,0:T(8,128)(2,1)} %pad_maximum_fusion.2), channel_id=1, source_target_pairs={{0,32},{32,0},{64,96},{96,64},{1,33},{33,1},{65,97},{97,65},{2,34}... | collective-permute-start | bytes 6291464 | tf_op jit(solution)/shard_map/ppermute | solution.py:62
  138.6 28.9 %collective-permute-start.9 = (bf16[128,2048]{1,0:T(8,128)(2,1)S(1)}, bf16[128,2048]{1,0:T(8,128)(2,1)S(1)}, u32[]{:S(2)}, u32[]{:S(2)}) collective-permute-start(bf16[128,2048]{1,0:T(8,128)(2,1)S(1)} %get-tuple-element.90), channel_id=1, source_target_pairs={{0,1},{1,0},{2,3},{3,2},{4,5},{5,4},{6,7},{7,6},{8,9},{9,8},{10,11... | collective-permute-start | bytes 1572872 | tf_op jit(solution)/shard_map/ppermute | solution.py:58
  138.6 28.9 %collective-permute-start.10 = (bf16[128,2048]{1,0:T(8,128)(2,1)S(1)}, bf16[128,2048]{1,0:T(8,128)(2,1)S(1)}, u32[]{:S(2)}, u32[]{:S(2)}) collective-permute-start(bf16[128,2048]{1,0:T(8,128)(2,1)S(1)} %get-tuple-element.90), channel_id=1, source_target_pairs={{0,64},{32,96},{64,0},{96,32},{1,65},{33,97},{65,1},{97,33},{2,66}... | collective-permute-start | bytes 1572872 | tf_op jit(solution)/shard_map/ppermute | solution.py:66
  140.0 29.1 %collective-permute-start.11 = (bf16[128,2048]{1,0:T(8,128)(2,1)S(1)}, bf16[128,2048]{1,0:T(8,128)(2,1)}, u32[]{:S(2)}, u32[]{:S(2)}) collective-permute-start(bf16[128,2048]{1,0:T(8,128)(2,1)S(1)} %get-tuple-element.90), channel_id=1, source_target_pairs={{0,65},{1,64},{2,67},{3,66},{4,69},{5,68},{6,71},{7,70},{8,73},{9,... | collective-permute-start | bytes 1572872 | tf_op jit(solution)/shard_map/ppermute | solution.py:70
  235.0 25.7 %collective-permute-start.24 = (bf16[128,2048]{1,0:T(8,128)(2,1)S(1)}, bf16[128,2048]{1,0:T(8,128)(2,1)S(1)}, u32[]{:S(2)}, u32[]{:S(2)}) collective-permute-start(bf16[128,2048]{1,0:T(8,128)(2,1)S(1)} %get-tuple-element.103), channel_id=1, source_target_pairs={{0,65},{1,64},{2,67},{3,66},{4,69},{5,68},{6,71},{7,70},{8,73},{9,... | collective-permute-start | bytes 1572872 | tf_op jit(solution)/shard_map/ppermute | solution.py:70
  242.9 38.0 %collective-permute-start.27 = (bf16[512,2048]{1,0:T(8,128)(2,1)S(1)}, bf16[512,2048]{1,0:T(8,128)(2,1)}, u32[]{:S(2)}, u32[]{:S(2)}) collective-permute-start(bf16[512,2048]{1,0:T(8,128)(2,1)S(1)} %get-tuple-element.55), channel_id=1, source_target_pairs={{0,32},{32,0},{64,96},{96,64},{1,33},{33,1},{65,97},{97,65},{2,34}... | collective-permute-start | bytes 6291464 | tf_op jit(solution)/shard_map/ppermute | solution.py:62
  301.8 37.3 %collective-permute-start.34 = (bf16[128,2048]{1,0:T(8,128)(2,1)}, bf16[128,2048]{1,0:T(8,128)(2,1)}, u32[]{:S(2)}, u32[]{:S(2)}) collective-permute-start(bf16[128,2048]{1,0:T(8,128)(2,1)} %get-tuple-element.100), channel_id=1, source_target_pairs={{0,65},{1,64},{2,67},{3,66},{4,69},{5,68},{6,71},{7,70},{8,73},{9,... | collective-permute-start | bytes 1572872 | tf_op jit(solution)/shard_map/ppermute | solution.py:70
  304.5 36.1 %collective-permute-start.33 = (bf16[128,2048]{1,0:T(8,128)(2,1)}, bf16[128,2048]{1,0:T(8,128)(2,1)}, u32[]{:S(2)}, u32[]{:S(2)}) collective-permute-start(bf16[128,2048]{1,0:T(8,128)(2,1)} %get-tuple-element.101), channel_id=1, source_target_pairs={{0,64},{32,96},{64,0},{96,32},{1,65},{33,97},{65,1},{97,33},{2,66}... | collective-permute-start | bytes 1572872 | tf_op jit(solution)/shard_map/ppermute | solution.py:66
  308.7 24.7 %collective-permute-start.35 = (bf16[128,2048]{1,0:T(8,128)(2,1)}, bf16[128,2048]{1,0:T(8,128)(2,1)}, u32[]{:S(2)}, u32[]{:S(2)}) collective-permute-start(bf16[128,2048]{1,0:T(8,128)(2,1)} %get-tuple-element.96), channel_id=1, source_target_pairs={{0,2},{1,3},{2,4},{3,5},{4,6},{5,7},{6,0},{7,1},{8,10},{9,11},{10,... | collective-permute-start | bytes 1572872 | tf_op jit(solution)/shard_map/ppermute | solution.py:92
  335.7 40.0 %collective-permute-start.30 = (bf16[512,640]{1,0:T(8,128)(2,1)S(1)}, bf16[512,640]{1,0:T(8,128)(2,1)S(1)}, u32[]{:S(2)}, u32[]{:S(2)}) collective-permute-start(bf16[512,640]{1,0:T(8,128)(2,1)S(1)} %get-tuple-element.94), channel_id=1, source_target_pairs={{0,24},{1,25},{2,26},{3,27},{4,28},{5,29},{6,30},{7,31},{8,0},{9,1... | collective-permute-start | bytes 1966088 | tf_op jit(solution)/shard_map/ppermute | solution.py:92
  339.1 40.3 %collective-permute-start.29 = (bf16[512,640]{1,0:T(8,128)(2,1)S(1)}, bf16[512,640]{1,0:T(8,128)(2,1)S(1)}, u32[]{:S(2)}, u32[]{:S(2)}) collective-permute-start(bf16[512,640]{1,0:T(8,128)(2,1)S(1)} %get-tuple-element.95), channel_id=1, source_target_pairs={{0,16},{1,17},{2,18},{3,19},{4,20},{5,21},{6,22},{7,23},{8,24},{9,... | collective-permute-start | bytes 1966088 | tf_op jit(solution)/shard_map/ppermute | solution.py:92
  340.6 40.6 %collective-permute-start.28 = (bf16[512,640]{1,0:T(8,128)(2,1)S(1)}, bf16[512,640]{1,0:T(8,128)(2,1)S(1)}, u32[]{:S(2)}, u32[]{:S(2)}) collective-permute-start(bf16[512,640]{1,0:T(8,128)(2,1)S(1)} %get-tuple-element.93), channel_id=1, source_target_pairs={{0,8},{1,9},{2,10},{3,11},{4,12},{5,13},{6,14},{7,15},{8,16},{9,17... | collective-permute-start | bytes 1966088 | tf_op jit(solution)/shard_map/ppermute | solution.py:92
  342.2 42.5 %collective-permute-start.31 = (bf16[256,2048]{1,0:T(8,128)(2,1)S(1)}, bf16[256,2048]{1,0:T(8,128)(2,1)S(1)}, u32[]{:S(2)}, u32[]{:S(2)}) collective-permute-start(bf16[256,2048]{1,0:T(8,128)(2,1)S(1)} %slice.669), channel_id=1, source_target_pairs={{0,32},{32,0},{64,96},{96,64},{1,33},{33,1},{65,97},{97,65},{2,34}... | collective-permute-start | bytes 3145736 | tf_op jit(solution)/shard_map/ppermute | solution.py:62
  343.8 27.7 %collective-permute-start.38 = (f32[32,128]{1,0:T(8,128)S(1)}, f32[32,128]{1,0:T(8,128)S(1)}, u32[]{:S(2)}, u32[]{:S(2)}) collective-permute-start(f32[32,128]{1,0:T(8,128)S(1)} %reshape.144), channel_id=1, source_target_pairs={{0,8},{1,9},{2,10},{3,11},{4,12},{5,13},{6,14},{7,15},{8,16},{9,17... | collective-permute-start | bytes 49160 | tf_op jit(solution)/shard_map/ppermute | solution.py:666
  406.3 41.2 %collective-permute-start.51 = (bf16[64,1280]{1,0:T(8,128)(2,1)}, bf16[64,1280]{1,0:T(8,128)(2,1)}, u32[]{:S(2)}, u32[]{:S(2)}) collective-permute-start(bf16[64,1280]{1,0:T(8,128)(2,1)} %fusion.24), channel_id=1, source_target_pairs={{0,65},{1,64},{2,67},{3,66},{4,69},{5,68},{6,71},{7,70},{8,73},{9,... | collective-permute-start | bytes 491528 | tf_op jit(solution)/shard_map/ppermute | solution.py:70
  413.3 32.5 %collective-permute-start.54 = (bf16[176,512]{1,0:T(8,128)(2,1)S(1)}, bf16[176,512]{1,0:T(8,128)(2,1)}, u32[]{:S(2)}, u32[]{:S(2)}) collective-permute-start(bf16[176,512]{1,0:T(8,128)(2,1)S(1)} %slice.487), channel_id=1, source_target_pairs={{0,0},{2,1},{4,2},{6,3},{1,4},{3,5},{5,6},{7,7},{32,8},{34,9},{36,... | collective-permute-start | bytes 540680 | tf_op jit(solution)/shard_map/ppermute | solution.py:70
  419.0 28.6 %collective-permute-start.50 = (bf16[64,1280]{1,0:T(8,128)(2,1)S(1)}, bf16[64,1280]{1,0:T(8,128)(2,1)S(1)}, u32[]{:S(2)}, u32[]{:S(2)}) collective-permute-start(bf16[64,1280]{1,0:T(8,128)(2,1)S(1)} %fusion.23), channel_id=1, source_target_pairs={{0,64},{32,96},{64,0},{96,32},{1,65},{33,97},{65,1},{97,33},{2,66}... | collective-permute-start | bytes 491528 | tf_op jit(solution)/shard_map/ppermute | solution.py:66
  425.3 34.2 %collective-permute-start.55 = (bf16[64,2816]{1,0:T(8,128)(2,1)S(1)}, bf16[64,2816]{1,0:T(8,128)(2,1)S(1)}, u32[]{:S(2)}, u32[]{:S(2)}) collective-permute-start(bf16[64,2816]{1,0:T(8,128)(2,1)S(1)} %pad_maximum_fusion.10), channel_id=1, source_target_pairs={{0,64},{32,96},{64,0},{96,32},{1,65},{33,97},{65,1},{97,33},{2,66}... | collective-permute-start | bytes 1081352 | tf_op jit(solution)/shard_map/ppermute | solution.py:66
  (120 other events, 1252.7 us)
Sparse Core Ops, SparseCore 0:
  21.4 57.2 all-gather.2
  81.4 71.6 all-gather.4
  217.7 83.2 reduce-scatter.1
